TPU v7x, 32 devices: a whole 2x2x4 slice. The times are simulated.
32 devices in a mesh: dp: 8 (over z, x), tensor: 4 (over y, core).
Axes of the slice: x: 2, y: 2, z: 4, core: 2. Of those that a mesh axis runs over, the one named last changes fastest.
Arguments:
- inputs: float32 [16384, 1600], P(('dp', 'tensor')), may hold values from -6 to 6
- teacher: float32 [16384, 1600], P(('dp', 'tensor')), may hold values from -6 to 6
- segment_ids: int32 [16384], P('dp'), may hold values from 0 to 23, never falling along the last dimension, each value on 1 to 1536 neighbouring positions
- valid: int32 [16384], P(('dp', 'tensor')), may hold values from 0 to 1, as said below
- norm_in_gain: bfloat16 [1600], P('dp'), may hold values from 0.5 to 1.5
- w_query: bfloat16 [1600, 1600], P('dp'), may hold values from -0.15625 to 0.15625
- w_key: bfloat16 [1600, 320], P('dp'), may hold values from -0.15625 to 0.15625
- w_value: bfloat16 [1600, 320], P('dp'), may hold values from -0.15625 to 0.15625
- w_attn_out: bfloat16 [1600, 1600], P(None, 'dp'), may hold values from -0.15625 to 0.15625
- w_mamba_in: bfloat16 [1600, 2, 3200], P('dp', None, 'tensor'), may hold values from -0.15625 to 0.15625
- conv_weight: bfloat16 [4, 3200], P(None, 'dp'), may hold values from -3 to 3
- conv_bias: bfloat16 [3200], P('dp'), may hold values from -1 to 1
- x_proj: bfloat16 [3200, 132], P('dp'), may hold values from -0.21875 to 0.21875
- dt_proj: bfloat16 [100, 3200], P(None, 'dp'), may hold values from -0.625 to 0.625
- dt_bias: bfloat16 [3200], P('dp'), may hold values from -4 to -0.5
- a_log: bfloat16 [3200], P('dp'), may hold values from -5 to -0.5
- d_skip: bfloat16 [3200], P('dp'), may hold values from 0.5 to 1.5
- w_mamba_out: bfloat16 [3200, 1600], P('tensor', 'dp'), may hold values from -0.109375 to 0.109375
- attn_norm_gain: bfloat16 [1600], P('dp'), may hold values from 0.5 to 1.5
- ssm_norm_gain: bfloat16 [1600], P('dp'), may hold values from 0.5 to 1.5
- norm_mid_gain: bfloat16 [1600], P('dp'), may hold values from 0.5 to 1.5
- w_gate: bfloat16 [1600, 5504], P('dp', 'tensor'), may hold values from -0.15625 to 0.15625
- w_up: bfloat16 [1600, 5504], P('dp', 'tensor'), may hold values from -0.15625 to 0.15625
- w_down: bfloat16 [5504, 1600], P('tensor', 'dp'), may hold values from -0.078125 to 0.078125
Outputs:
- out: float32 [16384, 1600], P(('dp', 'tensor'))
- grad_inputs: float32 [16384, 1600], P(('dp', 'tensor'))
- grad_norm_in_gain: float32 [1600], P('dp')
- grad_w_query: float32 [1600, 1600], P('dp')
- grad_w_key: float32 [1600, 320], P('dp')
- grad_w_value: float32 [1600, 320], P('dp')
- grad_w_attn_out: float32 [1600, 1600], P(None, 'dp')
- grad_w_mamba_in: float32 [1600, 2, 3200], P('dp', None, 'tensor')
- grad_conv_weight: float32 [4, 3200], P(None, 'dp')
- grad_conv_bias: float32 [3200], P('dp')
- grad_x_proj: float32 [3200, 132], P('dp')
- grad_dt_proj: float32 [100, 3200], P(None, 'dp')
- grad_dt_bias: float32 [3200], P('dp')
- grad_a_log: float32 [3200], P('dp')
- grad_d_skip: float32 [3200], P('dp')
- grad_w_mamba_out: float32 [3200, 1600], P('tensor', 'dp')
- grad_attn_norm_gain: float32 [1600], P('dp')
- grad_ssm_norm_gain: float32 [1600], P('dp')
- grad_norm_mid_gain: float32 [1600], P('dp')
- grad_w_gate: float32 [1600, 5504], P('dp', 'tensor')
- grad_w_up: float32 [1600, 5504], P('dp', 'tensor')
- grad_w_down: float32 [5504, 1600], P('tensor', 'dp')
Inputs may be any that keep to these rules, and one draw needn't show every extreme that they name: Every 16th token has valid = 1.
All inputs are finite; a program needn't handle non-finite values.
Results may differ from a plain program's by a relative error of at most 0.02.
The roundings to bfloat16 on the way count: a program that leaves them out, or rounds other values in their place, can miss the bound.
Values may be sent and summed in bfloat16 or wider, within the bound.
A program may use at most 448 MiB of HBM per device.

v0:
```python
import functools

import jax
import jax.numpy as jnp
from jax import lax
from jax.experimental import pallas as pl
from jax.experimental.pallas import tpu as pltpu
from jax.sharding import PartitionSpec as P

HEADS = 25
KV = 5
HEAD = 64
STATE = 16
RANK = 100
CONV = 4
WINDOW = 1024
BLOCK = 512
STRETCH = 64
LEN = 2048


EPSILON = 1e-06
MASKED = -1e30
HIGHEST = lax.Precision.HIGHEST


def normalize_t(values, gain):
    return values * lax.rsqrt(jnp.mean(values * values, axis=0, keepdims=True) + EPSILON) * gain


def join_rows_t(resid, attn_sum, ssm_sum, gain_attn, gain_ssm):
    return resid + 0.5 * (normalize_t(attn_sum, gain_attn) + normalize_t(ssm_sum, gain_ssm))


def dot_plain(left, right):
    return jnp.dot(left, right, preferred_element_type=jnp.float32)


def dot_last(left, right):
    return lax.dot_general(
        left, right, (((1,), (1,)), ((), ())), preferred_element_type=jnp.float32
    )


def dot_first(left, right):
    return lax.dot_general(
        left, right, (((0,), (0,)), ((), ())), preferred_element_type=jnp.float32
    )


def pick_groups(weight, first_slot, second_slot, group_width, axis):
    return jnp.concatenate(
        [
            lax.dynamic_slice_in_dim(weight, first_slot * group_width, group_width, axis),
            lax.dynamic_slice_in_dim(weight, second_slot * group_width, group_width, axis),
        ],
        axis=axis,
    )


PIECES = 4
MESH = pl.DeviceIdType.MESH


def tensor_peers():
    me = lax.axis_index("tensor")
    side = me + 1 - 2 * lax.rem(me, 2)
    cross = lax.rem(me + 2, 4)
    return me, side, cross, lax.rem(side + 2, 4)


def greet(peers):
    barrier = pltpu.get_barrier_semaphore()
    for peer in peers:
        pl.semaphore_signal(barrier, inc=1, device_id={"tensor": peer}, device_id_type=MESH)
    pl.semaphore_wait(barrier, len(peers))


def push(src, dst, sems, index, peer):
    copy = pltpu.make_async_remote_copy(
        src_ref=src,
        dst_ref=dst,
        send_sem=sems[0].at[index],
        recv_sem=sems[1].at[index],
        device_id={"tensor": peer},
        device_id_type=MESH,
    )
    copy.start()
    return copy


def columns(block, size):
    return pl.ds(pl.multiple_of(block * size, size), size)


def gather_kernel(part_ref, whole_ref, own_sem, *sems):
    me, side, cross, diag = tensor_peers()
    depth, size = part_ref.shape
    step = depth // PIECES
    mine = columns(me, size)
    theirs = columns(cross, size)
    greet((side, cross))
    own = pltpu.make_async_copy(part_ref, whole_ref.at[:, mine], own_sem)
    own.start()
    over, near, relay = [], [], []
    for piece in range(PIECES):
        rows = pl.ds(piece * step, step)
        over.append(
            push(part_ref.at[rows], whole_ref.at[rows, mine], sems[0:2], piece, cross)
        )
    for piece in range(PIECES):
        rows = pl.ds(piece * step, step)
        near.append(push(part_ref.at[rows], whole_ref.at[rows, mine], sems[2:4], piece, side))
    for piece in range(PIECES):
        rows = pl.ds(piece * step, step)
        over[piece].wait_recv()
        relay.append(
            push(whole_ref.at[rows, theirs], whole_ref.at[rows, theirs], sems[4:6], piece, side)
        )
    own.wait()
    for piece in range(PIECES):
        over[piece].wait_send()
        near[piece].wait()
        relay[piece].wait()


def gather_rows(part, call_id):
    depth, size = part.shape
    return pl.pallas_call(
        gather_kernel,
        name="gather_rows",
        in_specs=[pl.BlockSpec(memory_space=pl.ANY)],
        out_specs=pl.BlockSpec(memory_space=pl.ANY),
        out_shape=jax.ShapeDtypeStruct((depth, 4 * size), part.dtype),
        scratch_shapes=[pltpu.SemaphoreType.DMA] + [pltpu.SemaphoreType.DMA((PIECES,))] * 6,
        compiler_params=pltpu.CompilerParams(
            collective_id=call_id, has_side_effects=True, vmem_limit_bytes=1 << 20
        ),
        cost_estimate=pl.CostEstimate(
            flops=0, bytes_accessed=depth * size * 2 * 90, transcendentals=0
        ),
    )(part)


def first_kernel(part_ref, shard_ref, whole_ref, all_ref, own_sem, *sems):
    me, side, cross, diag = tensor_peers()
    depth, size = part_ref.shape
    step = depth // PIECES
    mine, theirs = columns(me, size), columns(cross, size)
    place = lax.axis_index("dp")
    spot, lane = lax.div(place, 2), lax.rem(place, 2)
    length = all_ref.shape[0] // 2
    partner = 2 * spot + 1 - lane
    barrier = pltpu.get_barrier_semaphore()
    for peer in (side, cross):
        pl.semaphore_signal(barrier, inc=1, device_id={"tensor": peer}, device_id_type=MESH)
    pl.semaphore_signal(barrier, inc=1, device_id={"dp": partner}, device_id_type=MESH)
    has_left, has_right = spot > 0, spot < length - 1

    @pl.when(has_left)
    def _():
        pl.semaphore_signal(barrier, inc=1, device_id={"dp": place - 2}, device_id_type=MESH)

    @pl.when(has_right)
    def _():
        pl.semaphore_signal(barrier, inc=1, device_id={"dp": place + 2}, device_id_type=MESH)

    pl.semaphore_wait(barrier, 3 + has_left.astype(jnp.int32) + has_right.astype(jnp.int32))

    def line(origin, group, peer, source):
        slot = all_ref.at[2 * origin + lane]
        return pltpu.make_async_remote_copy(
            src_ref=slot if source is None else source,
            dst_ref=slot,
            send_sem=sems[6 + 2 * group].at[origin],
            recv_sem=sems[7 + 2 * group].at[origin],
            device_id={"dp": peer},
            device_id_type=MESH,
        )

    to_right = lambda origin, source=None: line(origin, 0, place + 2, source)
    to_left = lambda origin, source=None: line(origin, 1, place - 2, source)
    to_partner = lambda origin, source=None: line(origin, 2, partner, source)

    own = pltpu.make_async_copy(part_ref, whole_ref.at[:, mine], own_sem.at[0])
    own.start()
    kept = pltpu.make_async_copy(shard_ref, all_ref.at[place], own_sem.at[1])
    kept.start()
    pl.when(has_right)(to_right(spot, shard_ref).start)
    pl.when(has_left)(to_left(spot, shard_ref).start)
    to_partner(spot, shard_ref).start()
    over, near, relay = [], [], []
    for piece in range(PIECES):
        rows = pl.ds(piece * step, step)
        over.append(push(part_ref.at[rows], whole_ref.at[rows, mine], sems[0:2], piece, cross))
    for piece in range(PIECES):
        rows = pl.ds(piece * step, step)
        near.append(push(part_ref.at[rows], whole_ref.at[rows, mine], sems[2:4], piece, side))

    def pass_on(hop):
        left, right = spot - hop, spot + hop

        @pl.when(left >= 0)
        def _():
            to_right(left).wait_recv()
            pl.when(has_right)(to_right(left).start)
            to_partner(left).start()

        @pl.when(right < length)
        def _():
            to_left(right).wait_recv()
            pl.when(has_left)(to_left(right).start)
            to_partner(right).start()

    hops = list(range(1, length))
    for piece in range(PIECES):
        rows = pl.ds(piece * step, step)
        over[piece].wait_recv()
        relay.append(
            push(whole_ref.at[rows, theirs], whole_ref.at[rows, theirs], sems[4:6], piece, side)
        )
        if piece and hops:
            pass_on(hops.pop(0))
    for hop in hops:
        pass_on(hop)
    own.wait()
    kept.wait()
    for piece in range(PIECES):
        over[piece].wait_send()
        near[piece].wait()
        relay[piece].wait()
    for origin in range(length):
        pl.when(has_right & (origin <= spot))(to_right(origin).wait_send)
        pl.when(has_left & (origin >= spot))(to_left(origin).wait_send)
        to_partner(origin).wait_send()
        arrival = pltpu.make_async_remote_copy(
            src_ref=shard_ref,
            dst_ref=all_ref.at[2 * origin + 1 - lane],
            send_sem=sems[10].at[origin],
            recv_sem=sems[11].at[origin],
            device_id={"dp": partner},
            device_id_type=MESH,
        )
        arrival.wait_recv()


def gather_first(part, shard):
    depth, size = part.shape
    groups = lax.axis_size("dp")
    anywhere = pl.BlockSpec(memory_space=pl.ANY)
    whole, stacked = pl.pallas_call(
        first_kernel,
        name="gather_first",
        in_specs=[anywhere] * 2,
        out_specs=[anywhere] * 2,
        out_shape=[
            jax.ShapeDtypeStruct((depth, 4 * size), part.dtype),
            jax.ShapeDtypeStruct((groups,) + shard.shape, shard.dtype),
        ],
        scratch_shapes=[pltpu.SemaphoreType.DMA((2,))]
        + [pltpu.SemaphoreType.DMA((PIECES,))] * 6
        + [pltpu.SemaphoreType.DMA((groups // 2,))] * 6,
        compiler_params=pltpu.CompilerParams(
            collective_id=14, has_side_effects=True, vmem_limit_bytes=1 << 20
        ),
        cost_estimate=pl.CostEstimate(flops=0, bytes_accessed=270 << 20, transcendentals=0),
    )(part, shard)
    return whole, stacked.reshape(-1, shard.shape[1])


def turn_kernel(combine, plan, n_in, n_out, *refs):
    part_ref, weight_ref = refs[:2]
    ins = refs[2 : 2 + n_in]
    whole_ref = refs[2 + n_in]
    outs = refs[3 + n_in : 3 + n_in + n_out]
    scratch = refs[3 + n_in + n_out :]
    weight_bufs, scratch = scratch[: len(plan)], scratch[len(plan) :]
    in_bufs, out_bufs = scratch[:n_in], scratch[n_in : n_in + n_out]
    weight_sem, in_sem, out_sem, own_sem = scratch[n_in + n_out : n_in + n_out + 4]
    sems = scratch[n_in + n_out + 4 :]
    me, side, cross, diag = tensor_peers()
    depth, size = part_ref.shape
    half = size // 2
    tiles = [(block, at) for block in (me, side) for at in (0, 1)]
    tiles += [(block, at) for at in (0, 1) for block in (cross, diag)]
    place = lambda block, at: pl.ds(pl.multiple_of(block * size + at * half, half), half)
    local = lambda at: pl.ds(at * half, half)

    weight_loads = [
        pltpu.make_async_copy(
            weight_ref.at[:, pl.ds(low, buf.shape[1])], buf, weight_sem.at[index]
        )
        for index, ((low, _), buf) in enumerate(zip(plan, weight_bufs))
    ]
    own = pltpu.make_async_copy(part_ref, whole_ref.at[:, columns(me, size)], own_sem)
    own.start()
    for load in weight_loads:
        load.start()

    def in_load(index, tile):
        return pltpu.make_async_copy(
            ins[index].at[place(*tiles[tile])],
            in_bufs[index].at[tile % 2],
            in_sem.at[index, tile % 2],
        )

    def out_store(index, tile):
        return pltpu.make_async_copy(
            out_bufs[index].at[tile % 2],
            outs[index].at[place(*tiles[tile])],
            out_sem.at[index, tile % 2],
        )

    for index in range(n_in):
        in_load(index, 0).start()
    greet((side, cross))
    over = [
        push(part_ref.at[:, local(at)], whole_ref.at[:, place(me, at)], sems[0:2], at, cross)
        for at in (0, 1)
    ]
    near = [
        push(part_ref.at[:, local(at)], whole_ref.at[:, place(me, at)], sems[2:4], at, side)
        for at in (0, 1)
    ]
    relay = [None, None]
    own.wait()
    for tile, (block, at) in enumerate(tiles):
        if tile + 1 < len(tiles):
            for index in range(n_in):
                in_load(index, tile + 1).start()
        if tile in (2, 3):
            near[at].wait_recv()
        if tile in (4, 6):
            over[at].wait_recv()
            relay[at] = push(
                whole_ref.at[:, place(cross, at)],
                whole_ref.at[:, place(cross, at)],
                sems[4:6],
                at,
                side,
            )
        if tile in (5, 7):
            relay[at].wait_recv()
        left = whole_ref[:, place(block, at)]
        products = []
        for index, (low, high) in enumerate(plan):
            if tile == 0:
                weight_loads[index].wait()
            products.append(dot_first(left, weight_bufs[index][:, : high - low]))
        for index in range(n_in):
            in_load(index, tile).wait()
        results = combine(products, [buf[tile % 2] for buf in in_bufs])
        for index, result in enumerate(results):
            if tile >= 2:
                out_store(index, tile - 2).wait()
            out_bufs[index][tile % 2] = result
            out_store(index, tile).start()
    for tile in (len(tiles) - 2, len(tiles) - 1):
        for index in range(n_out):
            out_store(index, tile).wait()
    for at in (0, 1):
        over[at].wait_send()
        near[at].wait_send()
        relay[at].wait_send()


def turn_rows(part, weight, ins, outs, plan, combine, call_id, name, micros):
    depth, size = part.shape
    half = size // 2
    anywhere = pl.BlockSpec(memory_space=pl.ANY)
    return pl.pallas_call(
        functools.partial(turn_kernel, combine, plan, len(ins), len(outs)),
        name=name,
        in_specs=[pl.BlockSpec(memory_space=pltpu.VMEM)] + [anywhere] * (1 + len(ins)),
        out_specs=[pl.BlockSpec(memory_space=pltpu.VMEM)] + [anywhere] * len(outs),
        out_shape=[jax.ShapeDtypeStruct((depth, 4 * size), part.dtype)]
        + [jax.ShapeDtypeStruct((4 * size, cols), dtype) for cols, dtype in outs],
        scratch_shapes=[
            pltpu.VMEM((depth, -(-(high - low) // 128) * 128), weight.dtype) for low, high in plan
        ]
        + [pltpu.VMEM((2, half, value.shape[1]), value.dtype) for value in ins]
        + [pltpu.VMEM((2, half, cols), dtype) for cols, dtype in outs]
        + [
            pltpu.SemaphoreType.DMA((len(plan),)),
            pltpu.SemaphoreType.DMA((max(len(ins), 1), 2)),
            pltpu.SemaphoreType.DMA((len(outs), 2)),
            pltpu.SemaphoreType.DMA,
        ]
        + [pltpu.SemaphoreType.DMA((2,))] * 6,
        compiler_params=pltpu.CompilerParams(
            collective_id=call_id, has_side_effects=True, vmem_limit_bytes=52 << 20
        ),
        cost_estimate=pl.CostEstimate(
            flops=0, bytes_accessed=int(micros * 3.6) << 20, transcendentals=0
        ),
    )(part, weight, *ins)


def forward_gate(products, _):
    gate, up = products
    return gate, up, (gate * jax.nn.sigmoid(gate) * up).astype(jnp.bfloat16)


def backward_gate(products, saved):
    (grad,), (gate, up) = products, saved
    sig = jax.nn.sigmoid(gate)
    grad_gate = grad * up * sig * (1.0 + gate * (1.0 - sig))
    return grad_gate.astype(jnp.bfloat16), (grad * gate * sig).astype(jnp.bfloat16)


def total_kernel(part_ref, out_ref, near_buf, own_buf, stage_buf, far_buf, low_buf, own_sem, *sems):
    me, side, cross, diag = tensor_peers()
    size, wide = low_buf.shape
    half = size // 2
    greet((side, cross))
    rows_of = lambda block, at: pl.ds(pl.multiple_of(block * size + at, half), half)
    pieces = (0, half)
    first = [
        push(part_ref.at[rows_of(diag, at)], near_buf.at[pl.ds(at, half)], sems[0:2], i, side)
        for i, at in enumerate(pieces)
    ]
    second = [
        push(part_ref.at[rows_of(side, at)], own_buf.at[pl.ds(at, half)], sems[2:4], i, side)
        for i, at in enumerate(pieces)
    ]
    third, over, near, relay = [], [], [], []
    for i, at in enumerate(pieces):
        rows = pl.ds(at, half)
        first[i].wait_recv()
        stage_buf[rows] = (part_ref[rows_of(cross, at)] + near_buf[rows]).astype(jnp.bfloat16)
        third.append(push(stage_buf.at[rows], far_buf.at[rows], sems[4:6], i, cross))
    for i, at in enumerate(pieces):
        rows = pl.ds(at, half)
        second[i].wait_recv()
        third[i].wait_recv()
        low_buf[rows] = (
            part_ref[rows_of(me, at)] + own_buf[rows] + far_buf[rows].astype(jnp.float32)
        ).astype(jnp.bfloat16)
        over.append(push(low_buf.at[rows], out_ref.at[rows_of(me, at)], sems[6:8], i, cross))
        near.append(push(low_buf.at[rows], out_ref.at[rows_of(me, at)], sems[8:10], i, side))
    own = pltpu.make_async_copy(
        low_buf, out_ref.at[pl.ds(pl.multiple_of(me * size, size), size)], own_sem
    )
    own.start()
    for i, at in enumerate(pieces):
        over[i].wait_recv()
        relay.append(
            push(out_ref.at[rows_of(cross, at)], out_ref.at[rows_of(cross, at)], sems[10:12], i, side)
        )
    own.wait()
    for i in range(2):
        for group in (first, second, third, over):
            group[i].wait_send()
        near[i].wait()
        relay[i].wait()


def total_rows(part, call_id):
    tokens, wide = part.shape
    size = tokens // 4
    whole = pl.BlockSpec(memory_space=pltpu.VMEM)
    return pl.pallas_call(
        total_kernel,
        name="total_rows",
        in_specs=[whole],
        out_specs=whole,
        out_shape=jax.ShapeDtypeStruct((tokens, wide), jnp.bfloat16),
        scratch_shapes=[
            pltpu.VMEM((size, wide), jnp.float32),
            pltpu.VMEM((size, wide), jnp.float32),
            pltpu.VMEM((size, wide), jnp.bfloat16),
            pltpu.VMEM((size, wide), jnp.bfloat16),
            pltpu.VMEM((size, wide), jnp.bfloat16),
            pltpu.SemaphoreType.DMA,
        ]
        + [pltpu.SemaphoreType.DMA((2,))] * 12,
        compiler_params=pltpu.CompilerParams(
            collective_id=call_id, has_side_effects=True, vmem_limit_bytes=32 << 20
        ),
        cost_estimate=pl.CostEstimate(flops=0, bytes_accessed=60 << 20, transcendentals=0),
    )(part)


def hello_kernel(gain_ref, count_ref, gains_ref, counts_ref, sum_buf, local_buf, *sems):
    me = lax.axis_index("tensor")
    place = lax.axis_index("dp")
    ranks, groups = local_buf.shape[0], gains_ref.shape[0]
    barrier = pltpu.get_barrier_semaphore()
    others = [{"tensor": lax.rem(me + hop, ranks)} for hop in range(1, ranks)]
    far = [{"dp": lax.rem(place + hop, groups)} for hop in range(1, groups)]
    for peer in others + far:
        pl.semaphore_signal(barrier, inc=1, device_id=peer, device_id_type=MESH)
    pl.semaphore_wait(barrier, len(others) + len(far))

    def send(src, dst, index, peer):
        copy = pltpu.make_async_remote_copy(
            src_ref=src,
            dst_ref=dst,
            send_sem=sems[0].at[index],
            recv_sem=sems[1].at[index],
            device_id=peer,
            device_id_type=MESH,
        )
        copy.start()
        return copy

    first = [send(count_ref, local_buf.at[me], i, peer) for i, peer in enumerate(others)]
    local_buf[me] = count_ref[...]
    gains_ref[place] = gain_ref[...]
    base = len(first)
    second = [send(gain_ref, gains_ref.at[place], base + i, peer) for i, peer in enumerate(far)]
    base += len(second)
    for copy in first:
        copy.wait()
    sum_buf[...] = jnp.sum(local_buf[...], axis=0)
    counts_ref[place] = sum_buf[...]
    third = [send(sum_buf, counts_ref.at[place], base + i, peer) for i, peer in enumerate(far)]
    for copy in second + third:
        copy.wait()


def hello(gains, count):
    wide = -(-gains.shape[1] // 128) * 128
    block = jnp.zeros((8, wide), jnp.float32)
    block = lax.dynamic_update_slice(block, gains.astype(jnp.float32), (0, 0))
    counts = jnp.full((8, 128), count, jnp.float32)
    groups, ranks = lax.axis_size("dp"), lax.axis_size("tensor")
    copies = ranks - 1 + 2 * (groups - 1)
    whole = pl.BlockSpec(memory_space=pltpu.VMEM)
    gains_all, counts_all = pl.pallas_call(
        hello_kernel,
        name="hello",
        in_specs=[whole, whole],
        out_specs=[whole, whole],
        out_shape=[
            jax.ShapeDtypeStruct((groups, 8, wide), jnp.float32),
            jax.ShapeDtypeStruct((groups, 8, 128), jnp.float32),
        ],
        scratch_shapes=[
            pltpu.VMEM((8, 128), jnp.float32),
            pltpu.VMEM((ranks, 8, 128), jnp.float32),
        ]
        + [pltpu.SemaphoreType.DMA((copies,))] * 2,
        compiler_params=pltpu.CompilerParams(collective_id=0, has_side_effects=True),
        cost_estimate=pl.CostEstimate(flops=0, bytes_accessed=30 << 20, transcendentals=0),
    )(block, counts)
    gains_full = gains_all[:, :4, : gains.shape[1]].transpose(1, 0, 2).reshape(4, -1)
    return gains_full, jnp.sum(counts_all[:, 0, 0])


TILE = 400


def weights_kernel(plan, *refs):
    out_ref = refs[-1]
    index = 0
    for mode, offset, size, pad in plan:
        left = refs[index][...]
        if mode == "copy":
            product = left
            index += 1
        else:
            right = refs[index + 1][...]
            product = dot_last(left, right) if mode == "flip" else dot_plain(left, right)
            index += 2
        out_ref[:, offset : offset + size] = product.astype(jnp.bfloat16)
        if pad:
            out_ref[:, offset + size : offset + size + pad] = jnp.zeros(
                (out_ref.shape[0], pad), jnp.bfloat16
            )


def weight_grads(pairs, name, micros, tight=False):
    rows = pairs[0][0].shape[0]
    tile = TILE if rows % TILE == 0 else rows
    plan, specs, operands, offset = [], [], [], 0
    for left, right, flip in pairs:
        source = left if right is None else right
        size = source.shape[0] if flip else source.shape[1]
        pad = 0 if tight else -size % 128
        mode = "copy" if right is None else "flip" if flip else "plain"
        plan.append((mode, offset, size, pad))
        offset += size + pad
        specs.append(pl.BlockSpec((tile, left.shape[1]), lambda i: (i, 0)))
        operands.append(left)
        if right is not None:
            specs.append(
                pl.BlockSpec(right.shape, lambda i: (0, 0), pipeline_mode=pl.Buffered(1))
            )
            operands.append(right)
    return pl.pallas_call(
        functools.partial(weights_kernel, plan),
        name=name,
        grid=(rows // tile,),
        in_specs=specs,
        out_specs=pl.BlockSpec((tile, offset), lambda i: (i, 0)),
        out_shape=jax.ShapeDtypeStruct((rows, offset), jnp.bfloat16),
        compiler_params=pltpu.CompilerParams(vmem_limit_bytes=52 << 20),
        cost_estimate=pl.CostEstimate(
            flops=0, bytes_accessed=int(micros * 3.6) << 20, transcendentals=0
        ),
    )(*operands)


def farewell_kernel(part_ref, out_ref, group_buf, sum_buf, rank_buf, *sems):
    me = lax.axis_index("tensor")
    place = lax.axis_index("dp")
    ranks, groups = rank_buf.shape[0], group_buf.shape[0]
    barrier = pltpu.get_barrier_semaphore()
    others = [lax.rem(me + hop, ranks) for hop in range(1, ranks)]
    far = [lax.rem(place + hop, groups) for hop in range(1, groups)]
    for peer in others:
        pl.semaphore_signal(barrier, inc=1, device_id={"tensor": peer}, device_id_type=MESH)
    for peer in far:
        pl.semaphore_signal(barrier, inc=1, device_id={"dp": peer}, device_id_type=MESH)
    pl.semaphore_wait(barrier, len(others) + len(far))

    def send(src, dst, index, peer):
        copy = pltpu.make_async_remote_copy(
            src_ref=src,
            dst_ref=dst,
            send_sem=sems[0].at[index],
            recv_sem=sems[1].at[index],
            device_id=peer,
            device_id_type=MESH,
        )
        copy.start()
        return copy

    first = [
        send(part_ref.at[peer], group_buf.at[place], i, {"dp": peer}) for i, peer in enumerate(far)
    ]
    group_buf[place] = part_ref[place]
    for copy in first:
        copy.wait()
    sum_buf[...] = jnp.sum(group_buf[...], axis=0)
    rank_buf[me] = sum_buf[...]
    second = [
        send(sum_buf, rank_buf.at[me], len(first) + i, {"tensor": peer})
        for i, peer in enumerate(others)
    ]
    for copy in second:
        copy.wait()
    out_ref[...] = jnp.sum(rank_buf[...], axis=0)


def farewell(grads):
    groups, ranks = lax.axis_size("dp"), lax.axis_size("tensor")
    kinds, total = grads.shape
    own = total // groups
    wide = -(-own // 128) * 128
    parts = jnp.pad(
        grads.reshape(kinds, groups, own).transpose(1, 0, 2),
        ((0, 0), (0, 8 - kinds), (0, wide - own)),
    )
    whole = pl.BlockSpec(memory_space=pltpu.VMEM)
    summed = pl.pallas_call(
        farewell_kernel,
        name="farewell",
        in_specs=[whole],
        out_specs=whole,
        out_shape=jax.ShapeDtypeStruct((8, wide), jnp.float32),
        scratch_shapes=[
            pltpu.VMEM((groups, 8, wide), jnp.float32),
            pltpu.VMEM((8, wide), jnp.float32),
            pltpu.VMEM((ranks, 8, wide), jnp.float32),
        ]
        + [pltpu.SemaphoreType.DMA((groups + ranks - 2,))] * 2,
        compiler_params=pltpu.CompilerParams(
            collective_id=4, has_side_effects=True, vmem_limit_bytes=4 << 20
        ),
        cost_estimate=pl.CostEstimate(flops=0, bytes_accessed=40 << 20, transcendentals=0),
    )(parts)
    return summed[:kinds, :own]


def stack_kernel(part_ref, whole_ref, own_sem, *sems):
    me, side, cross, diag = tensor_peers()
    step = part_ref.shape[1] // 2
    greet((side, cross))
    own = pltpu.make_async_copy(part_ref, whole_ref.at[me], own_sem)
    own.start()
    cols = [pl.ds(0, step), pl.ds(step, step)]
    over = [
        push(part_ref.at[:, at], whole_ref.at[me, :, at], sems[0:2], i, cross)
        for i, at in enumerate(cols)
    ]
    near = [
        push(part_ref.at[:, at], whole_ref.at[me, :, at], sems[2:4], i, side)
        for i, at in enumerate(cols)
    ]
    relay = []
    for i, at in enumerate(cols):
        over[i].wait_recv()
        relay.append(
            push(whole_ref.at[cross, :, at], whole_ref.at[cross, :, at], sems[4:6], i, side)
        )
    own.wait()
    for i in range(2):
        over[i].wait_send()
        near[i].wait()
        relay[i].wait()


def gather_stack(part, call_id):
    return pl.pallas_call(
        stack_kernel,
        name="gather_stack",
        in_specs=[pl.BlockSpec(memory_space=pl.ANY)],
        out_specs=pl.BlockSpec(memory_space=pl.ANY),
        out_shape=jax.ShapeDtypeStruct((4,) + part.shape, part.dtype),
        scratch_shapes=[pltpu.SemaphoreType.DMA] + [pltpu.SemaphoreType.DMA((2,))] * 6,
        compiler_params=pltpu.CompilerParams(
            collective_id=call_id, has_side_effects=True, vmem_limit_bytes=1 << 20
        ),
        cost_estimate=pl.CostEstimate(flops=0, bytes_accessed=60 << 20, transcendentals=0),
    )(part)


def product_kernel(plan, leads, right_flips, *refs):
    left_count = len(leads)
    lefts = [ref if lead is None else ref.at[lead] for ref, (lead, _) in zip(refs, leads)]
    right_count = len(right_flips)
    rights = refs[left_count : left_count + right_count]
    out_ref = refs[left_count + right_count]
    scratch = refs[left_count + right_count + 1 :]
    left_bufs = scratch[:left_count]
    right_bufs = scratch[left_count : left_count + right_count]
    diag_buf, side_buf, near_buf, own_buf, stage_buf, far_buf, left_sem, right_sem = scratch[
        left_count + right_count : left_count + right_count + 8
    ]
    sems = scratch[left_count + right_count + 8 :]
    me, side, cross, diag = tensor_peers()
    depth, size = out_ref.shape
    step = depth // PIECES
    rows_of = lambda piece: pl.ds(pl.multiple_of(piece * step, 16), step)

    def left_load(index, piece):
        rows = rows_of(piece)
        start = leads[index][1]
        source = lefts[index].at[rows]
        if start is not None:
            source = lefts[index].at[rows, pl.ds(start, left_bufs[index].shape[1])]
        return pltpu.make_async_copy(source, left_bufs[index].at[rows], left_sem.at[index, piece])

    def right_load(index, order, block):
        at = columns(block, size)
        view = (slice(None), at) if right_flips[index] else (at,)
        return pltpu.make_async_copy(
            rights[index].at[view], right_bufs[index].at[view], right_sem.at[index, order]
        )

    turns = (diag, cross, side, me)
    for order, block in enumerate(turns):
        for index in range(right_count):
            right_load(index, order, block).start()
        for index in range(left_count):
            left_load(index, order).start()
    greet((side, cross))

    def product(piece, block):
        rows, at = rows_of(piece), columns(block, size)
        total = jnp.zeros((step, size), jnp.float32)
        for left, low_col, high_col, right in plan:
            weight = left_bufs[left][rows, low_col:high_col]
            if right_flips[right]:
                total += dot_plain(weight, right_bufs[right][:, at])
            else:
                total += dot_last(weight, right_bufs[right][at, :])
        return total

    def transfer(src, dst, group, piece, peer):
        rows = rows_of(piece)
        return pltpu.make_async_remote_copy(
            src_ref=src.at[rows],
            dst_ref=dst.at[rows],
            send_sem=sems[2 * group].at[piece],
            recv_sem=sems[2 * group + 1].at[piece],
            device_id={"tensor": peer},
            device_id_type=MESH,
        )

    first = lambda piece: transfer(diag_buf, near_buf, 0, piece, side)
    second = lambda piece: transfer(side_buf, own_buf, 1, piece, side)
    third = lambda piece: transfer(stage_buf, far_buf, 2, piece, cross)

    for order in (0, 1):
        for index in range(right_count):
            right_load(index, order, turns[order]).wait()

    def outward(piece, carry):
        rows = rows_of(piece)
        for index in range(left_count):
            left_load(index, piece).wait()
        diag_buf[rows] = product(piece, diag).astype(jnp.bfloat16)
        first(piece).start()
        kept = product(piece, cross)
        first(piece).wait_recv()
        stage_buf[rows] = (kept + near_buf[rows].astype(jnp.float32)).astype(jnp.bfloat16)
        third(piece).start()
        return carry

    lax.fori_loop(0, PIECES, outward, 0)
    for order in (2, 3):
        for index in range(right_count):
            right_load(index, order, turns[order]).wait()

    def inward(piece, carry):
        rows = rows_of(piece)
        side_buf[rows] = product(piece, side).astype(jnp.bfloat16)
        second(piece).start()
        out_ref[rows] = product(piece, me)
        return carry

    lax.fori_loop(0, PIECES, inward, 0)

    def finish(piece, carry):
        rows = rows_of(piece)
        second(piece).wait_recv()
        third(piece).wait_recv()
        out_ref[rows] += own_buf[rows].astype(jnp.float32) + far_buf[rows].astype(jnp.float32)
        first(piece).wait_send()
        second(piece).wait_send()
        third(piece).wait_send()
        return carry

    lax.fori_loop(0, PIECES, finish, 0)


def product_reduce(lefts, rights, plan, call_id, name, micros):
    leads = tuple((lead, start) for _, lead, start, _ in lefts)
    widths = [size for _, _, _, size in lefts]
    lefts = [left for left, _, _, _ in lefts]
    depth = lefts[0].shape[-2]
    right_flips = tuple(flip for _, flip in rights)
    tokens = rights[0][0].shape[1] if right_flips[0] else rights[0][0].shape[0]
    size = tokens // 4
    anywhere = pl.BlockSpec(memory_space=pl.ANY)
    return pl.pallas_call(
        functools.partial(product_kernel, plan, leads, right_flips),
        name=name,
        in_specs=[anywhere] * (len(lefts) + len(rights)),
        out_specs=pl.BlockSpec(memory_space=pltpu.VMEM),
        out_shape=jax.ShapeDtypeStruct((depth, size), jnp.float32),
        scratch_shapes=[pltpu.VMEM((depth, size), jnp.bfloat16) for size in widths]
        + [pltpu.VMEM(right.shape, right.dtype) for right, _ in rights]
        + [pltpu.VMEM((depth, size), jnp.bfloat16)] * 6
        + [
            pltpu.SemaphoreType.DMA((len(lefts), PIECES)),
            pltpu.SemaphoreType.DMA((len(rights), 4)),
        ]
        + [pltpu.SemaphoreType.DMA((PIECES,))] * 6,
        compiler_params=pltpu.CompilerParams(
            collective_id=call_id, has_side_effects=True, vmem_limit_bytes=48 << 20
        ),
        cost_estimate=pl.CostEstimate(
            flops=0, bytes_accessed=int(micros * 3.6) << 20, transcendentals=0
        ),
    )(*lefts, *[right for right, _ in rights])


def spread_kernel(part_ref, out_ref, own_sem, *sems):
    rank, place = lax.axis_index("tensor"), lax.axis_index("dp")
    share = out_ref.shape[0]
    target, slot = lax.div(place, share), lax.rem(place, share)
    replica = lax.rem(place, 4)
    barrier = pltpu.get_barrier_semaphore()
    for index in range(share):
        source = rank * share + index

        @pl.when((source != place) | (replica != rank))
        def _():
            pl.semaphore_signal(
                barrier,
                inc=1,
                device_id={"dp": source, "tensor": replica},
                device_id_type=MESH,
            )

    goals = [(rank + 4 * index != place) | (target != rank) for index in range(share)]
    pl.semaphore_wait(barrier, sum(goal.astype(jnp.int32) for goal in goals))

    def outgoing(index):
        goal = rank + 4 * index
        copy = pltpu.make_async_remote_copy(
            src_ref=part_ref,
            dst_ref=out_ref.at[slot],
            send_sem=sems[0].at[index],
            recv_sem=sems[1].at[slot],
            device_id={"dp": goal, "tensor": target},
            device_id_type=MESH,
        )
        return copy, (goal != place) | (target != rank)

    own = pltpu.make_async_copy(part_ref, out_ref.at[slot], own_sem)
    for index in range(share):
        copy, away = outgoing(index)
        pl.when(away)(copy.start)
        pl.when(jnp.logical_not(away))(own.start)
    for index in range(share):
        copy, away = outgoing(index)
        pl.when(away)(copy.wait_send)
        pl.when(jnp.logical_not(away))(own.wait)
        source = rank * share + index
        arrival = pltpu.make_async_remote_copy(
            src_ref=part_ref,
            dst_ref=out_ref.at[index],
            send_sem=sems[0].at[index],
            recv_sem=sems[1].at[index],
            device_id={"dp": source, "tensor": replica},
            device_id_type=MESH,
        )
        pl.when((source != place) | (replica != rank))(arrival.wait_recv)


def inner_spread(part):
    groups, ranks = lax.axis_size("dp"), lax.axis_size("tensor")
    share = groups // ranks
    rows, cols = part.shape
    padded = jnp.pad(part, ((0, -rows % 16), (0, -cols % 128)))
    whole = pl.BlockSpec(memory_space=pltpu.VMEM)
    spread = pl.pallas_call(
        spread_kernel,
        name="inner_spread",
        in_specs=[whole],
        out_specs=whole,
        out_shape=jax.ShapeDtypeStruct((share,) + padded.shape, part.dtype),
        scratch_shapes=[pltpu.SemaphoreType.DMA] + [pltpu.SemaphoreType.DMA((share,))] * 2,
        compiler_params=pltpu.CompilerParams(
            collective_id=12, has_side_effects=True, vmem_limit_bytes=8 << 20
        ),
        cost_estimate=pl.CostEstimate(flops=0, bytes_accessed=40 << 20, transcendentals=0),
    )(padded)
    return spread[:, :rows, :cols].reshape(share * rows, cols)


def final_kernel(part_ref, inner_ref, whole_ref, owned_ref, own_sem, *sems):
    me, side, cross, diag = tensor_peers()
    place = lax.axis_index("dp")
    ranks = owned_ref.shape[0]
    share = lax.axis_size("dp") // ranks
    owner, slot = me * share + lax.div(place, ranks), lax.rem(place, ranks)
    source_rank, source_base = lax.div(place, share), ranks * lax.rem(place, share)
    barrier = pltpu.get_barrier_semaphore()
    for peer in (side, cross):
        pl.semaphore_signal(barrier, inc=1, device_id={"tensor": peer}, device_id_type=MESH)
    for index in range(ranks):
        source = source_base + index

        @pl.when((source != place) | (source_rank != me))
        def _():
            pl.semaphore_signal(
                barrier,
                inc=1,
                device_id={"dp": source, "tensor": source_rank},
                device_id_type=MESH,
            )

    goals = [(owner != place) | (me != index) for index in range(ranks)]
    pl.semaphore_wait(barrier, 2 + sum(goal.astype(jnp.int32) for goal in goals))

    step = part_ref.shape[1] // 2
    own = pltpu.make_async_copy(part_ref, whole_ref.at[me], own_sem.at[0])
    own.start()
    cols = [pl.ds(0, step), pl.ds(step, step)]
    over = [
        push(part_ref.at[:, at], whole_ref.at[me, :, at], sems[0:2], i, cross)
        for i, at in enumerate(cols)
    ]
    near = [
        push(part_ref.at[:, at], whole_ref.at[me, :, at], sems[2:4], i, side)
        for i, at in enumerate(cols)
    ]
    kept = pltpu.make_async_copy(inner_ref, owned_ref.at[slot], own_sem.at[1])

    def outgoing(index):
        copy = pltpu.make_async_remote_copy(
            src_ref=inner_ref,
            dst_ref=owned_ref.at[slot],
            send_sem=sems[6].at[index],
            recv_sem=sems[7].at[slot],
            device_id={"dp": owner, "tensor": index},
            device_id_type=MESH,
        )
        return copy, (owner != place) | (me != index)

    for index in range(ranks):
        copy, away = outgoing(index)
        pl.when(away)(copy.start)
        pl.when(jnp.logical_not(away))(kept.start)
    relay = []
    for i, at in enumerate(cols):
        over[i].wait_recv()
        relay.append(
            push(whole_ref.at[cross, :, at], whole_ref.at[cross, :, at], sems[4:6], i, side)
        )
    own.wait()
    for i in range(2):
        over[i].wait_send()
        near[i].wait()
        relay[i].wait()
    for index in range(ranks):
        copy, away = outgoing(index)
        pl.when(away)(copy.wait_send)
        pl.when(jnp.logical_not(away))(kept.wait)
        source = source_base + index
        arrival = pltpu.make_async_remote_copy(
            src_ref=inner_ref,
            dst_ref=owned_ref.at[index],
            send_sem=sems[6].at[index],
            recv_sem=sems[7].at[index],
            device_id={"dp": source, "tensor": source_rank},
            device_id_type=MESH,
        )
        pl.when((source != place) | (source_rank != me))(arrival.wait_recv)


def gather_final(part, inner):
    anywhere = pl.BlockSpec(memory_space=pl.ANY)
    return pl.pallas_call(
        final_kernel,
        name="gather_final",
        in_specs=[anywhere] * 2,
        out_specs=[anywhere] * 2,
        out_shape=[
            jax.ShapeDtypeStruct((4,) + part.shape, part.dtype),
            jax.ShapeDtypeStruct((4,) + inner.shape, inner.dtype),
        ],
        scratch_shapes=[pltpu.SemaphoreType.DMA((2,))]
        + [pltpu.SemaphoreType.DMA((2,))] * 6
        + [pltpu.SemaphoreType.DMA((4,))] * 2,
        compiler_params=pltpu.CompilerParams(
            collective_id=9, has_side_effects=True, vmem_limit_bytes=1 << 20
        ),
        cost_estimate=pl.CostEstimate(flops=0, bytes_accessed=60 << 20, transcendentals=0),
    )(part, inner)


BQ = 256
BK = 256


def attn_bias(q_base, k_base, segq_row, segk_col):
    q_pos = q_base + lax.broadcasted_iota(jnp.int32, (BK, BQ), 1)
    k_pos = k_base + lax.broadcasted_iota(jnp.int32, (BK, BQ), 0)
    offset = q_pos - k_pos
    allowed = (offset >= 0) & (offset < WINDOW) & (segk_col == segq_row)
    return jnp.where(allowed, 0.0, MASKED)


def flip_rows(cols_ref, rows_scr):
    for at in range(0, rows_scr.shape[0], BK):
        block = cols_ref[:, at : at + BK].astype(jnp.float32)
        rows_scr[at : at + BK] = jnp.transpose(block).astype(jnp.bfloat16)


def attn_fwd_kernel(first_ref, qt_ref, kt_ref, vt_ref, segr_ref, mask_ref, ot_ref, lse_ref,
                    max_scr, sum_scr, acc_scr, k_scr):
    heads = qt_ref.shape[0] // HEAD
    block = pl.program_id(1)
    q_base = block * BQ

    @pl.when(block == 0)
    def _():
        flip_rows(kt_ref, k_scr)

    max_scr[...] = jnp.full_like(max_scr, MASKED)
    sum_scr[...] = jnp.zeros_like(sum_scr)
    acc_scr[...] = jnp.zeros_like(acc_scr)
    segq_row = segr_ref[0:1, :]

    def body(j, carry):
        k_base = pl.multiple_of(j * BK, BK)
        rows = pl.ds(k_base, BK)
        bias = attn_bias(q_base, k_base, segq_row, mask_ref[rows, 4:5])
        k_blk = k_scr[rows, :]
        v_blk = vt_ref[:, rows]
        for head in range(heads):
            cols = slice(head * HEAD, (head + 1) * HEAD)
            scores = dot_plain(k_blk, qt_ref[cols, :]) * 0.125 + bias
            old_max = max_scr[head : head + 1]
            new_max = jnp.maximum(old_max, jnp.max(scores, axis=0, keepdims=True))
            expo = jnp.exp(scores - new_max)
            ratio = jnp.exp(old_max - new_max)
            max_scr[head : head + 1] = new_max
            sum_scr[head : head + 1] = sum_scr[head : head + 1] * ratio + jnp.sum(
                expo, axis=0, keepdims=True
            )
            acc_scr[cols] = acc_scr[cols] * ratio + dot_plain(v_blk, expo.astype(jnp.bfloat16))
        return carry

    start = first_ref[pl.program_id(0) * pl.num_programs(1) + block]
    lax.fori_loop(start, block + 1, body, 0)
    for head in range(heads):
        cols = slice(head * HEAD, (head + 1) * HEAD)
        total = jnp.maximum(sum_scr[head : head + 1], 1e-30)
        ot_ref[cols] = (acc_scr[cols] / total).astype(jnp.bfloat16)
        lse_ref[0, head : head + 1] = max_scr[head : head + 1] + jnp.log(total)


def attn_specs(slots, group, tokens):
    queries = pl.BlockSpec((group, BQ), lambda s, i, f: (s, i))
    base = slots * group // HEAD
    keys = pl.BlockSpec((HEAD, tokens), lambda s, i, f: (base + s, 0))
    values = pl.BlockSpec((HEAD, tokens), lambda s, i, f: (base + slots + s, 0))
    stats = pl.BlockSpec((1, 8, BQ), lambda s, i, f: (s, 0, i))
    seg_row = pl.BlockSpec((1, BQ), lambda s, i, f: (0, i))
    seg_col = pl.BlockSpec((tokens, 8), lambda s, i, f: (0, 0))
    return queries, keys, values, stats, seg_row, seg_col


def attn_forward(first, qkv_t, seg_row, masks, slots):
    tokens = qkv_t.shape[1]
    group = qkv_t.shape[0] // slots - 2 * HEAD
    queries, keys, values, stats, segr, segc = attn_specs(slots, group, tokens)
    return pl.pallas_call(
        attn_fwd_kernel,
        name="attn_fwd",
        grid_spec=pltpu.PrefetchScalarGridSpec(
            num_scalar_prefetch=1,
            grid=(slots, tokens // BQ),
            in_specs=[queries, keys, values, segr, segc],
            out_specs=[queries, stats],
            scratch_shapes=[
                pltpu.VMEM((8, BQ), jnp.float32),
                pltpu.VMEM((8, BQ), jnp.float32),
                pltpu.VMEM((group, BQ), jnp.float32),
                pltpu.VMEM((tokens, HEAD), jnp.bfloat16),
            ],
        ),
        out_shape=[
            jax.ShapeDtypeStruct((slots * group, tokens), jnp.bfloat16),
            jax.ShapeDtypeStruct((slots, 8, tokens), jnp.float32),
        ],
        compiler_params=pltpu.CompilerParams(vmem_limit_bytes=32 << 20),
        cost_estimate=pl.CostEstimate(flops=0, bytes_accessed=150 << 20, transcendentals=0),
    )(first, qkv_t, qkv_t, qkv_t, seg_row, masks)


def attn_bwd_kernel(first_ref, qt_ref, dot_ref, ot_ref, lse_ref, kt_ref, vt_ref, segr_ref, mask_ref,
                    grad_ref, delta_scr, acc_scr, q_scr, do_scr, k_scr, v_scr, gk_scr, gv_scr):
    group = qt_ref.shape[0]
    heads = group // HEAD
    slot = pl.program_id(0)
    slots = pl.num_programs(0)
    block = pl.program_id(1)
    q_base = pl.multiple_of(block * BQ, BQ)

    @pl.when(block == 0)
    def _():
        flip_rows(kt_ref, k_scr)
        flip_rows(vt_ref, v_scr)
        gk_scr[...] = jnp.zeros_like(gk_scr)
        gv_scr[...] = jnp.zeros_like(gv_scr)

    acc_scr[...] = jnp.zeros_like(acc_scr)
    start = first_ref[slot * pl.num_programs(1) + block]

    @pl.when(start <= block)
    def _():
        for head in range(heads):
            cols = slice(head * HEAD, (head + 1) * HEAD)
            grad_out = dot_ref[cols].astype(jnp.float32)
            delta_scr[head : head + 1] = jnp.sum(
                grad_out * ot_ref[cols].astype(jnp.float32), axis=0, keepdims=True
            )
            q_scr[head] = jnp.transpose(qt_ref[cols].astype(jnp.float32)).astype(jnp.bfloat16)
            do_scr[head] = jnp.transpose(grad_out).astype(jnp.bfloat16)

    segq_row = segr_ref[0:1, :]

    def body(j, carry):
        k_base = pl.multiple_of(j * BK, BK)
        rows = pl.ds(k_base, BK)
        bias = attn_bias(q_base, k_base, segq_row, mask_ref[rows, 4:5])
        k_blk = k_scr[rows, :]
        kt_blk = kt_ref[:, rows]
        v_blk = v_scr[rows, :]
        gk = jnp.zeros((BK, HEAD), jnp.float32)
        gv = jnp.zeros((BK, HEAD), jnp.float32)
        for head in range(heads):
            cols = slice(head * HEAD, (head + 1) * HEAD)
            scores = dot_plain(k_blk, qt_ref[cols, :]) * 0.125 + bias
            probs = jnp.exp(scores - lse_ref[0, head : head + 1])
            grad_p = dot_plain(v_blk, dot_ref[cols, :])
            grad_s = (probs * (grad_p - delta_scr[head : head + 1])).astype(jnp.bfloat16)
            gv += dot_plain(probs.astype(jnp.bfloat16), do_scr[head])
            gk += dot_plain(grad_s, q_scr[head])
            acc_scr[cols] += dot_plain(kt_blk, grad_s)
        gk_scr[rows, :] += gk * 0.125
        gv_scr[rows, :] += gv
        return carry

    lax.fori_loop(start, block + 1, body, 0)
    grad_ref[pl.ds(pl.multiple_of(slot * group, HEAD), group), pl.ds(q_base, BQ)] = (
        acc_scr[...] * 0.125
    ).astype(jnp.bfloat16)

    @pl.when(block == pl.num_programs(1) - 1)
    def _():
        key_rows = pl.ds(pl.multiple_of(slots * group + slot * HEAD, HEAD), HEAD)
        value_rows = pl.ds(pl.multiple_of(slots * group + (slots + slot) * HEAD, HEAD), HEAD)
        for at in range(0, gk_scr.shape[0], BK):
            cols = pl.ds(at, BK)
            grad_ref[key_rows, cols] = jnp.transpose(gk_scr[at : at + BK]).astype(jnp.bfloat16)
            grad_ref[value_rows, cols] = jnp.transpose(gv_scr[at : at + BK]).astype(jnp.bfloat16)


def attn_backward(first, qkv_t, do_t, o_t, lse, seg_row, masks, slots):
    width, tokens = qkv_t.shape
    group = width // slots - 2 * HEAD
    queries, keys, values, stats, segr, segc = attn_specs(slots, group, tokens)
    return pl.pallas_call(
        attn_bwd_kernel,
        name="attn_bwd",
        grid_spec=pltpu.PrefetchScalarGridSpec(
            num_scalar_prefetch=1,
            grid=(slots, tokens // BQ),
            in_specs=[queries, queries, queries, stats, keys, values, segr, segc],
            out_specs=pl.BlockSpec((width, tokens), lambda s, i, f: (0, 0)),
            scratch_shapes=[
                pltpu.VMEM((8, BQ), jnp.float32),
                pltpu.VMEM((group, BQ), jnp.float32),
                pltpu.VMEM((group // HEAD, BQ, HEAD), jnp.bfloat16),
                pltpu.VMEM((group // HEAD, BQ, HEAD), jnp.bfloat16),
                pltpu.VMEM((tokens, HEAD), jnp.bfloat16),
                pltpu.VMEM((tokens, HEAD), jnp.bfloat16),
                pltpu.VMEM((tokens, HEAD), jnp.float32),
                pltpu.VMEM((tokens, HEAD), jnp.float32),
            ],
        ),
        out_shape=jax.ShapeDtypeStruct((width, tokens), jnp.bfloat16),
        compiler_params=pltpu.CompilerParams(vmem_limit_bytes=40 << 20),
        cost_estimate=pl.CostEstimate(flops=0, bytes_accessed=160 << 20, transcendentals=0),
    )(first, qkv_t, do_t, o_t, lse, qkv_t, qkv_t, seg_row, masks)


def first_blocks(segs_flat):
    tokens = segs_flat.shape[0]
    starts = segs_flat[::BQ]
    positions = jnp.arange(tokens // BQ, dtype=jnp.int32) * BQ
    seg_start = jnp.sum((segs_flat[None, :] < starts[:, None]).astype(jnp.int32), axis=1)
    return jnp.maximum(jnp.maximum(seg_start, positions - WINDOW + 1), 0) // BK


def conv_rows(x_in, conv_w, conv_b, segs_grid):
    seq_count, seq_len = segs_grid.shape
    width = x_in.shape[1]
    grid = x_in.reshape(seq_count, seq_len, width)
    pad_x = jnp.concatenate([jnp.zeros((seq_count, CONV - 1, width), jnp.float32), grid], axis=1)
    pad_seg = jnp.concatenate([jnp.full((seq_count, CONV - 1), -1, jnp.int32), segs_grid], axis=1)
    total = jnp.zeros((seq_count, seq_len, width), jnp.float32) + conv_b
    for tap in range(CONV):
        same = (pad_seg[:, tap : tap + seq_len] == segs_grid).astype(jnp.float32)
        total = total + conv_w[tap] * pad_x[:, tap : tap + seq_len] * same[:, :, None]
    return jax.nn.silu(total).reshape(seq_count * seq_len, width)


CHUNK = 64
ROWS = 256
RANGE = 120.0
LANES = 256


def spans(width, size):
    return [(at, min(at + size, width)) for at in range(0, width, size)]


def softplus_parts(pre):
    small = jnp.exp(-jnp.abs(pre))
    step = jnp.maximum(pre, 0.0) + jnp.log1p(small)
    slope = jnp.where(pre >= 0.0, 1.0, small) / (1.0 + small)
    return step, slope


def split_sum(tri, values):
    high = values.astype(jnp.bfloat16)
    low = (values - high.astype(jnp.float32)).astype(jnp.bfloat16)
    return dot_plain(tri, high) + dot_plain(tri, low)


def tri_matrix(size, upper):
    row = lax.broadcasted_iota(jnp.int32, (size, size), 0)
    col = lax.broadcasted_iota(jnp.int32, (size, size), 1)
    order = (col >= row) if upper else (row >= col)
    return order & (lax.div(row, CHUNK) == lax.div(col, CHUNK))


def scan_setup(dbl_ref, dtw_ref, vec_ref, step_scr, cum_scr, slope_scr):
    width = dtw_ref.shape[1]
    tri = tri_matrix(ROWS, False).astype(jnp.bfloat16)
    dt_low = dbl_ref[:, :RANK]
    lowest = jnp.zeros((), jnp.float32)
    for lo, hi in spans(width, LANES):
        pre = dot_plain(dt_low, dtw_ref[:, lo:hi]) + vec_ref[0:1, lo:hi]
        step, slope = softplus_parts(pre)
        cum = split_sum(tri, -step * jnp.exp(vec_ref[1:2, lo:hi]))
        step_scr[:, lo:hi] = step
        cum_scr[:, lo:hi] = cum
        if slope_scr is not None:
            slope_scr[:, lo:hi] = slope
        least = jnp.zeros((1, hi - lo), jnp.float32)
        for at in range(0, ROWS, CHUNK):
            least = jnp.minimum(least, cum[at + CHUNK - 1 : at + CHUNK])
        lowest = jnp.minimum(lowest, jnp.min(least))
    return lowest


def chunk_maps(dbl_ref, mask_ref, segr_ref, at):
    rows = slice(at, at + CHUNK)
    b_map = dbl_ref[rows, 128 : 128 + STATE]
    c_map = dbl_ref[rows, 128 + STATE : 128 + 2 * STATE]
    linked = mask_ref[rows, 0:1]
    tail = mask_ref[rows, 1:2]
    keep = mask_ref[at + CHUNK - 1 : at + CHUNK, 2:3]
    allowed = tri_matrix(CHUNK, False) & (mask_ref[rows, 4:5] == segr_ref[0:1, rows])
    gram = jnp.where(allowed, dot_last(c_map, b_map), 0.0)
    c_link = c_map.astype(jnp.float32) * linked
    b_tail = b_map.astype(jnp.float32) * tail
    return b_map, c_map, linked, tail, keep, allowed, gram, c_link, b_tail


def mixer(square, side, bottom):
    corner = jnp.zeros((STATE, STATE), jnp.float32)
    top = jnp.concatenate([square, side], axis=1)
    low = jnp.concatenate([jnp.transpose(bottom), corner], axis=1)
    return jnp.concatenate([top, low], axis=0).astype(jnp.bfloat16)


def token_column(block, lane_index):
    lanes = lax.broadcasted_iota(jnp.int32, block.shape, 1)
    return jnp.sum(jnp.where(lanes == lane_index, block, 0.0), axis=1, keepdims=True)


def scan_fwd_kernel(
    xa_ref, z_ref, dbl_ref, mask_ref, segr_ref, dtw_ref, vec_ref,
    out_ref, hsave_ref, h_scr, step_scr, cum_scr, y_scr,
):
    width = xa_ref.shape[1]

    @pl.when(pl.program_id(0) == 0)
    def _():
        h_scr[...] = jnp.zeros_like(h_scr)

    lowest = scan_setup(dbl_ref, dtw_ref, vec_ref, step_scr, cum_scr, None)

    @pl.when(lowest >= -RANGE)
    def _():
        for index, at in enumerate(range(0, ROWS, CHUNK)):
            rows = slice(at, at + CHUNK)
            _, _, _, _, keep, _, gram, c_link, b_tail = chunk_maps(dbl_ref, mask_ref, segr_ref, at)
            forward = mixer(gram, c_link, b_tail)
            for lo, hi in spans(width, LANES):
                cum = cum_scr[rows, lo:hi]
                half = 0.5 * cum[CHUNK - 1 : CHUNK]
                gap = cum - half
                rise = jnp.exp(half)
                h_old = h_scr[:, lo:hi]
                hsave_ref[index, :, lo:hi] = h_old
                x_f = xa_ref[rows, lo:hi].astype(jnp.float32)
                sources = jnp.concatenate(
                    [jnp.exp(-gap) * (step_scr[rows, lo:hi] * x_f), rise * h_old], axis=0
                ).astype(jnp.bfloat16)
                mixed = dot_plain(forward, sources)
                total = jnp.exp(gap) * mixed[:CHUNK] + vec_ref[2:3, lo:hi] * x_f
                out_ref[rows, lo:hi] = (total * jax.nn.silu(z_ref[rows, lo:hi])).astype(
                    jnp.bfloat16
                )
                h_scr[:, lo:hi] = rise * mixed[CHUNK:] + (rise * rise * keep) * h_old

    @pl.when(lowest < -RANGE)
    def _():
        for index, at in enumerate(range(0, ROWS, CHUNK)):
            rows = slice(at, at + CHUNK)
            hsave_ref[index] = h_scr[...]
            b_cols = jnp.transpose(dbl_ref[rows, 128 : 128 + STATE].astype(jnp.float32))
            c_cols = jnp.transpose(dbl_ref[rows, 128 + STATE : 128 + 2 * STATE].astype(jnp.float32))
            y_scr[...] = xa_ref[rows].astype(jnp.float32)
            rate = jnp.exp(vec_ref[1:2])

            def token(t, carry):
                step = step_scr[pl.ds(at + t, 1)]
                keep = mask_ref[pl.ds(at + t, 1)][:, 3:4]
                state = (jnp.exp(-step * rate) * keep) * h_scr[...] + token_column(b_cols, t) * (
                    step * y_scr[pl.ds(t, 1)]
                )
                h_scr[...] = state
                y_scr[pl.ds(t, 1)] = (
                    jnp.sum(state * token_column(c_cols, t), axis=0, keepdims=True)
                    + vec_ref[2:3] * y_scr[pl.ds(t, 1)]
                )
                return carry

            lax.fori_loop(0, CHUNK, token, 0)
            out_ref[rows] = (y_scr[...] * jax.nn.silu(z_ref[rows])).astype(jnp.bfloat16)


def scan_bwd_kernel(
    xa_ref, z_ref, dbl_ref, mask_ref, segr_ref, dtw_ref, vec_ref, hsave_ref, gs_ref,
    gz_ref, gx_ref, gdbl_ref, gdtw_ref, gvec_ref,
    g_scr, step_scr, cum_scr, slope_scr, gl_scr, gu_scr, gpre_scr, hall_scr, y_scr,
):
    width = xa_ref.shape[1]

    @pl.when(pl.program_id(0) == 0)
    def _():
        g_scr[...] = jnp.zeros_like(g_scr)
        gdtw_ref[...] = jnp.zeros_like(gdtw_ref)
        gvec_ref[...] = jnp.zeros_like(gvec_ref)

    lowest = scan_setup(dbl_ref, dtw_ref, vec_ref, step_scr, cum_scr, slope_scr)
    count = ROWS // CHUNK

    @pl.when(lowest >= -RANGE)
    def _():
        for index in range(count - 1, -1, -1):
            at = index * CHUNK
            rows = slice(at, at + CHUNK)
            b_map, c_map, linked, tail, keep, allowed, gram, c_link, b_tail = chunk_maps(
                dbl_ref, mask_ref, segr_ref, at
            )
            forward = mixer(gram, c_link, b_tail)
            reverse = mixer(jnp.transpose(gram), b_tail, c_link)
            cross = jnp.zeros((CHUNK + STATE, CHUNK + STATE), jnp.float32)
            for lo, hi in spans(width, LANES):
                cum = cum_scr[rows, lo:hi]
                half = 0.5 * cum[CHUNK - 1 : CHUNK]
                gap = cum - half
                fall = jnp.exp(gap)
                grow = jnp.exp(-gap)
                rise = jnp.exp(half)
                h_old = hsave_ref[index, :, lo:hi]
                g_new = g_scr[:, lo:hi]
                step = step_scr[rows, lo:hi]
                x_f = xa_ref[rows, lo:hi].astype(jnp.float32)
                skip = vec_ref[2:3, lo:hi]
                sources = jnp.concatenate([grow * (step * x_f), rise * h_old], axis=0).astype(
                    jnp.bfloat16
                )
                mixed = dot_plain(forward, sources)
                inner = mixed[:CHUNK]
                z_f = z_ref[rows, lo:hi]
                grad = gs_ref[rows, lo:hi]
                sig = jax.nn.sigmoid(z_f)
                gated = z_f * sig
                gy = grad * gated
                gz_ref[rows, lo:hi] = (
                    grad * (fall * inner + skip * x_f) * (sig + gated * (1.0 - sig))
                ).astype(jnp.bfloat16)
                sinks = jnp.concatenate([fall * gy, rise * g_new], axis=0).astype(jnp.bfloat16)
                pulled = dot_plain(reverse, sinks)
                back = pulled[:CHUNK]
                cross += dot_last(sinks, sources)
                sinks_f = sinks.astype(jnp.float32)
                sources_f = sources.astype(jnp.float32)
                ends = jnp.sum(sinks_f[CHUNK:] * mixed[CHUNK:], axis=0, keepdims=True) + (
                    rise * rise * keep
                ) * jnp.sum(g_new * h_old, axis=0, keepdims=True)
                diff = sinks_f[:CHUNK] * inner - sources_f[:CHUNK] * back
                gl_scr[rows, lo:hi] = diff
                gl_scr[at + CHUNK - 1 : at + CHUNK, lo:hi] = diff[CHUNK - 1 : CHUNK] + ends
                g_scr[:, lo:hi] = rise * pulled[CHUNK:] + (rise * rise * keep) * g_new
                gu = grow * back
                gu_scr[rows, lo:hi] = gu
                gx_ref[rows, lo:hi] = step * gu + skip * gy
                gvec_ref[2:3, lo:hi] += jnp.sum(gy * x_f, axis=0, keepdims=True)
            g_gram = jnp.where(allowed, cross[:CHUNK, :CHUNK], 0.0).astype(jnp.bfloat16)
            gdbl_ref[rows, 128 : 128 + STATE] = dot_first(g_gram, c_map) + tail * jnp.transpose(
                cross[CHUNK:, :CHUNK]
            )
            gdbl_ref[rows, 128 + STATE : 128 + 2 * STATE] = (
                dot_plain(g_gram, b_map) + linked * cross[:CHUNK, CHUNK:]
            )
        triu = tri_matrix(ROWS, True).astype(jnp.bfloat16)
        for lo, hi in spans(width, LANES):
            gl_scr[:, lo:hi] = split_sum(triu, gl_scr[:, lo:hi])

    @pl.when(lowest < -RANGE)
    def _():
        rate = jnp.exp(vec_ref[1:2])

        def chunk_step(reverse, carry):
            index = count - 1 - reverse
            at = pl.multiple_of(index * CHUNK, CHUNK)
            rows = pl.ds(at, CHUNK)
            b_cols = jnp.transpose(dbl_ref[rows, 128 : 128 + STATE].astype(jnp.float32))
            c_cols = jnp.transpose(dbl_ref[rows, 128 + STATE : 128 + 2 * STATE].astype(jnp.float32))
            hall_scr[0] = hsave_ref[index]
            y_scr[...] = xa_ref[rows].astype(jnp.float32)
            gu_scr[rows] = gs_ref[rows] * jax.nn.silu(z_ref[rows])

            def forward(t, inner_carry):
                step = step_scr[pl.ds(at + t, 1)]
                keep = mask_ref[pl.ds(at + t, 1)][:, 3:4]
                state = (jnp.exp(-step * rate) * keep) * hall_scr[t] + token_column(b_cols, t) * (
                    step * y_scr[pl.ds(t, 1)]
                )
                hall_scr[t + 1] = state
                return inner_carry

            lax.fori_loop(0, CHUNK, forward, 0)

            def backward(back, inner_carry):
                g_b, g_c = inner_carry
                t = CHUNK - 1 - back
                step = step_scr[pl.ds(at + t, 1)]
                keep = mask_ref[pl.ds(at + t, 1)][:, 3:4]
                decay = jnp.exp(-step * rate) * keep
                gy = gu_scr[pl.ds(at + t, 1)]
                x_f = y_scr[pl.ds(t, 1)]
                c_col = token_column(c_cols, t)
                b_col = token_column(b_cols, t)
                here = hall_scr[t + 1]
                grad = g_scr[...] + c_col * gy
                lanes = lax.broadcasted_iota(jnp.int32, (STATE, CHUNK), 1)
                g_b = jnp.where(
                    lanes == t, jnp.sum(grad * (step * x_f), axis=1, keepdims=True), g_b
                )
                g_c = jnp.where(lanes == t, jnp.sum(here * gy, axis=1, keepdims=True), g_c)
                gl_scr[pl.ds(at + t, 1)] = decay * jnp.sum(
                    grad * hall_scr[t], axis=0, keepdims=True
                )
                gu_scr[pl.ds(at + t, 1)] = jnp.sum(grad * b_col, axis=0, keepdims=True)
                y_scr[pl.ds(t, 1)] = (
                    jnp.sum(here * c_col, axis=0, keepdims=True) + vec_ref[2:3] * x_f
                )
                g_scr[...] = decay * grad
                return g_b, g_c

            blank = jnp.zeros((STATE, CHUNK), jnp.float32)
            g_b, g_c = lax.fori_loop(0, CHUNK, backward, (blank, blank))
            gdbl_ref[rows, 128 : 128 + STATE] = jnp.transpose(g_b)
            gdbl_ref[rows, 128 + STATE : 128 + 2 * STATE] = jnp.transpose(g_c)
            z_f = z_ref[rows]
            grad = gs_ref[rows]
            sig = jax.nn.sigmoid(z_f)
            gz_ref[rows] = (grad * y_scr[...] * (sig * (1.0 + z_f * (1.0 - sig)))).astype(
                jnp.bfloat16
            )
            gy = grad * (z_f * sig)
            x_f = xa_ref[rows].astype(jnp.float32)
            gx_ref[rows] = step_scr[rows] * gu_scr[rows] + vec_ref[2:3] * gy
            gvec_ref[2:3] += jnp.sum(gy * x_f, axis=0, keepdims=True)
            return carry

        lax.fori_loop(0, count, chunk_step, 0)

    for lo, hi in spans(width, LANES):
        rate = jnp.exp(vec_ref[1:2, lo:hi])
        x_f = xa_ref[:, lo:hi].astype(jnp.float32)
        gl = rate * gl_scr[:, lo:hi]
        gpre = (x_f * gu_scr[:, lo:hi] - gl) * slope_scr[:, lo:hi]
        gvec_ref[0:1, lo:hi] += jnp.sum(gpre, axis=0, keepdims=True)
        gvec_ref[1:2, lo:hi] -= jnp.sum(step_scr[:, lo:hi] * gl, axis=0, keepdims=True)
        gpre_scr[:, lo:hi] = gpre.astype(jnp.bfloat16)
    gdtw_ref[...] += dot_first(dbl_ref[:, :RANK], gpre_scr[...])
    gdbl_ref[:, :RANK] = dot_last(gpre_scr[...], dtw_ref[...])


def scan_specs(width, backward, blocks):
    def at(i):
        return (blocks - 1 - i) if backward else i

    rows = lambda cols: pl.BlockSpec((ROWS, cols), lambda i: (at(i), 0))
    whole = lambda *shape: pl.BlockSpec(shape, lambda i: (0, 0))
    return [
        rows(width),
        rows(width),
        rows(256),
        rows(8),
        pl.BlockSpec((1, ROWS), lambda i: (0, at(i))),
        whole(RANK, width),
        whole(8, width),
    ], pl.BlockSpec((ROWS // CHUNK, STATE, width), lambda i: (at(i), 0, 0)), rows, whole


def scan_forward(x_act, z_gate, dbl, masks, seg_row, dt_weight, vectors):
    tokens, width = x_act.shape
    blocks = tokens // ROWS
    in_specs, state_spec, rows, whole = scan_specs(width, False, blocks)
    return pl.pallas_call(
        scan_fwd_kernel,
        name="scan_fwd",
        grid=(blocks,),
        in_specs=in_specs,
        out_specs=[rows(width), state_spec],
        out_shape=[
            jax.ShapeDtypeStruct((tokens, width), jnp.bfloat16),
            jax.ShapeDtypeStruct((tokens // CHUNK, STATE, width), jnp.float32),
        ],
        scratch_shapes=[
            pltpu.VMEM((STATE, width), jnp.float32),
            pltpu.VMEM((ROWS, width), jnp.float32),
            pltpu.VMEM((ROWS, width), jnp.float32),
            pltpu.VMEM((CHUNK, width), jnp.float32),
        ],
        compiler_params=pltpu.CompilerParams(vmem_limit_bytes=40 << 20),
        cost_estimate=pl.CostEstimate(
            flops=0, bytes_accessed=93 << 20, transcendentals=0
        ),
    )(x_act, z_gate, dbl, masks, seg_row, dt_weight, vectors)


def scan_backward(x_act, z_gate, dbl, masks, seg_row, dt_weight, vectors, states, grad_rows):
    tokens, width = x_act.shape
    blocks = tokens // ROWS
    in_specs, state_spec, rows, whole = scan_specs(width, True, blocks)
    return pl.pallas_call(
        scan_bwd_kernel,
        name="scan_bwd",
        grid=(blocks,),
        in_specs=in_specs + [state_spec, rows(width)],
        out_specs=[rows(width), rows(width), rows(256), whole(RANK, width), whole(8, width)],
        out_shape=[
            jax.ShapeDtypeStruct((tokens, width), jnp.bfloat16),
            jax.ShapeDtypeStruct((tokens, width), jnp.float32),
            jax.ShapeDtypeStruct((tokens, 256), jnp.float32),
            jax.ShapeDtypeStruct((RANK, width), jnp.float32),
            jax.ShapeDtypeStruct((8, width), jnp.float32),
        ],
        scratch_shapes=[
            pltpu.VMEM((STATE, width), jnp.float32),
            pltpu.VMEM((ROWS, width), jnp.float32),
            pltpu.VMEM((ROWS, width), jnp.float32),
            pltpu.VMEM((ROWS, width), jnp.float32),
            pltpu.VMEM((ROWS, width), jnp.float32),
            pltpu.VMEM((ROWS, width), jnp.float32),
            pltpu.VMEM((ROWS, width), jnp.bfloat16),
            pltpu.VMEM((CHUNK + 1, STATE, width), jnp.float32),
            pltpu.VMEM((CHUNK, width), jnp.float32),
        ],
        compiler_params=pltpu.CompilerParams(vmem_limit_bytes=48 << 20),
        cost_estimate=pl.CostEstimate(
            flops=0, bytes_accessed=244 << 20, transcendentals=0
        ),
    )(x_act, z_gate, dbl, masks, seg_row, dt_weight, vectors, states, grad_rows)


def scan_masks(segs_flat):
    tokens = segs_flat.shape[0]
    before = jnp.concatenate([jnp.full((1,), -1, jnp.int32), segs_flat[:-1]])
    chunked = segs_flat.reshape(tokens // CHUNK, CHUNK)
    prior = before.reshape(tokens // CHUNK, CHUNK)[:, :1]
    last = chunked[:, CHUNK - 1 :]
    linked = chunked == prior
    tail = chunked == last
    keep = jnp.broadcast_to(last == prior, chunked.shape)
    same = (segs_flat == before).reshape(chunked.shape)
    blank = jnp.zeros_like(linked)
    stacked = jnp.stack([linked, tail, keep, same], axis=-1).reshape(tokens, 4).astype(jnp.float32)
    number = segs_flat.astype(jnp.float32)
    masks = jnp.concatenate(
        [stacked, number[:, None], jnp.zeros((tokens, 3), jnp.float32)], axis=1
    )
    return masks, number[None, :]


def per_device(
    inputs,
    teacher,
    segment_ids,
    valid,
    norm_in_gain,
    w_query,
    w_key,
    w_value,
    w_attn_out,
    w_mamba_in,
    conv_weight,
    conv_bias,
    x_proj,
    dt_proj,
    dt_bias,
    a_log,
    d_skip,
    w_mamba_out,
    attn_norm_gain,
    ssm_norm_gain,
    norm_mid_gain,
    w_gate,
    w_up,
    w_down,
):
    rank_index = lax.axis_index("tensor")
    first_slot, second_slot = rank_index, KV - 1
    per_slot = HEADS // KV
    group_width = per_slot * HEAD
    query_width = 2 * group_width
    qkv_width = query_width + 4 * HEAD
    width = inputs.shape[1]
    inner_width = w_mamba_out.shape[0]
    low = lambda values: values.astype(jnp.bfloat16)
    gather_dp = lambda part: lax.all_gather(part, "dp", axis=0, tiled=True)
    scatter_dp = lambda part: lax.psum_scatter(part, "dp", scatter_dimension=0, tiled=True)
    gather_t = lambda part: gather_rows(part, 1)
    tie = lax.optimization_barrier

    own_width = w_query.shape[0]
    out_local = pick_groups(w_attn_out, first_slot, second_slot, group_width, 0).T
    mamba_local = jnp.concatenate(
        [out_local, w_mamba_in.reshape(own_width, 2 * inner_width), w_mamba_out.T], axis=1
    )
    x_at, z_at = query_width, query_width + inner_width
    back_at = z_at + inner_width
    mamba_local = jnp.pad(mamba_local, ((0, 0), (0, -mamba_local.shape[1] % 128)))
    mamba_all = gather_dp(mamba_local)
    part_of = lambda at: (mamba_all, None, at // 128 * 128, -(-(at % 128 + inner_width) // 128) * 128)
    w_query, w_key, w_value, norm_in_gain, _ = tie(
        (w_query, w_key, w_value, norm_in_gain, mamba_local)
    )
    group_rows = 4 * inputs.shape[0]
    seq_count = group_rows // LEN
    segs_grid = segment_ids.reshape(seq_count, LEN)
    segs_flat = (segs_grid + 128 * jnp.arange(seq_count, dtype=jnp.int32)[:, None]).reshape(-1)
    scan_mask, seg_row = scan_masks(segs_flat)
    starts = first_blocks(segs_flat)
    blocks = jnp.arange(group_rows // BQ, dtype=jnp.int32)
    shared_here = blocks // (group_rows // BQ // 4) == rank_index
    firsts = jnp.concatenate([starts, jnp.where(shared_here, starts, blocks + 1)])
    first_local = jnp.concatenate(
        [
            pick_groups(w_query, first_slot, second_slot, group_width, 1),
            pick_groups(w_key, first_slot, second_slot, HEAD, 1),
            pick_groups(w_value, first_slot, second_slot, HEAD, 1),
        ],
        axis=1,
    )
    gain_rows = jnp.stack([norm_in_gain, attn_norm_gain, ssm_norm_gain, norm_mid_gain])
    gains, valid_total = hello(gain_rows, jnp.sum(valid).astype(jnp.float32))
    gain_in, gain_attn, gain_ssm, gain_mid = [gains[index][:, None] for index in range(4)]
    inputs_t = inputs.T
    normed_in, pull_in = jax.vjp(normalize_t, inputs_t, gain_in)
    normed_low, first_local, w_gate, w_up, w_down = tie(
        (low(normed_in), first_local, w_gate, w_up, w_down)
    )
    whole_in, qkv_w = gather_first(normed_low, first_local)
    whole_in, w_gate, w_up, w_down = tie((whole_in, w_gate, w_up, w_down))
    qkv_cols = low(dot_first(qkv_w, whole_in))
    attended_t, log_totals = attn_forward(firsts, qkv_cols, seg_row, scan_mask, 2)
    attended_t, x_proj, dt_proj, conv_weight = tie((attended_t, x_proj, dt_proj, conv_weight))
    inner_local = jnp.concatenate(
        [
            dt_bias[:, None],
            a_log[:, None],
            d_skip[:, None],
            conv_bias[:, None],
            conv_weight.T,
            x_proj,
            dt_proj.T,
        ],
        axis=1,
    )
    inner_rows = inner_spread(inner_local)
    attended_t, inner_rows = tie((attended_t, inner_rows))
    attn_sum = product_reduce(
        [(mamba_all, None, 0, query_width)],
        [(attended_t, True)],
        [(0, 0, query_width, 0)],
        10,
        "attn_reduce",
        43,
    )
    out_w = mamba_all[:, :query_width]
    weight_x = mamba_all[:, x_at:z_at]
    weight_z = mamba_all[:, z_at:back_at]
    mamba_out_w = mamba_all[:, back_at : back_at + inner_width]
    x_in = dot_first(whole_in, weight_x)
    ff_width = w_gate.shape[1]
    ff_step = -(-ff_width // 128) * 128
    blank = jnp.zeros((own_width, ff_step - ff_width), jnp.bfloat16)
    ffn_all = gather_dp(jnp.concatenate([w_gate, blank, w_up, blank, w_down.T, blank], axis=1))
    vector_rows = inner_rows[:, :8].astype(jnp.float32).T
    xproj_rows = inner_rows[:, 8 : 8 + RANK + 2 * STATE]
    dt_weight = inner_rows[:, 8 + RANK + 2 * STATE :].T
    xproj_pad = jnp.concatenate(
        [
            xproj_rows[:, :RANK],
            jnp.zeros((inner_width, 128 - RANK), jnp.bfloat16),
            xproj_rows[:, RANK:],
            jnp.zeros((inner_width, 128 - 2 * STATE), jnp.bfloat16),
        ],
        axis=1,
    )
    x_pre, pull_conv = jax.vjp(
        lambda x_part, taps, shift: conv_rows(x_part, taps, shift, segs_grid),
        x_in,
        vector_rows[4:],
        vector_rows[3],
    )
    x_act = low(x_pre)
    dbl_pad = total_rows(dot_plain(x_act, xproj_pad), 3)
    z_gate = dot_first(whole_in, weight_z)
    ssm_rows, states = scan_forward(
        x_act, z_gate, dbl_pad, scan_mask, seg_row, dt_weight, vector_rows
    )
    ssm_sum = product_reduce(
        [part_of(back_at)],
        [(ssm_rows, False)],
        [(0, back_at % 128, back_at % 128 + inner_width, 0)],
        11,
        "ssm_reduce",
        43,
    )
    mixed, pull_join = jax.vjp(join_rows_t, inputs_t, attn_sum, ssm_sum, gain_attn, gain_ssm)
    normed_mid, pull_mid = jax.vjp(normalize_t, mixed, gain_mid)
    normed_low, ffn_all = tie((low(normed_mid), ffn_all))
    whole_mid, gate_rows, up_rows, hidden = turn_rows(
        normed_low,
        ffn_all,
        [],
        [(ff_width, jnp.float32), (ff_width, jnp.float32), (ff_width, jnp.bfloat16)],
        [(0, ff_width), (ff_step, ff_step + ff_width)],
        forward_gate,
        15,
        "gate_turn",
        52,
    )
    ffn_rows = product_reduce(
        [(ffn_all, None, 2 * ff_step, ff_step)], [(hidden, False)], [(0, 0, ff_width, 0)], 6, "down_reduce", 45
    )
    result = mixed + ffn_rows
    all_rows = inputs.shape[0] * lax.axis_size("dp") * lax.axis_size("tensor")
    grad_out = all_rows / valid_total * valid.astype(jnp.float32)[None, :] * (result - teacher.T)
    grad_ffn, grad_gate, grad_up = turn_rows(
        low(grad_out),
        ffn_all,
        [gate_rows, up_rows],
        [(ff_width, jnp.bfloat16), (ff_width, jnp.bfloat16)],
        [(2 * ff_step, 2 * ff_step + ff_width)],
        backward_gate,
        16,
        "grad_turn",
        52,
    )
    ffn_grads = weight_grads(
        [
            (whole_mid, grad_gate, False),
            (whole_mid, grad_up, False),
            (grad_ffn, hidden, False),
        ],
        "ffn_weight_grads",
        44,
    )
    grad_gate, grad_up, ffn_grads = tie((grad_gate, grad_up, ffn_grads))
    ffn_shard = scatter_dp(ffn_grads)
    grad_mid_rows = product_reduce(
        [(ffn_all, None, 0, 2 * ff_step)],
        [(grad_gate, False), (grad_up, False)],
        [(0, 0, ff_width, 0), (0, ff_step, ff_step + ff_width, 1)],
        7,
        "mid_reduce",
        50,
    )
    grad_mixed_norm, grad_gain_mid = pull_mid(grad_mid_rows)
    grad_mixed = grad_out + grad_mixed_norm
    grad_resid, grad_attn_sum, grad_ssm_sum, grad_gain_attn, grad_gain_ssm = pull_join(grad_mixed)
    grad_ssm_whole = gather_t(low(grad_ssm_sum))
    grad_attn_low, grad_ssm_whole = tie((low(grad_attn_sum), grad_ssm_whole))
    grad_attn_whole = gather_t(grad_attn_low)
    grad_ssm_whole, grad_attn_whole = tie((grad_ssm_whole, grad_attn_whole))
    grad_ssm_rows = dot_first(grad_ssm_whole, mamba_out_w)
    grad_gate_part, grad_act_scan, grad_dbl_part, grad_dtproj, grad_vectors = scan_backward(
        x_act, z_gate, dbl_pad, scan_mask, seg_row, dt_weight, vector_rows, states, grad_ssm_rows
    )
    mid_grads = weight_grads(
        [
            (grad_attn_whole, attended_t, True),
            (grad_ssm_whole, ssm_rows, False),
            (whole_in, grad_gate_part, False),
        ],
        "mid_weight_grads",
        26,
        tight=True,
    )
    grad_att_t = low(
        lax.dot_general(
            out_w, grad_attn_whole, (((0,), (0,)), ((), ())), preferred_element_type=jnp.float32
        )
    )
    grad_dbl_part, mid_grads, ffn_shard = tie((grad_dbl_part, mid_grads, ffn_shard))
    mid_shard = scatter_dp(mid_grads)
    grad_qkv = attn_backward(
        firsts, qkv_cols, grad_att_t, attended_t, log_totals, seg_row, scan_mask, 2
    )
    grad_dbl = total_rows(grad_dbl_part, 3)
    grad_act = grad_act_scan + dot_last(grad_dbl, xproj_pad)
    grad_xproj_w = dot_first(x_act, grad_dbl)
    grad_x_part, grad_taps, grad_shift = pull_conv(grad_act)
    grad_x_low = low(grad_x_part)
    inner_grads = jnp.concatenate(
        [
            grad_vectors[:3].T,
            grad_shift[:, None],
            grad_taps.T,
            grad_xproj_w[:, :RANK],
            grad_xproj_w[:, 128 : 128 + 2 * STATE],
            grad_dtproj.T,
        ],
        axis=1,
    )
    last_grads = weight_grads(
        [
            (whole_in, grad_x_low, False),
            (whole_in, grad_qkv, True),
            (low(inner_grads).reshape(width, -1), None, False),
        ],
        "last_weight_grads",
        20,
    )
    grad_x_low, grad_qkv, last_grads, mid_shard = tie(
        (grad_x_low, grad_qkv, last_grads, mid_shard)
    )
    last_shard = scatter_dp(last_grads)
    grad_in_rows = product_reduce(
        [
            (qkv_w, None, None, qkv_width),
            part_of(x_at),
            part_of(z_at),
        ],
        [(grad_qkv, True), (grad_x_low, False), (grad_gate_part, False)],
        [
            (0, 0, qkv_width, 0),
            (1, x_at % 128, x_at % 128 + inner_width, 1),
            (2, z_at % 128, z_at % 128 + inner_width, 2),
        ],
        8,
        "in_reduce",
        52,
    )
    grad_in_norm, grad_gain_in = pull_in(grad_in_rows)
    grad_inputs = grad_resid + grad_in_norm
    gain_grads = jnp.concatenate(
        [grad_gain_in, grad_gain_attn, grad_gain_ssm, grad_gain_mid], axis=1
    )
    gains_own = farewell(gain_grads.T)
    wide = lambda part: jnp.pad(part, ((0, 0), (0, -part.shape[1] % 256)))
    out_stack = gather_stack(wide(mid_shard[:, :query_width]), 5)
    gains_own, last_shard, grad_inputs, out_stack = tie(
        (gains_own, last_shard, grad_inputs, out_stack)
    )
    inner_step = -(-inner_width // 128) * 128
    inner_at = inner_step + qkv_width
    shared_all, owned = gather_final(wide(last_shard[:, inner_step:inner_at]), last_shard[:, inner_at:])
    inner_cols = inner_grads.size // width
    inner_sum = owned[:, :, :inner_cols].astype(jnp.float32).reshape(-1, inner_grads.shape[1])
    mamba_at = query_width
    gate_at = query_width + inner_width
    def merge(stack, start, size):
        own = [stack[rank, :, start : start + size].astype(jnp.float32) for rank in range(4)]
        both = jnp.sum(
            stack[:, :, start + size : start + 2 * size].astype(jnp.float32), axis=0
        )
        return jnp.concatenate(own + [both], axis=1)

    return (
        result.T,
        grad_inputs.T,
        gains_own[0],
        merge(shared_all, 0, group_width),
        merge(shared_all, query_width, HEAD),
        merge(shared_all, query_width + 2 * HEAD, HEAD),
        merge(out_stack, 0, group_width).T,
        jnp.stack(
            [last_shard[:, :inner_width], mid_shard[:, gate_at : gate_at + inner_width]], axis=1
        ).astype(jnp.float32),
        inner_sum[:, 4:8].T,
        inner_sum[:, 3],
        inner_sum[:, 8 : 8 + RANK + 2 * STATE],
        inner_sum[:, 8 + RANK + 2 * STATE :].T,
        inner_sum[:, 0],
        inner_sum[:, 1],
        inner_sum[:, 2],
        mid_shard[:, mamba_at : mamba_at + inner_width].T.astype(jnp.float32),
        gains_own[1],
        gains_own[2],
        gains_own[3],
        ffn_shard[:, :ff_width].astype(jnp.float32),
        ffn_shard[:, ff_step : ff_step + ff_width].astype(jnp.float32),
        ffn_shard[:, 2 * ff_step : 2 * ff_step + ff_width].astype(jnp.float32).T,
    )


def solution(mesh):
    placed = (
        P(("dp", "tensor"), None),
        P(("dp", "tensor"), None),
        P("dp"),
        P(("dp", "tensor")),
        P("dp"),
        P("dp", None),
        P("dp", None),
        P("dp", None),
        P(None, "dp"),
        P("dp", None, "tensor"),
        P(None, "dp"),
        P("dp"),
        P("dp", None),
        P(None, "dp"),
        P("dp"),
        P("dp"),
        P("dp"),
        P("tensor", "dp"),
        P("dp"),
        P("dp"),
        P("dp"),
        P("dp", "tensor"),
        P("dp", "tensor"),
        P("tensor", "dp"),
    )
    return jax.shard_map(
        per_device,
        mesh=mesh,
        in_specs=placed,
        out_specs=(
            P(("dp", "tensor"), None),
            P(("dp", "tensor"), None),
            P("dp"),
            P("dp", None),
            P("dp", None),
            P("dp", None),
            P(None, "dp"),
            P("dp", None, "tensor"),
            P(None, "dp"),
            P("dp"),
            P("dp", None),
            P(None, "dp"),
            P("dp"),
            P("dp"),
            P("dp"),
            P("tensor", "dp"),
            P("dp"),
            P("dp"),
            P("dp"),
            P("dp", "tensor"),
            P("dp", "tensor"),
            P("tensor", "dp"),
        ),
        check_vma=False,
    )
```

profile of v0, /device:TPU:17, one launch (start us, length us, event | category | flops | bytes accessed | tf_op | source)
XLA Modules:
  0.0 1085.4 jit_solution(4829158966121487502)
XLA Ops:
  7.2 2.1 reshape.293
  10.7 2.5 concatenate.54
  17.0 11.2 %hello.1 = (f32[8,8,256]{2,1,0:T(8,128)}, f32[8,8,128]{2,1,0:T(8,128)}) custom-call(f32[8,256]{1,0:T(8,128)} %fusion.32.gain_ref, f32[8,128]{1,0:T(8,128)} %broadcast_in_dim.73.count_ref), custom_call_target="tpu_custom_call" | custom-call | bytes 31457280 | tf_op jit(solution)/shard_map/hello/pallas_call | solution.py:530
  30.7 2.4 fusion.10
  34.1 58.4 %gather_first.1 = (bf16[1600,2048]{1,0:T(8,128)(2,1)S(1)}, bf16[8,200,896]{2,1,0:T(8,128)(2,1)S(1)}) custom-call(bf16[1600,512]{1,0:T(8,128)(2,1)S(1)} %multiply_convert_fusion.2.part_ref, bf16[200,896]{1,0:T(8,128)(2,1)S(1)} %concatenate.56.shard_ref), custom_call_target="tpu_custom_call" | custom-call | bytes 283115520 | tf_op jit(solution)/shard_map/gather_first/pallas_call | solution.py:251
  92.5 2.8 copy-done.4
  95.3 1.6 copy-done.22
  96.9 2.5 concatenate.63
  102.3 10.0 convolution_convert_fusion.qt_ref.kt_ref.vt_ref
  112.4 35.2 %attn_fwd.1 = (bf16[640,2048]{1,0:T(8,128)(2,1)S(1)}, f32[2,8,2048]{2,1,0:T(8,128)S(1)}) custom-call(s32[16]{0:T(128)S(1)} %pad_add_fusion.4.first_ref, bf16[896,2048]{1,0:T(8,128)(2,1)S(1)} %convolution_convert_fusion.qt_ref.kt_ref.vt_ref, bf16[896,2048]{1,0:T(8,128)(2,1)S(1)} %convolution_convert_fusion.qt_ref.kt_ref.vt_ref, ...), custom_call_target="tpu_custom_call" | custom-call | bytes 157286400 | tf_op jit(solution)/shard_map/attn_fwd/pallas_call | solution.py:1116
  147.6 1.5 copy-done.14
  150.5 43.5 %inner_spread.1 = bf16[2,400,256]{2,1,0:T(8,128)(2,1)S(1)} custom-call(bf16[400,256]{1,0:T(8,128)(2,1)S(1)} %pad.49.part_ref), custom_call_target="tpu_custom_call" | custom-call | bytes 41943040 | tf_op jit(solution)/shard_map/inner_spread/pallas_call | solution.py:922
  194.9 1.4 slice_reduce_fusion.10
  197.9 10.8 fusion.16
  208.8 8.2 fusion.4
  217.0 1.3 fusion.20.part_ref
  218.3 20.8 %total_rows.2.dbl_ref = bf16[2048,256]{1,0:T(8,128)(2,1)S(1)} custom-call(f32[2048,256]{1,0:T(8,128)S(1)} %fusion.20.part_ref), custom_call_target="tpu_custom_call" | custom-call | bytes 62914560 | tf_op jit(solution)/shard_map/total_rows/pallas_call | solution.py:462
  239.2 13.4 %fusion.14.z_ref = f32[2048,800]{1,0:T(8,128)} fusion(bf16[1600,2048]{1,0:T(8,128)(2,1)} %copy-done.4, bf16[1600,3072]{1,0:T(8,128)(2,1)} %all-gather.3.cloned.1.call-done.refs_0_.refs_1_.refs_2_), kind=kOutput, calls=%fused_computation.55 | convolution fusion | flops 5242880000 | bytes 15974400 | tf_op jit(solution)/shard_map/dot_general | solution.py:46
  252.6 21.0 %scan_fwd.1 = (bf16[2048,800]{1,0:T(8,128)(2,1)S(1)}, f32[32,16,800]{2,1,0:T(8,128)S(1)}) custom-call(bf16[2048,800]{1,0:T(8,128)(2,1)S(1)} %get-tuple-element.287.xa_ref, f32[2048,800]{1,0:T(8,128)} %fusion.14.z_ref, bf16[2048,256]{1,0:T(8,128)(2,1)S(1)} %total_rows.2.dbl_ref, f32[2048,8]{1,0:T(8,128)S(1)} %copy.134.mask_ref, f32[1,2048]{1,0:T(1,128)S(1)} %bitcast.161, ...), custom_call_target="tpu_custom_call" | custom-call | bytes 97517568 | tf_op jit(solution)/shard_map/scan_fwd/pallas_call | solution.py:1581
  273.6 1.8 copy-done.17
  275.4 41.3 %attn_reduce.1 = f32[1600,512]{1,0:T(8,128)S(1)} custom-call(bf16[1600,3072]{1,0:T(8,128)(2,1)} %all-gather.3.cloned.1.call-done.refs_0_.refs_1_.refs_2_, bf16[640,2048]{1,0:T(8,128)(2,1)S(1)} %copy-done.15), custom_call_target="tpu_custom_call" | custom-call | bytes 161480704 | tf_op jit(solution)/shard_map/attn_reduce/pallas_call | solution.py:839
  316.7 42.4 %ssm_reduce.1 = f32[1600,512]{1,0:T(8,128)S(1)} custom-call(bf16[1600,3072]{1,0:T(8,128)(2,1)} %all-gather.3.cloned.1.call-done.refs_0_.refs_1_.refs_2_, bf16[2048,800]{1,0:T(8,128)(2,1)} %copy-done.17), custom_call_target="tpu_custom_call" | custom-call | bytes 161480704 | tf_op jit(solution)/shard_map/ssm_reduce/pallas_call | solution.py:839
  360.9 1.3 copy-done.35
  365.3 1.6 multiply_convert_fusion.1.refs_0_
  366.8 5.3 all-gather.5.cloned.1.call-done.refs_1_.refs_0_
  372.1 1.4 copy-done.20
  373.5 49.8 %gate_turn.1 = (bf16[1600,2048]{1,0:T(8,128)(2,1)}, f32[2048,1376]{1,0:T(8,128)}, f32[2048,1376]{1,0:T(8,128)}, bf16[2048,1376]{1,0:T(8,128)(2,1)}) custom-call(bf16[1600,512]{1,0:T(8,128)(2,1)S(1)} %copy-done.20, bf16[1600,4224]{1,0:T(8,128)(2,1)} %all-gather.5.cloned.1.call-done.refs_1_.refs_0_), custom_call_target="tpu_custom_call" | custom-call | bytes 196083712 | tf_op jit(solution)/shard_map/gate_turn/pallas_call | solution.py:371
  423.4 42.2 %down_reduce.1 = f32[1600,512]{1,0:T(8,128)S(1)} custom-call(bf16[1600,4224]{1,0:T(8,128)(2,1)} %all-gather.5.cloned.1.call-done.refs_1_.refs_0_, bf16[2048,1376]{1,0:T(8,128)(2,1)} %get-tuple-element.109.refs_1_.refs_5_), custom_call_target="tpu_custom_call" | custom-call | bytes 169869312 | tf_op jit(solution)/shard_map/down_reduce/pallas_call | solution.py:839
  465.6 1.4 fusion.19.refs_0_
  467.6 48.5 %grad_turn.1 = (bf16[1600,2048]{1,0:T(8,128)(2,1)}, bf16[2048,1376]{1,0:T(8,128)(2,1)}, bf16[2048,1376]{1,0:T(8,128)(2,1)}) custom-call(bf16[1600,512]{1,0:T(8,128)(2,1)S(1)} %fusion.19.refs_0_, bf16[1600,4224]{1,0:T(8,128)(2,1)} %all-gather.5.cloned.1.call-done.refs_1_.refs_0_, f32[2048,1376]{1,0:T(8,128)} %get-tuple-element.112.refs_2_, ...), custom_call_target="tpu_custom_call" | custom-call | bytes 196083712 | tf_op jit(solution)/shard_map/grad_turn/pallas_call | solution.py:371
  516.1 41.0 %ffn_weight_grads.1 = bf16[1600,4224]{1,0:T(8,128)(2,1)} custom-call(bf16[1600,2048]{1,0:T(8,128)(2,1)} %get-tuple-element.116.refs_0_.refs_2_, bf16[2048,1376]{1,0:T(8,128)(2,1)} %get-tuple-element.118.refs_1_, bf16[1600,2048]{1,0:T(8,128)(2,1)} %get-tuple-element.116.refs_0_.refs_2_, bf16[2048,1376]{1,0:T(8,128)(2,1)} %get-tuple-element.119.refs_3_.refs_2_, ...), custom_call_target="tpu_custom_call" | custom-call | bytes 165675008 | tf_op jit(solution)/shard_map/ffn_weight_grads/pallas_call | solution.py:591
  557.2 44.8 %mid_reduce.1 = f32[1600,512]{1,0:T(8,128)S(1)} custom-call(bf16[1600,4224]{1,0:T(8,128)(2,1)} %all-gather.5.cloned.1.call-done.refs_1_.refs_0_, bf16[2048,1376]{1,0:T(8,128)(2,1)} %get-tuple-element.118.refs_1_, bf16[2048,1376]{1,0:T(8,128)(2,1)} %get-tuple-element.119.refs_3_.refs_2_), custom_call_target="tpu_custom_call" | custom-call | bytes 188743680 | tf_op jit(solution)/shard_map/mid_reduce/pallas_call | solution.py:839
  602.1 1.5 multiply_reduce_fusion.10
  605.1 4.5 multiply_reduce_fusion.8
  609.7 1.5 fusion.7
  611.3 39.9 %gather_rows.2.refs_2_ = bf16[1600,2048]{1,0:T(8,128)(2,1)S(1)} custom-call(bf16[1600,512]{1,0:T(8,128)(2,1)S(1)} %get-tuple-element.296.part_ref), custom_call_target="tpu_custom_call" | custom-call | bytes 147456000 | tf_op jit(solution)/shard_map/gather_rows/pallas_call | solution.py:129
  651.3 39.9 %gather_rows.3.refs_0_ = bf16[1600,2048]{1,0:T(8,128)(2,1)S(1)} custom-call(bf16[1600,512]{1,0:T(8,128)(2,1)S(1)} %get-tuple-element.121.part_ref), custom_call_target="tpu_custom_call" | custom-call | bytes 147456000 | tf_op jit(solution)/shard_map/gather_rows/pallas_call | solution.py:129
  691.2 2.6 copy-done.12
  693.8 12.1 %fusion.12.gs_ref = f32[2048,800]{1,0:T(8,128)} fusion(bf16[1600,2048]{1,0:T(8,128)(2,1)S(1)} %gather_rows.2.refs_2_, bf16[1600,3072]{1,0:T(8,128)(2,1)} %all-gather.3.cloned.1.call-done.refs_0_.refs_1_.refs_2_), kind=kOutput, calls=%fused_computation.53 | convolution fusion | flops 5242880000 | bytes 15974400 | tf_op jit(solution)/shard_map/dot_general | solution.py:46
  705.9 39.5 %scan_bwd.1 = (bf16[2048,800]{1,0:T(8,128)(2,1)}, f32[2048,800]{1,0:T(8,128)}, f32[2048,256]{1,0:T(8,128)}, f32[100,800]{1,0:T(8,128)S(1)}, f32[8,800]{1,0:T(8,128)S(1)}) custom-call(bf16[2048,800]{1,0:T(8,128)(2,1)} %copy-done.6, f32[2048,800]{1,0:T(8,128)} %fusion.14.z_ref, bf16[2048,256]{1,0:T(8,128)(2,1)S(1)} %copy-done.19, f32[2048,8]{1,0:T(8,128)S(1)} %copy-done.11, ...), custom_call_target="tpu_custom_call" | custom-call | bytes 255852544 | tf_op jit(solution)/shard_map/scan_bwd/pallas_call | solution.py:1608
  745.4 26.9 %mid_weight_grads.1 = bf16[1600,2240]{1,0:T(8,128)(2,1)} custom-call(bf16[1600,2048]{1,0:T(8,128)(2,1)} %copy-done.12, bf16[640,2048]{1,0:T(8,128)(2,1)} %copy-done.14, bf16[1600,2048]{1,0:T(8,128)(2,1)} %copy-done.13, bf16[2048,800]{1,0:T(8,128)(2,1)} %copy-done.17, bf16[1600,2048]{1,0:T(8,128)(2,1)} %copy-done.4, bf16[2048,800]{1,0:T(8,128)(2,1)} %get-tuple-element.126.refs_5_), custom_call_target="tpu_custom_call" | custom-call | bytes 97517568 | tf_op jit(solution)/shard_map/mid_weight_grads/pallas_call | solution.py:591
  772.3 4.3 reduce-scatter.10.cloned.1.call-done
  776.8 8.6 convolution_convert_fusion.1.dot_ref
  785.4 37.3 %attn_bwd.1.refs_3_ = bf16[896,2048]{1,0:T(8,128)(2,1)S(1)} custom-call(s32[16]{0:T(128)S(1)} %copy-done.30, bf16[896,2048]{1,0:T(8,128)(2,1)S(1)} %copy-done.1, bf16[640,2048]{1,0:T(8,128)(2,1)S(1)} %convolution_convert_fusion.1.dot_ref, bf16[640,2048]{1,0:T(8,128)(2,1)S(1)} %copy-done.16, f32[2,8,2048]{2,1,0:T(8,128)S(1)} %copy-done.28, ...), custom_call_target="tpu_custom_call" | custom-call | bytes 167772160 | tf_op jit(solution)/shard_map/attn_bwd/pallas_call | solution.py:1213
  822.8 20.6 %total_rows.3 = bf16[2048,256]{1,0:T(8,128)(2,1)S(1)} custom-call(f32[2048,256]{1,0:T(8,128)S(1)} %copy-done.24), custom_call_target="tpu_custom_call" | custom-call | bytes 62914560 | tf_op jit(solution)/shard_map/total_rows/pallas_call | solution.py:462
  845.0 26.7 %multiply_reduce_fusion.2 = (f32[800]{0:T(1024)S(1)}, f32[800]{0:T(1024)S(1)}, f32[800]{0:T(1024)S(1)}, f32[800]{0:T(1024)S(1)}, bf16[800]{0:T(1024)(128)(2,1)S(...) fusion(f32[1,2048,800]{2,1,0:T(8,128)} %bitcast.165, ...), kind=kOutput, calls=%fused_computation.12 | convolution fusion | flops 883093760 | bytes 53741376 | tf_op jit(solution)/shard_map/dot_general | solution.py:40
  873.1 13.0 %fusion.3.refs_1_.refs_4_ = bf16[2048,800]{1,0:T(8,128)(2,1)} fusion(f32[1,2048,800]{2,1,0:T(8,128)} %get-tuple-element.291, f32[1,2048,800]{2,1,0:T(8,128)} %get-tuple-element.292, f32[1,2048,800]{2,1,0:T(8,128)} %get-tuple-element.293, f32[1,2048,800]{2,1,0:T(8,128)} %get-tuple-element.294), kind=kLoop, calls=%fused_computation.23 | loop fusion | flops 6553600 | bytes 29491200 | tf_op jit(solution)/shard_map/convert_element_type | solution.py:1692
  886.1 19.6 %last_weight_grads.1 = bf16[1600,1920]{1,0:T(8,128)(2,1)} custom-call(bf16[1600,2048]{1,0:T(8,128)(2,1)} %copy-done.4, bf16[2048,800]{1,0:T(8,128)(2,1)} %fusion.3.refs_1_.refs_4_, bf16[1600,2048]{1,0:T(8,128)(2,1)} %copy-done.4, bf16[896,2048]{1,0:T(8,128)(2,1)} %copy-done.5, bf16[1600,120]{1,0:T(8,128)(2,1)S(1)} %convert_element_type.204.refs_4_), custom_call_target="tpu_custom_call" | custom-call | bytes 75497472 | tf_op jit(solution)/shard_map/last_weight_grads/pallas_call | solution.py:591
  905.6 7.9 reduce-scatter.8.cloned.1.call-done
  913.7 1.8 convert_bitcast_fusion
  916.6 44.6 %in_reduce.1 = f32[1600,512]{1,0:T(8,128)S(1)} custom-call(bf16[1600,896]{1,0:T(8,128)(2,1)S(1)} %bitcast.158, bf16[1600,3072]{1,0:T(8,128)(2,1)} %all-gather.3.cloned.1.call-done.refs_0_.refs_1_.refs_2_, bf16[1600,3072]{1,0:T(8,128)(2,1)} %all-gather.3.cloned.1.call-done.refs_0_.refs_1_.refs_2_, bf16[896,2048]{1,0:T(8,128)(2,1)} %copy-done.5, ...), custom_call_target="tpu_custom_call" | custom-call | bytes 196083712 | tf_op jit(solution)/shard_map/in_reduce/pallas_call | solution.py:839
  962.4 12.7 %farewell.1 = f32[8,256]{1,0:T(8,128)S(1)} custom-call(f32[8,8,256]{2,1,0:T(8,128)S(1)} %pad.58.part_ref), custom_call_target="tpu_custom_call" | custom-call | bytes 41943040 | tf_op jit(solution)/shard_map/farewell/pallas_call | solution.py:657
  976.1 10.8 gather_stack.1
  988.0 2.2 convert_bitcast_fusion.1
  990.2 4.4 fusion.8
  994.6 40.8 %reduce-scatter.12.cloned.1.call-done = bf16[200,1920]{1,0:T(8,128)(2,1)} async-done(((bf16[1600,1920]{1,0:T(8,128)(2,1)}), bf16[200,1920]{1,0:T(8,128)(2,1)}) %reduce-scatter.12.cloned.1.call-update) | async-done | bytes 768016 | tf_op jit(solution)/shard_map/optimization_barrier | solution.py:1938
  1035.4 2.2 convert_reduce_fusion
  1037.6 2.0 bitcast_convert_fusion
  1041.5 19.1 %gather_final.1 = (bf16[4,200,1024]{2,1,0:T(8,128)(2,1)S(1)}, bf16[4,200,128]{2,1,0:T(8,128)(2,1)S(1)}) custom-call(bf16[200,1024]{1,0:T(8,128)(2,1)S(1)} %pad.60.part_ref, bf16[200,128]{1,0:T(8,128)(2,1)S(1)} %slice.278.inner_ref), custom_call_target="tpu_custom_call" | custom-call | bytes 62914560 | tf_op jit(solution)/shard_map/gather_final/pallas_call | solution.py:1020
  1067.4 1.8 copy.155
  1069.2 1.6 copy.156
  1071.8 1.8 concatenate.69
  1073.6 2.4 concatenate.66
  1076.0 1.8 concatenate.68
  (345 shorter events, 38.3 us)
Async XLA Ops:
  7.2 190.7 %all-gather.3.cloned.1.call-start = ((), (), s32[]{:S(2)}) async-start(), calls=%async_computation.3 | async-start | bytes 11059200 | tf_op jit(solution)/shard_map/all_gather | solution.py:1693
  10.7 18.5 %copy-start.67 = (bf16[200,320]{1,0:T(8,128)(2,1)S(1)}, bf16[200,320]{1,0:T(8,128)(2,1)}, u32[]{:S(2)}) copy-start(bf16[200,320]{1,0:T(8,128)(2,1)} %param.31) | copy-start | bytes 384004
  10.7 18.5 %copy-start.68 = (bf16[200,320]{1,0:T(8,128)(2,1)S(1)}, bf16[200,320]{1,0:T(8,128)(2,1)}, u32[]{:S(2)}) copy-start(bf16[200,320]{1,0:T(8,128)(2,1)} %param.30) | copy-start | bytes 384004
  14.4 357.7 %all-gather.5.cloned.1.call-start = ((), (), s32[]{:S(2)}) async-start(), calls=%async_computation.4 | async-start | bytes 15206400 | tf_op jit(solution)/shard_map/all_gather | solution.py:1693
  33.1 59.3 %copy-start.80 = (f32[512]{0:T(512)}, f32[512]{0:T(512)S(1)}, u32[]{:S(2)}) copy-start(f32[512]{0:T(512)S(1)} %fusion.10) | copy-start | bytes 6148
  33.7 58.8 %copy-start.70 = (f32[512]{0:T(512)}, f32[512]{0:T(512)S(1)}, u32[]{:S(2)}) copy-start(f32[512]{0:T(512)S(1)} %fusion.36) | copy-start | bytes 6148
  33.7 63.2 %copy-start.50 = (bf16[200,1376]{1,0:T(8,128)(2,1)S(1)}, bf16[200,1376]{1,0:T(8,128)(2,1)}, u32[]{:S(2)}) copy-start(bf16[200,1376]{1,0:T(8,128)(2,1)} %param.45) | copy-start | bytes 1651204
  33.7 63.2 %copy-start.51 = (bf16[200,1376]{1,0:T(8,128)(2,1)S(1)}, bf16[200,1376]{1,0:T(8,128)(2,1)}, u32[]{:S(2)}) copy-start(bf16[200,1376]{1,0:T(8,128)(2,1)} %param.46) | copy-start | bytes 1651204
  33.7 63.2 %copy-start.52 = (bf16[1376,200]{0,1:T(8,128)(2,1)S(1)}, bf16[1376,200]{0,1:T(8,128)(2,1)}, u32[]{:S(2)}) copy-start(bf16[1376,200]{0,1:T(8,128)(2,1)} %param.47) | copy-start | bytes 1651204
  34.1 65.5 %copy-start.58 = (s32[2048]{0:T(1024)S(1)}, s32[2048]{0:T(1024)}, u32[]{:S(2)}) copy-start(s32[2048]{0:T(1024)} %param.26) | copy-start | bytes 24580
  99.5 677.2 %reduce-scatter.10.cloned.1.call-start = ((), (), s32[]{:S(2)}) async-start(), calls=%async_computation.6 | async-start | bytes 15206400
  102.0 150.5 %copy-start.10 = (f32[2048,8]{1,0:T(8,128)}, f32[2048,8]{1,0:T(8,128)S(1)}, u32[]{:S(2)}) copy-start(f32[2048,8]{1,0:T(8,128)S(1)} %copy.134.mask_ref) | copy-start | bytes 196612
  102.3 10.0 copy-start.29
  112.3 35.3 %copy-start = (bf16[896,2048]{1,0:T(8,128)(2,1)}, bf16[896,2048]{1,0:T(8,128)(2,1)S(1)}, u32[]{:S(2)}) copy-start(bf16[896,2048]{1,0:T(8,128)(2,1)S(1)} %convolution_convert_fusion.qt_ref.kt_ref.vt_ref) | copy-start | bytes 11010052
  112.3 37.5 %copy-start.95 = (bf16[4,400]{1,0:T(4,128)(2,1)S(1)}, bf16[4,400]{1,0:T(4,128)(2,1)}, u32[]{:S(2)}) copy-start(bf16[4,400]{1,0:T(4,128)(2,1)} %param.34) | copy-start | bytes 9604
  112.4 37.6 %copy-start.63 = (bf16[400,132]{0,1:T(8,128)(2,1)S(1)}, bf16[400,132]{0,1:T(8,128)(2,1)}, u32[]{:S(2)}) copy-start(bf16[400,132]{0,1:T(8,128)(2,1)} %param.36) | copy-start | bytes 316804
  112.4 37.8 %copy-start.66 = (bf16[100,400]{0,1:T(8,128)(2,1)S(1)}, bf16[100,400]{0,1:T(8,128)(2,1)}, u32[]{:S(2)}) copy-start(bf16[100,400]{0,1:T(8,128)(2,1)} %param.37) | copy-start | bytes 240004
  194.1 22.9 %copy-start.59 = (bf16[800,32]{1,0:T(8,128)(2,1)}, bf16[800,32]{1,0:T(8,128)(2,1)S(1)}, u32[]{:S(2)}) copy-start(bf16[800,32]{1,0:T(8,128)(2,1)S(1)} %slice.264) | copy-start | bytes 153604
  194.3 22.8 %copy-start.61 = (bf16[800,100]{1,0:T(8,128)(2,1)}, bf16[800,100]{1,0:T(8,128)(2,1)S(1)}, u32[]{:S(2)}) copy-start(bf16[800,100]{1,0:T(8,128)(2,1)S(1)} %slice.263) | copy-start | bytes 480004
  194.6 22.4 %copy-start.105 = (bf16[256]{0:T(256)(128)(2,1)}, bf16[256]{0:T(256)(128)(2,1)S(1)}, u32[]{:S(2)}) copy-start(bf16[256]{0:T(256)(128)(2,1)S(1)} %pad.70.clone) | copy-start | bytes 1540
  194.7 22.4 %copy-start.107 = (bf16[256]{0:T(256)(128)(2,1)}, bf16[256]{0:T(256)(128)(2,1)S(1)}, u32[]{:S(2)}) copy-start(bf16[256]{0:T(256)(128)(2,1)S(1)} %pad.68.clone) | copy-start | bytes 1540
  197.1 11.7 %copy-start.86 = (f32[800]{0:T(1024)}, f32[800]{0:T(1024)S(1)}, u32[]{:S(2)}) copy-start(f32[800]{0:T(1024)S(1)} %get-tuple-element.280) | copy-start | bytes 9604
  197.1 11.7 %copy-start.88 = (f32[800]{0:T(1024)}, f32[800]{0:T(1024)S(1)}, u32[]{:S(2)}) copy-start(f32[800]{0:T(1024)S(1)} %get-tuple-element.281) | copy-start | bytes 9604
  197.1 11.7 %copy-start.90 = (f32[800]{0:T(1024)}, f32[800]{0:T(1024)S(1)}, u32[]{:S(2)}) copy-start(f32[800]{0:T(1024)S(1)} %get-tuple-element.282) | copy-start | bytes 9604
  197.1 11.7 %copy-start.92 = (f32[800]{0:T(1024)}, f32[800]{0:T(1024)S(1)}, u32[]{:S(2)}) copy-start(f32[800]{0:T(1024)S(1)} %get-tuple-element.283) | copy-start | bytes 9604
  208.7 8.3 copy-start.39
  217.0 35.6 %copy-start.6 = (bf16[2048,800]{1,0:T(8,128)(2,1)}, bf16[2048,800]{1,0:T(8,128)(2,1)S(1)}, u32[]{:S(2)}) copy-start(bf16[2048,800]{1,0:T(8,128)(2,1)S(1)} %get-tuple-element.287.xa_ref) | copy-start | bytes 9830404
  239.2 13.4 %copy-start.18 = (bf16[2048,256]{1,0:T(8,128)(2,1)}, bf16[2048,256]{1,0:T(8,128)(2,1)S(1)}, u32[]{:S(2)}) copy-start(bf16[2048,256]{1,0:T(8,128)(2,1)S(1)} %total_rows.2.dbl_ref) | copy-start | bytes 3145732
  252.6 22.8 %copy-start.15 = (bf16[640,2048]{1,0:T(8,128)(2,1)S(1)}, bf16[640,2048]{1,0:T(8,128)(2,1)}, u32[]{:S(2)}) copy-start(bf16[640,2048]{1,0:T(8,128)(2,1)} %copy-done.14) | copy-start | bytes 7864324
  275.4 41.3 %copy-start.25 = (f32[32,16,800]{2,1,0:T(8,128)}, f32[32,16,800]{2,1,0:T(8,128)S(1)}, u32[]{:S(2)}) copy-start(f32[32,16,800]{2,1,0:T(8,128)S(1)} %get-tuple-element.110.hsave_ref) | copy-start | bytes 4915204
  423.3 42.2 %copy-start.32 = (f32[1600,512]{1,0:T(8,128)S(1)}, f32[1600,512]{1,0:T(8,128)}, u32[]{:S(2)}) copy-start(f32[1600,512]{1,0:T(8,128)} %copy-done.31) | copy-start | bytes 9830404
  423.4 42.2 %copy-start.40 = (f32[512,1600]{0,1:T(8,128)S(1)}, f32[512,1600]{0,1:T(8,128)}, u32[]{:S(2)}) copy-start(f32[512,1600]{0,1:T(8,128)} %param.25) | copy-start | bytes 9830404
  423.4 42.2 %copy-start.76 = (f32[512]{0:T(512)S(1)}, f32[512]{0:T(512)}, u32[]{:S(2)}) copy-start(f32[512]{0:T(512)} %convert_multiply_fusion) | copy-start | bytes 6148
  557.1 356.4 %reduce-scatter.8.cloned.1.call-start = ((), (), s32[]{:S(2)}) async-start(), calls=%async_computation.5 | async-start | bytes 8294400 | tf_op jit(solution)/shard_map/reduce_scatter | solution.py:1694
  557.2 44.8 %copy-start.33 = (f32[1600,512]{1,0:T(8,128)S(1)}, f32[1600,512]{1,0:T(8,128)}, u32[]{:S(2)}) copy-start(f32[1600,512]{1,0:T(8,128)} %copy-done.31) | copy-start | bytes 9830404
  557.2 46.4 %copy-start.41 = (f32[512,1600]{0,1:T(8,128)S(1)}, f32[512,1600]{0,1:T(8,128)}, u32[]{:S(2)}) copy-start(f32[512,1600]{0,1:T(8,128)} %param.25) | copy-start | bytes 9830404
  651.3 39.9 %copy-start.13 = (bf16[1600,2048]{1,0:T(8,128)(2,1)}, bf16[1600,2048]{1,0:T(8,128)(2,1)S(1)}, u32[]{:S(2)}) copy-start(bf16[1600,2048]{1,0:T(8,128)(2,1)S(1)} %gather_rows.2.refs_2_) | copy-start | bytes 19660804
  693.8 12.1 %copy-start.11 = (f32[2048,8]{1,0:T(8,128)S(1)}, f32[2048,8]{1,0:T(8,128)}, u32[]{:S(2)}) copy-start(f32[2048,8]{1,0:T(8,128)} %copy-done.10) | copy-start | bytes 196612
  693.8 12.1 %copy-start.19 = (bf16[2048,256]{1,0:T(8,128)(2,1)S(1)}, bf16[2048,256]{1,0:T(8,128)(2,1)}, u32[]{:S(2)}) copy-start(bf16[2048,256]{1,0:T(8,128)(2,1)} %copy-done.18) | copy-start | bytes 3145732
  693.8 12.1 %copy-start.26 = (f32[32,16,800]{2,1,0:T(8,128)S(1)}, f32[32,16,800]{2,1,0:T(8,128)}, u32[]{:S(2)}) copy-start(f32[32,16,800]{2,1,0:T(8,128)} %copy-done.25) | copy-start | bytes 4915204
  776.7 8.7 copy-start.28
  776.7 8.7 copy-start.30
  776.7 258.7 %reduce-scatter.12.cloned.1.call-start = ((), (), s32[]{:S(2)}) async-start(), calls=%async_computation.7 | async-start | bytes 6912000
  776.8 8.7 copy-start.1
  776.8 8.7 copy-start.16
  785.4 37.4 %copy-start.24 = (f32[2048,256]{1,0:T(8,128)S(1)}, f32[2048,256]{1,0:T(8,128)}, u32[]{:S(2)}) copy-start(f32[2048,256]{1,0:T(8,128)} %get-tuple-element.128.part_ref) | copy-start | bytes 6291460
  822.7 22.1 %copy-start.5 = (bf16[896,2048]{1,0:T(8,128)(2,1)}, bf16[896,2048]{1,0:T(8,128)(2,1)S(1)}, u32[]{:S(2)}) copy-start(bf16[896,2048]{1,0:T(8,128)(2,1)S(1)} %attn_bwd.1.refs_3_) | copy-start | bytes 11010052
  822.7 20.7 %copy-start.7 = (bf16[2048,800]{1,0:T(8,128)(2,1)S(1)}, bf16[2048,800]{1,0:T(8,128)(2,1)}, u32[]{:S(2)}) copy-start(bf16[2048,800]{1,0:T(8,128)(2,1)} %copy-done.6) | copy-start | bytes 9830404
  905.6 8.0 copy-start.69
  905.6 8.0 copy-start.42
  916.6 44.6 %copy-start.36 = (f32[512,1600]{0,1:T(8,128)S(1)}, f32[512,1600]{0,1:T(8,128)}, u32[]{:S(2)}) copy-start(f32[512,1600]{0,1:T(8,128)} %param.24) | copy-start | bytes 9830404
  916.6 44.6 %copy-start.65 = (f32[1600]{0:T(1024)S(1)}, f32[1600]{0:T(1024)}, u32[]{:S(2)}) copy-start(f32[1600]{0:T(1024)} %copy-done.64) | copy-start | bytes 19204
  916.6 44.6 %copy-start.71 = (f32[512]{0:T(512)S(1)}, f32[512]{0:T(512)}, u32[]{:S(2)}) copy-start(f32[512]{0:T(512)} %copy-done.70) | copy-start | bytes 6148
  961.3 13.8 %copy-start.100 = (pred[768]{0:T(1024)(128)(4,1)S(1)}, pred[768]{0:T(1024)(128)(4,1)}, u32[]{:S(2)}) copy-start(pred[768]{0:T(1024)(128)(4,1)} %constant.85.clone.1) | copy-start | bytes 2308
  961.3 26.7 %copy-start.81 = (f32[512]{0:T(512)S(1)}, f32[512]{0:T(512)}, u32[]{:S(2)}) copy-start(f32[512]{0:T(512)} %copy-done.80) | copy-start | bytes 6148
  962.3 27.9 %copy-start.37 = (f32[512,1600]{0,1:T(8,128)S(1)}, f32[512,1600]{0,1:T(8,128)}, u32[]{:S(2)}) copy-start(f32[512,1600]{0,1:T(8,128)} %param.24) | copy-start | bytes 9830404
  1035.4 6.0 slice-start
  1067.4 6.2 copy-start.46
  1067.4 6.2 copy-start.47
  1067.4 6.2 copy-start.48
  1071.8 6.0 copy-start.53
  1071.8 6.0 copy-start.54
  1071.8 6.0 copy-start.55
  1071.8 6.0 copy-start.56
  (51 other events, 143.5 us)
Sparse Core Ops, SparseCore 0:
  14.5 166.6 all-gather.2
  183.4 188.6 all-gather.4
  557.2 219.3 reduce-scatter.9
  780.2 133.3 reduce-scatter.7
  917.6 117.7 reduce-scatter.11
where the time goes:
time: 1090 us
  Pallas kernels  811 us (74%)
  matrix products  84.1 us (8%)
  other arithmetic  58.4 us (5%)
  waiting for transfers between devices  58.4 us (5%)
  local copies, waits for them, and re-layouts  56.2 us (5%)
  between operations  17.2 us (2%)
    pallas_call x5, Pallas kernels, product_reduce(): pl.pallas_call(functools.partial(product_kernel, plan, leads, right_flips...  215 us
    pallas_call x2, Pallas kernels, turn_rows(): pl.pallas_call(functools.partial(turn_kernel, combine, plan, len(ins), le...  98.3 us
    pallas_call x3, Pallas kernels, weight_grads(): pl.pallas_call(functools.partial(weights_kernel, plan), name=name, grid=(...  87.5 us
    pallas_call x2, Pallas kernels, gather_rows(): pl.pallas_call(gather_kernel, name='gather_rows', in_specs=[pl.BlockSpec(...  79.8 us
    pallas_call x1, Pallas kernels, gather_first(): pl.pallas_call(first_kernel, name='gather_first', in_specs=[anywhere] * 2...  58.4 us
    dot_general x5, matrix products, dot_first(): lax.dot_general(left, right, (((0,), (0,)), ((), ())), preferred_element_...  47.5 us
    pallas_call x1, Pallas kernels, inner_spread(): pl.pallas_call(spread_kernel, name='inner_spread', in_specs=[whole], out_...  43.5 us
    pallas_call x2, Pallas kernels, total_rows(): pl.pallas_call(total_kernel, name='total_rows', in_specs=[whole], out_spe...  41.4 us
  transfers between devices with their start and end apart: 5, of which 4 were waited for; matrix products, arithmetic and copies ran while one was open for 13% of the time, Pallas kernels for 56%

commit v1 on v0

--- a/solution.py
+++ b/solution.py
@@ -280,9 +280,9 @@
     sems = scratch[n_in + n_out + 4 :]
     me, side, cross, diag = tensor_peers()
     depth, size = part_ref.shape
-    half = size // 2
-    tiles = [(block, at) for block in (me, side) for at in (0, 1)]
-    tiles += [(block, at) for at in (0, 1) for block in (cross, diag)]
+    half = size // PIECES
+    tiles = [(block, at) for block in (me, side) for at in range(PIECES)]
+    tiles += [(block, at) for at in range(PIECES) for block in (cross, diag)]
     place = lambda block, at: pl.ds(pl.multiple_of(block * size + at * half, half), half)
     local = lambda at: pl.ds(at * half, half)
 
@@ -316,21 +316,21 @@
     greet((side, cross))
     over = [
         push(part_ref.at[:, local(at)], whole_ref.at[:, place(me, at)], sems[0:2], at, cross)
-        for at in (0, 1)
+        for at in range(PIECES)
     ]
     near = [
         push(part_ref.at[:, local(at)], whole_ref.at[:, place(me, at)], sems[2:4], at, side)
-        for at in (0, 1)
+        for at in range(PIECES)
     ]
-    relay = [None, None]
+    relay = [None] * PIECES
     own.wait()
     for tile, (block, at) in enumerate(tiles):
         if tile + 1 < len(tiles):
             for index in range(n_in):
                 in_load(index, tile + 1).start()
-        if tile in (2, 3):
+        if PIECES <= tile < 2 * PIECES:
             near[at].wait_recv()
-        if tile in (4, 6):
+        if tile >= 2 * PIECES and tile % 2 == 0:
             over[at].wait_recv()
             relay[at] = push(
                 whole_ref.at[:, place(cross, at)],
@@ -339,7 +339,7 @@
                 at,
                 side,
             )
-        if tile in (5, 7):
+        if tile >= 2 * PIECES and tile % 2 == 1:
             relay[at].wait_recv()
         left = whole_ref[:, place(block, at)]
         products = []
@@ -358,7 +358,7 @@
     for tile in (len(tiles) - 2, len(tiles) - 1):
         for index in range(n_out):
             out_store(index, tile).wait()
-    for at in (0, 1):
+    for at in range(PIECES):
         over[at].wait_send()
         near[at].wait_send()
         relay[at].wait_send()
@@ -366,7 +366,7 @@
 
 def turn_rows(part, weight, ins, outs, plan, combine, call_id, name, micros):
     depth, size = part.shape
-    half = size // 2
+    half = size // PIECES
     anywhere = pl.BlockSpec(memory_space=pl.ANY)
     return pl.pallas_call(
         functools.partial(turn_kernel, combine, plan, len(ins), len(outs)),
@@ -386,7 +386,7 @@
             pltpu.SemaphoreType.DMA((len(outs), 2)),
             pltpu.SemaphoreType.DMA,
         ]
-        + [pltpu.SemaphoreType.DMA((2,))] * 6,
+        + [pltpu.SemaphoreType.DMA((PIECES,))] * 6,
         compiler_params=pltpu.CompilerParams(
             collective_id=call_id, has_side_effects=True, vmem_limit_bytes=52 << 20
         ),
@@ -548,7 +548,7 @@
     return gains_full, jnp.sum(counts_all[:, 0, 0])
 
 
-TILE = 400
+TILE = 320
 
 
 def weights_kernel(plan, *refs):
@@ -934,7 +934,9 @@
     return spread[:, :rows, :cols].reshape(share * rows, cols)
 
 
-def final_kernel(part_ref, inner_ref, whole_ref, owned_ref, own_sem, *sems):
+def final_kernel(starts, last_ref, whole_ref, owned_ref, own_sem, *sems):
+    part_ref = last_ref.at[:, pl.ds(starts[0], whole_ref.shape[2])]
+    inner_ref = last_ref.at[:, pl.ds(starts[1], owned_ref.shape[2])]
     me, side, cross, diag = tensor_peers()
     place = lax.axis_index("dp")
     ranks = owned_ref.shape[0]
@@ -959,16 +961,18 @@
     goals = [(owner != place) | (me != index) for index in range(ranks)]
     pl.semaphore_wait(barrier, 2 + sum(goal.astype(jnp.int32) for goal in goals))
 
-    step = part_ref.shape[1] // 2
+    span = whole_ref.shape[2]
+    step = -(-span // 256) * 128
     own = pltpu.make_async_copy(part_ref, whole_ref.at[me], own_sem.at[0])
     own.start()
-    cols = [pl.ds(0, step), pl.ds(step, step)]
+    cols = [pl.ds(0, step), pl.ds(step, span - step)]
+    shift = lambda at: pl.ds(starts[0] + at.start, at.size)
     over = [
-        push(part_ref.at[:, at], whole_ref.at[me, :, at], sems[0:2], i, cross)
+        push(last_ref.at[:, shift(at)], whole_ref.at[me, :, at], sems[0:2], i, cross)
         for i, at in enumerate(cols)
     ]
     near = [
-        push(part_ref.at[:, at], whole_ref.at[me, :, at], sems[2:4], i, side)
+        push(last_ref.at[:, shift(at)], whole_ref.at[me, :, at], sems[2:4], i, side)
         for i, at in enumerate(cols)
     ]
     kept = pltpu.make_async_copy(inner_ref, owned_ref.at[slot], own_sem.at[1])
@@ -1015,16 +1019,17 @@
         pl.when((source != place) | (source_rank != me))(arrival.wait_recv)
 
 
-def gather_final(part, inner):
+def gather_final(last, start, middle):
     anywhere = pl.BlockSpec(memory_space=pl.ANY)
+    rows, total = last.shape
     return pl.pallas_call(
-        final_kernel,
+        functools.partial(final_kernel, (start, middle)),
         name="gather_final",
-        in_specs=[anywhere] * 2,
+        in_specs=[anywhere],
         out_specs=[anywhere] * 2,
         out_shape=[
-            jax.ShapeDtypeStruct((4,) + part.shape, part.dtype),
-            jax.ShapeDtypeStruct((4,) + inner.shape, inner.dtype),
+            jax.ShapeDtypeStruct((4, rows, middle - start), last.dtype),
+            jax.ShapeDtypeStruct((4, rows, total - middle), last.dtype),
         ],
         scratch_shapes=[pltpu.SemaphoreType.DMA((2,))]
         + [pltpu.SemaphoreType.DMA((2,))] * 6
@@ -1033,7 +1038,7 @@
             collective_id=9, has_side_effects=True, vmem_limit_bytes=1 << 20
         ),
         cost_estimate=pl.CostEstimate(flops=0, bytes_accessed=60 << 20, transcendentals=0),
-    )(part, inner)
+    )(last)
 
 
 BQ = 256
@@ -1935,14 +1940,7 @@
     gains_own = farewell(gain_grads.T)
     wide = lambda part: jnp.pad(part, ((0, 0), (0, -part.shape[1] % 256)))
     out_stack = gather_stack(wide(mid_shard[:, :query_width]), 5)
-    gains_own, last_shard, grad_inputs, out_stack = tie(
-        (gains_own, last_shard, grad_inputs, out_stack)
-    )
     inner_step = -(-inner_width // 128) * 128
-    inner_at = inner_step + qkv_width
-    shared_all, owned = gather_final(wide(last_shard[:, inner_step:inner_at]), last_shard[:, inner_at:])
-    inner_cols = inner_grads.size // width
-    inner_sum = owned[:, :, :inner_cols].astype(jnp.float32).reshape(-1, inner_grads.shape[1])
     mamba_at = query_width
     gate_at = query_width + inner_width
     def merge(stack, start, size):
@@ -1952,6 +1950,21 @@
         )
         return jnp.concatenate(own + [both], axis=1)
 
+    early = (
+        gains_own,
+        grad_inputs,
+        merge(out_stack, 0, group_width),
+        mid_shard[:, mamba_at : mamba_at + inner_width].astype(jnp.float32),
+        ffn_shard[:, :ff_width].astype(jnp.float32),
+        ffn_shard[:, ff_step : ff_step + ff_width].astype(jnp.float32),
+        ffn_shard[:, 2 * ff_step : 2 * ff_step + ff_width].astype(jnp.float32),
+    )
+    early, last_shard = tie((early, last_shard))
+    gains_own, grad_inputs, grad_out_own, grad_back_own, grad_gate_own, grad_up_own, grad_down_own = early
+    inner_at = inner_step + qkv_width
+    shared_all, owned = gather_final(last_shard, inner_step, inner_at)
+    inner_cols = inner_grads.size // width
+    inner_sum = owned[:, :, :inner_cols].astype(jnp.float32).reshape(-1, inner_grads.shape[1])
     return (
         result.T,
         grad_inputs.T,
@@ -1959,7 +1972,7 @@
         merge(shared_all, 0, group_width),
         merge(shared_all, query_width, HEAD),
         merge(shared_all, query_width + 2 * HEAD, HEAD),
-        merge(out_stack, 0, group_width).T,
+        grad_out_own.T,
         jnp.stack(
             [last_shard[:, :inner_width], mid_shard[:, gate_at : gate_at + inner_width]], axis=1
         ).astype(jnp.float32),
@@ -1970,13 +1983,13 @@
         inner_sum[:, 0],
         inner_sum[:, 1],
         inner_sum[:, 2],
-        mid_shard[:, mamba_at : mamba_at + inner_width].T.astype(jnp.float32),
+        grad_back_own.T,
         gains_own[1],
         gains_own[2],
         gains_own[3],
-        ffn_shard[:, :ff_width].astype(jnp.float32),
-        ffn_shard[:, ff_step : ff_step + ff_width].astype(jnp.float32),
-        ffn_shard[:, 2 * ff_step : 2 * ff_step + ff_width].astype(jnp.float32).T,
+        grad_gate_own,
+        grad_up_own,
+        grad_down_own.T,
     )
 
 

time: 1090 us -> 1080 us (level)
    pallas_call x1, Pallas kernels: 43.5 us -> 21.6 us  [inner_spread(): pl.pallas_call(spread_kernel, name='inner_spread', in_specs=[whole], out_...]
    pallas_call x1, Pallas kernels: 35.2 us -> 50.7 us  [attn_forward(): pl.pallas_call(attn_fwd_kernel, name='attn_fwd', grid_spec=pltpu.Prefetch...]
    pallas_call x1, Pallas kernels: 37.3 us -> 51.1 us  [attn_backward(): pl.pallas_call(attn_bwd_kernel, name='attn_bwd', grid_spec=pltpu.Prefetch...]
    unnamed x221 -> x219, local copies, waits for them, and re-layouts: 26.4 us -> 25.6 us
  transfers between devices with their start and end apart: 5 -> 5, of which waited for: 4 -> 3; matrix products, arithmetic and copies ran while one was open for 13% -> 14% of each run, Pallas kernels for 56% -> 57%
where the time goes in v1:
time: 1080 us; the launch traced here: 1070 us
  Pallas kernels  809 us (75%)
  matrix products  84 us (8%)
  other arithmetic  56.9 us (5%)
  local copies, waits for them, and re-layouts  53.7 us (5%)
  waiting for transfers between devices  51.6 us (5%)
  between operations  17.3 us (2%)
    pallas_call x5, Pallas kernels, product_reduce(): pl.pallas_call(functools.partial(product_kernel, plan, leads, right_flips...  215 us
    pallas_call x2, Pallas kernels, turn_rows(): pl.pallas_call(functools.partial(turn_kernel, combine, plan, len(ins), le...  91.9 us
    pallas_call x3, Pallas kernels, weight_grads(): pl.pallas_call(functools.partial(weights_kernel, plan), name=name, grid=(...  86.9 us
    pallas_call x2, Pallas kernels, gather_rows(): pl.pallas_call(gather_kernel, name='gather_rows', in_specs=[pl.BlockSpec(...  79.8 us
    pallas_call x1, Pallas kernels, gather_first(): pl.pallas_call(first_kernel, name='gather_first', in_specs=[anywhere] * 2...  58.3 us
    pallas_call x1, Pallas kernels, attn_backward(): pl.pallas_call(attn_bwd_kernel, name='attn_bwd', grid_spec=pltpu.Prefetch...  51.1 us
    pallas_call x1, Pallas kernels, attn_forward(): pl.pallas_call(attn_fwd_kernel, name='attn_fwd', grid_spec=pltpu.Prefetch...  50.7 us
    dot_general x5, matrix products, dot_first(): lax.dot_general(left, right, (((0,), (0,)), ((), ())), preferred_element_...  47.5 us
  transfers between devices with their start and end apart: 5, of which 3 were waited for; matrix products, arithmetic and copies ran while one was open for 14% of the time, Pallas kernels for 57%

profile of v1, /device:TPU:17, one launch (start us, length us, event | category | flops | bytes accessed | tf_op | source)
XLA Modules:
  0.0 1072.6 jit_solution(14924147543911416268)
XLA Ops:
  7.2 2.1 reshape.293
  9.4 1.1 constant_dynamic-slice_fusion.3
  10.7 2.5 concatenate.54
  17.0 11.2 %hello.1 = (f32[8,8,256]{2,1,0:T(8,128)}, f32[8,8,128]{2,1,0:T(8,128)}) custom-call(f32[8,256]{1,0:T(8,128)} %fusion.32.gain_ref, f32[8,128]{1,0:T(8,128)} %broadcast_in_dim.73.count_ref), custom_call_target="tpu_custom_call" | custom-call | bytes 31457280 | tf_op jit(solution)/shard_map/hello/pallas_call | solution.py:530
  29.4 1.1 fusion.44
  30.7 2.4 fusion.10
  34.1 58.3 %gather_first.1 = (bf16[1600,2048]{1,0:T(8,128)(2,1)S(1)}, bf16[8,200,896]{2,1,0:T(8,128)(2,1)S(1)}) custom-call(bf16[1600,512]{1,0:T(8,128)(2,1)S(1)} %multiply_convert_fusion.2.part_ref, bf16[200,896]{1,0:T(8,128)(2,1)S(1)} %concatenate.56.shard_ref), custom_call_target="tpu_custom_call" | custom-call | bytes 283115520 | tf_op jit(solution)/shard_map/gather_first/pallas_call | solution.py:251
  92.5 2.8 copy-done.4
  95.3 1.5 copy-done.21
  96.9 2.6 concatenate.63
  102.4 10.0 convolution_convert_fusion.qt_ref.kt_ref.vt_ref
  112.4 50.7 %attn_fwd.1 = (bf16[640,2048]{1,0:T(8,128)(2,1)S(1)}, f32[2,8,2048]{2,1,0:T(8,128)S(1)}) custom-call(s32[16]{0:T(128)S(1)} %pad_add_fusion.4.first_ref, bf16[896,2048]{1,0:T(8,128)(2,1)S(1)} %convolution_convert_fusion.qt_ref.kt_ref.vt_ref, bf16[896,2048]{1,0:T(8,128)(2,1)S(1)} %convolution_convert_fusion.qt_ref.kt_ref.vt_ref, ...), custom_call_target="tpu_custom_call" | custom-call | bytes 157286400 | tf_op jit(solution)/shard_map/attn_fwd/pallas_call | solution.py:1121
  163.1 1.5 copy-done.14
  166.0 21.6 %inner_spread.1 = bf16[2,400,256]{2,1,0:T(8,128)(2,1)S(1)} custom-call(bf16[400,256]{1,0:T(8,128)(2,1)S(1)} %pad.45.part_ref), custom_call_target="tpu_custom_call" | custom-call | bytes 41943040 | tf_op jit(solution)/shard_map/inner_spread/pallas_call | solution.py:922
  188.5 1.4 slice_reduce_fusion.10
  191.5 10.8 %fusion.16 = f32[2048,800]{1,0:T(8,128)S(1)} fusion(bf16[1600,2048]{1,0:T(8,128)(2,1)} %copy-done.4, bf16[1600,3072]{1,0:T(8,128)(2,1)} %all-gather.3.cloned.1.call-done.refs_0_.refs_1_.refs_2_), kind=kOutput, calls=%fused_computation.57 | convolution fusion | flops 5242880000 | bytes 15974400 | tf_op jit(solution)/shard_map/dot_general | solution.py:46
  202.4 8.2 fusion.4
  210.6 1.3 fusion.20.part_ref
  211.9 22.7 %total_rows.2.dbl_ref = bf16[2048,256]{1,0:T(8,128)(2,1)S(1)} custom-call(f32[2048,256]{1,0:T(8,128)S(1)} %fusion.20.part_ref), custom_call_target="tpu_custom_call" | custom-call | bytes 62914560 | tf_op jit(solution)/shard_map/total_rows/pallas_call | solution.py:462
  234.7 13.4 %fusion.14.z_ref = f32[2048,800]{1,0:T(8,128)} fusion(bf16[1600,2048]{1,0:T(8,128)(2,1)} %copy-done.4, bf16[1600,3072]{1,0:T(8,128)(2,1)} %all-gather.3.cloned.1.call-done.refs_0_.refs_1_.refs_2_), kind=kOutput, calls=%fused_computation.55 | convolution fusion | flops 5242880000 | bytes 15974400 | tf_op jit(solution)/shard_map/dot_general | solution.py:46
  248.1 21.3 %scan_fwd.1 = (bf16[2048,800]{1,0:T(8,128)(2,1)S(1)}, f32[32,16,800]{2,1,0:T(8,128)S(1)}) custom-call(bf16[2048,800]{1,0:T(8,128)(2,1)S(1)} %get-tuple-element.295.xa_ref, f32[2048,800]{1,0:T(8,128)} %fusion.14.z_ref, bf16[2048,256]{1,0:T(8,128)(2,1)S(1)} %total_rows.2.dbl_ref, f32[2048,8]{1,0:T(8,128)S(1)} %copy.134.mask_ref, f32[1,2048]{1,0:T(1,128)S(1)} %bitcast.159, ...), custom_call_target="tpu_custom_call" | custom-call | bytes 97517568 | tf_op jit(solution)/shard_map/scan_fwd/pallas_call | solution.py:1586
  269.4 1.8 copy-done.17
  271.2 41.3 %attn_reduce.1 = f32[1600,512]{1,0:T(8,128)S(1)} custom-call(bf16[1600,3072]{1,0:T(8,128)(2,1)} %all-gather.3.cloned.1.call-done.refs_0_.refs_1_.refs_2_, bf16[640,2048]{1,0:T(8,128)(2,1)S(1)} %copy-done.15), custom_call_target="tpu_custom_call" | custom-call | bytes 161480704 | tf_op jit(solution)/shard_map/attn_reduce/pallas_call | solution.py:839
  312.6 42.4 %ssm_reduce.1 = f32[1600,512]{1,0:T(8,128)S(1)} custom-call(bf16[1600,3072]{1,0:T(8,128)(2,1)} %all-gather.3.cloned.1.call-done.refs_0_.refs_1_.refs_2_, bf16[2048,800]{1,0:T(8,128)(2,1)} %copy-done.17), custom_call_target="tpu_custom_call" | custom-call | bytes 161480704 | tf_op jit(solution)/shard_map/ssm_reduce/pallas_call | solution.py:839
  356.7 1.4 copy-done.35
  358.1 1.3 multiply_reduce_fusion.11
  360.0 1.1 copy-done.31
  361.2 1.5 multiply_convert_fusion.1.refs_0_
  362.7 12.7 %all-gather.5.cloned.1.call-done.refs_1_.refs_0_ = bf16[1600,4224]{1,0:T(8,128)(2,1)} async-done(((bf16[200,4224]{1,0:T(8,128)(2,1)}), bf16[1600,4224]{1,0:T(8,128)(2,1)}) %all-gather.5.cloned.1.call-update) | async-done | bytes 13516816 | tf_op jit(solution)/shard_map/all_gather | solution.py:1698
  375.4 1.4 copy-done.20
  376.8 46.6 %gate_turn.1 = (bf16[1600,2048]{1,0:T(8,128)(2,1)}, f32[2048,1376]{1,0:T(8,128)}, f32[2048,1376]{1,0:T(8,128)}, bf16[2048,1376]{1,0:T(8,128)(2,1)}) custom-call(bf16[1600,512]{1,0:T(8,128)(2,1)S(1)} %copy-done.20, bf16[1600,4224]{1,0:T(8,128)(2,1)} %all-gather.5.cloned.1.call-done.refs_1_.refs_0_), custom_call_target="tpu_custom_call" | custom-call | bytes 196083712 | tf_op jit(solution)/shard_map/gate_turn/pallas_call | solution.py:371
  423.5 42.9 %down_reduce.1 = f32[1600,512]{1,0:T(8,128)S(1)} custom-call(bf16[1600,4224]{1,0:T(8,128)(2,1)} %all-gather.5.cloned.1.call-done.refs_1_.refs_0_, bf16[2048,1376]{1,0:T(8,128)(2,1)} %get-tuple-element.113.refs_1_.refs_5_), custom_call_target="tpu_custom_call" | custom-call | bytes 169869312 | tf_op jit(solution)/shard_map/down_reduce/pallas_call | solution.py:839
  466.5 1.4 fusion.19.refs_0_
  468.5 45.3 %grad_turn.1 = (bf16[1600,2048]{1,0:T(8,128)(2,1)}, bf16[2048,1376]{1,0:T(8,128)(2,1)}, bf16[2048,1376]{1,0:T(8,128)(2,1)}) custom-call(bf16[1600,512]{1,0:T(8,128)(2,1)S(1)} %fusion.19.refs_0_, bf16[1600,4224]{1,0:T(8,128)(2,1)} %all-gather.5.cloned.1.call-done.refs_1_.refs_0_, f32[2048,1376]{1,0:T(8,128)} %get-tuple-element.116.refs_2_, ...), custom_call_target="tpu_custom_call" | custom-call | bytes 196083712 | tf_op jit(solution)/shard_map/grad_turn/pallas_call | solution.py:371
  513.8 40.7 %ffn_weight_grads.1 = bf16[1600,4224]{1,0:T(8,128)(2,1)} custom-call(bf16[1600,2048]{1,0:T(8,128)(2,1)} %get-tuple-element.120.refs_0_.refs_2_, bf16[2048,1376]{1,0:T(8,128)(2,1)} %get-tuple-element.122.refs_1_, bf16[1600,2048]{1,0:T(8,128)(2,1)} %get-tuple-element.120.refs_0_.refs_2_, bf16[2048,1376]{1,0:T(8,128)(2,1)} %get-tuple-element.123.refs_3_.refs_2_, ...), custom_call_target="tpu_custom_call" | custom-call | bytes 165675008 | tf_op jit(solution)/shard_map/ffn_weight_grads/pallas_call | solution.py:591
  554.5 44.2 %mid_reduce.1 = f32[1600,512]{1,0:T(8,128)S(1)} custom-call(bf16[1600,4224]{1,0:T(8,128)(2,1)} %all-gather.5.cloned.1.call-done.refs_1_.refs_0_, bf16[2048,1376]{1,0:T(8,128)(2,1)} %get-tuple-element.122.refs_1_, bf16[2048,1376]{1,0:T(8,128)(2,1)} %get-tuple-element.123.refs_3_.refs_2_), custom_call_target="tpu_custom_call" | custom-call | bytes 188743680 | tf_op jit(solution)/shard_map/mid_reduce/pallas_call | solution.py:839
  598.8 1.5 multiply_reduce_fusion.10
  601.8 4.7 multiply_reduce_fusion.8
  606.5 1.6 fusion.7
  608.2 39.9 %gather_rows.2.refs_2_ = bf16[1600,2048]{1,0:T(8,128)(2,1)S(1)} custom-call(bf16[1600,512]{1,0:T(8,128)(2,1)S(1)} %get-tuple-element.304.part_ref), custom_call_target="tpu_custom_call" | custom-call | bytes 147456000 | tf_op jit(solution)/shard_map/gather_rows/pallas_call | solution.py:129
  648.1 39.9 %gather_rows.3.refs_0_ = bf16[1600,2048]{1,0:T(8,128)(2,1)S(1)} custom-call(bf16[1600,512]{1,0:T(8,128)(2,1)S(1)} %get-tuple-element.125.part_ref), custom_call_target="tpu_custom_call" | custom-call | bytes 147456000 | tf_op jit(solution)/shard_map/gather_rows/pallas_call | solution.py:129
  688.1 2.6 copy-done.12
  690.7 12.0 %fusion.12.gs_ref = f32[2048,800]{1,0:T(8,128)} fusion(bf16[1600,2048]{1,0:T(8,128)(2,1)S(1)} %gather_rows.2.refs_2_, bf16[1600,3072]{1,0:T(8,128)(2,1)} %all-gather.3.cloned.1.call-done.refs_0_.refs_1_.refs_2_), kind=kOutput, calls=%fused_computation.53 | convolution fusion | flops 5242880000 | bytes 15974400 | tf_op jit(solution)/shard_map/dot_general | solution.py:46
  702.8 39.8 %scan_bwd.1 = (bf16[2048,800]{1,0:T(8,128)(2,1)}, f32[2048,800]{1,0:T(8,128)}, f32[2048,256]{1,0:T(8,128)}, f32[100,800]{1,0:T(8,128)S(1)}, f32[8,800]{1,0:T(8,128)S(1)}) custom-call(bf16[2048,800]{1,0:T(8,128)(2,1)} %copy-done.6, f32[2048,800]{1,0:T(8,128)} %fusion.14.z_ref, bf16[2048,256]{1,0:T(8,128)(2,1)S(1)} %copy-done.19, f32[2048,8]{1,0:T(8,128)S(1)} %copy-done.11, ...), custom_call_target="tpu_custom_call" | custom-call | bytes 255852544 | tf_op jit(solution)/shard_map/scan_bwd/pallas_call | solution.py:1613
  742.5 26.7 %mid_weight_grads.1 = bf16[1600,2240]{1,0:T(8,128)(2,1)} custom-call(bf16[1600,2048]{1,0:T(8,128)(2,1)} %copy-done.12, bf16[640,2048]{1,0:T(8,128)(2,1)} %copy-done.14, bf16[1600,2048]{1,0:T(8,128)(2,1)} %copy-done.13, bf16[2048,800]{1,0:T(8,128)(2,1)} %copy-done.17, bf16[1600,2048]{1,0:T(8,128)(2,1)} %copy-done.4, bf16[2048,800]{1,0:T(8,128)(2,1)} %get-tuple-element.130.refs_5_), custom_call_target="tpu_custom_call" | custom-call | bytes 97517568 | tf_op jit(solution)/shard_map/mid_weight_grads/pallas_call | solution.py:591
  769.3 4.4 reduce-scatter.10.cloned.1.call-done
  773.8 8.6 convolution_convert_fusion.1.dot_ref
  782.5 51.1 %attn_bwd.1.refs_3_ = bf16[896,2048]{1,0:T(8,128)(2,1)S(1)} custom-call(s32[16]{0:T(128)S(1)} %copy-done.30, bf16[896,2048]{1,0:T(8,128)(2,1)S(1)} %copy-done.1, bf16[640,2048]{1,0:T(8,128)(2,1)S(1)} %convolution_convert_fusion.1.dot_ref, bf16[640,2048]{1,0:T(8,128)(2,1)S(1)} %copy-done.16, f32[2,8,2048]{2,1,0:T(8,128)S(1)} %copy-done.28, ...), custom_call_target="tpu_custom_call" | custom-call | bytes 167772160 | tf_op jit(solution)/shard_map/attn_bwd/pallas_call | solution.py:1218
  833.7 20.5 %total_rows.3 = bf16[2048,256]{1,0:T(8,128)(2,1)S(1)} custom-call(f32[2048,256]{1,0:T(8,128)S(1)} %copy-done.23), custom_call_target="tpu_custom_call" | custom-call | bytes 62914560 | tf_op jit(solution)/shard_map/total_rows/pallas_call | solution.py:462
  854.3 1.3 convolution_convert_fusion.2
  855.7 26.6 %multiply_reduce_fusion.2 = (f32[800]{0:T(1024)S(1)}, f32[800]{0:T(1024)S(1)}, f32[800]{0:T(1024)S(1)}, f32[800]{0:T(1024)S(1)}, bf16[800]{0:T(1024)(128)(2,1)S(...) fusion(f32[1,2048,800]{2,1,0:T(8,128)} %bitcast.163, ...), kind=kOutput, calls=%fused_computation.12 | convolution fusion | flops 883093760 | bytes 53741376 | tf_op jit(solution)/shard_map/dot_general | solution.py:40
  883.7 12.7 %fusion.3.refs_1_.refs_4_ = bf16[2048,800]{1,0:T(8,128)(2,1)} fusion(f32[1,2048,800]{2,1,0:T(8,128)} %get-tuple-element.299, f32[1,2048,800]{2,1,0:T(8,128)} %get-tuple-element.300, f32[1,2048,800]{2,1,0:T(8,128)} %get-tuple-element.301, f32[1,2048,800]{2,1,0:T(8,128)} %get-tuple-element.302), kind=kLoop, calls=%fused_computation.23 | loop fusion | flops 6553600 | bytes 29491200 | tf_op jit(solution)/shard_map/convert_element_type | solution.py:1697
  896.5 19.5 %last_weight_grads.1 = bf16[1600,1920]{1,0:T(8,128)(2,1)} custom-call(bf16[1600,2048]{1,0:T(8,128)(2,1)} %copy-done.4, bf16[2048,800]{1,0:T(8,128)(2,1)} %fusion.3.refs_1_.refs_4_, bf16[1600,2048]{1,0:T(8,128)(2,1)} %copy-done.4, bf16[896,2048]{1,0:T(8,128)(2,1)} %copy-done.5, bf16[1600,120]{1,0:T(8,128)(2,1)S(1)} %convert_element_type.201.refs_4_), custom_call_target="tpu_custom_call" | custom-call | bytes 75497472 | tf_op jit(solution)/shard_map/last_weight_grads/pallas_call | solution.py:591
  917.4 1.8 slice_convert_fusion
  919.3 44.1 %in_reduce.1 = f32[1600,512]{1,0:T(8,128)S(1)} custom-call(bf16[1600,896]{1,0:T(8,128)(2,1)S(1)} %bitcast.156, bf16[1600,3072]{1,0:T(8,128)(2,1)} %all-gather.3.cloned.1.call-done.refs_0_.refs_1_.refs_2_, bf16[1600,3072]{1,0:T(8,128)(2,1)} %all-gather.3.cloned.1.call-done.refs_0_.refs_1_.refs_2_, bf16[896,2048]{1,0:T(8,128)(2,1)} %copy-done.5, ...), custom_call_target="tpu_custom_call" | custom-call | bytes 196083712 | tf_op jit(solution)/shard_map/in_reduce/pallas_call | solution.py:839
  964.4 9.7 farewell.1
  975.2 10.8 %gather_stack.1 = bf16[4,200,768]{2,1,0:T(8,128)(2,1)S(1)} custom-call(bf16[200,768]{1,0:T(8,128)(2,1)S(1)} %slice_select_fusion.part_ref), custom_call_target="tpu_custom_call" | custom-call | bytes 62914560 | tf_op jit(solution)/shard_map/gather_stack/pallas_call | solution.py:706
  988.0 2.4 concatenate.66
  990.4 2.2 slice_bitcast_fusion
  992.6 5.5 fusion.8
  998.1 34.4 %reduce-scatter.12.cloned.1.call-done.last_ref = bf16[200,1920]{1,0:T(8,128)(2,1)} async-done(((bf16[1600,1920]{1,0:T(8,128)(2,1)}), bf16[200,1920]{1,0:T(8,128)(2,1)}) %reduce-scatter.12.cloned.1.call-update) | async-done | bytes 768016 | tf_op jit(solution)/shard_map/optimization_barrier | solution.py:1962
  1034.7 17.6 %gather_final.1 = (bf16[4,200,896]{2,1,0:T(8,128)(2,1)S(1)}, bf16[4,200,128]{2,1,0:T(8,128)(2,1)S(1)}) custom-call(bf16[200,1920]{1,0:T(8,128)(2,1)S(1)} %copy-done.26), custom_call_target="tpu_custom_call" | custom-call | bytes 62914560 | tf_op jit(solution)/shard_map/gather_final/pallas_call | solution.py:1025
  1058.9 1.8 copy.155
  1062.4 1.8 concatenate.67
  (339 shorter events, 35.0 us)
Async XLA Ops:
  7.2 184.3 %all-gather.3.cloned.1.call-start = ((), (), s32[]{:S(2)}) async-start(), calls=%async_computation.3 | async-start | bytes 11059200 | tf_op jit(solution)/shard_map/all_gather | solution.py:1698
  10.6 5.2 copy-start.102
  10.6 5.2 copy-start.103
  10.7 18.5 %copy-start.66 = (bf16[200,320]{1,0:T(8,128)(2,1)S(1)}, bf16[200,320]{1,0:T(8,128)(2,1)}, u32[]{:S(2)}) copy-start(bf16[200,320]{1,0:T(8,128)(2,1)} %param.31) | copy-start | bytes 384004
  10.7 18.5 %copy-start.67 = (bf16[200,320]{1,0:T(8,128)(2,1)S(1)}, bf16[200,320]{1,0:T(8,128)(2,1)}, u32[]{:S(2)}) copy-start(bf16[200,320]{1,0:T(8,128)(2,1)} %param.30) | copy-start | bytes 384004
  14.4 361.0 %all-gather.5.cloned.1.call-start = ((), (), s32[]{:S(2)}) async-start(), calls=%async_computation.4 | async-start | bytes 15206400 | tf_op jit(solution)/shard_map/all_gather | solution.py:1698
  33.1 59.3 %copy-start.79 = (f32[512]{0:T(512)}, f32[512]{0:T(512)S(1)}, u32[]{:S(2)}) copy-start(f32[512]{0:T(512)S(1)} %fusion.10) | copy-start | bytes 6148
  33.7 58.8 %copy-start.69 = (f32[512]{0:T(512)}, f32[512]{0:T(512)S(1)}, u32[]{:S(2)}) copy-start(f32[512]{0:T(512)S(1)} %fusion.36) | copy-start | bytes 6148
  33.7 63.2 %copy-start.45 = (bf16[200,1376]{1,0:T(8,128)(2,1)S(1)}, bf16[200,1376]{1,0:T(8,128)(2,1)}, u32[]{:S(2)}) copy-start(bf16[200,1376]{1,0:T(8,128)(2,1)} %param.45) | copy-start | bytes 1651204
  33.7 63.2 %copy-start.46 = (bf16[200,1376]{1,0:T(8,128)(2,1)S(1)}, bf16[200,1376]{1,0:T(8,128)(2,1)}, u32[]{:S(2)}) copy-start(bf16[200,1376]{1,0:T(8,128)(2,1)} %param.46) | copy-start | bytes 1651204
  33.7 63.2 %copy-start.47 = (bf16[1376,200]{0,1:T(8,128)(2,1)S(1)}, bf16[1376,200]{0,1:T(8,128)(2,1)}, u32[]{:S(2)}) copy-start(bf16[1376,200]{0,1:T(8,128)(2,1)} %param.47) | copy-start | bytes 1651204
  34.1 65.5 %copy-start.57 = (s32[2048]{0:T(1024)S(1)}, s32[2048]{0:T(1024)}, u32[]{:S(2)}) copy-start(s32[2048]{0:T(1024)} %param.26) | copy-start | bytes 24580
  99.5 674.2 %reduce-scatter.10.cloned.1.call-start = ((), (), s32[]{:S(2)}) async-start(), calls=%async_computation.6 | async-start | bytes 15206400
  102.1 146.0 %copy-start.10 = (f32[2048,8]{1,0:T(8,128)}, f32[2048,8]{1,0:T(8,128)S(1)}, u32[]{:S(2)}) copy-start(f32[2048,8]{1,0:T(8,128)S(1)} %copy.134.mask_ref) | copy-start | bytes 196612
  102.4 10.0 copy-start.29
  112.3 50.8 %copy-start = (bf16[896,2048]{1,0:T(8,128)(2,1)}, bf16[896,2048]{1,0:T(8,128)(2,1)S(1)}, u32[]{:S(2)}) copy-start(bf16[896,2048]{1,0:T(8,128)(2,1)S(1)} %convolution_convert_fusion.qt_ref.kt_ref.vt_ref) | copy-start | bytes 11010052
  112.4 53.0 %copy-start.94 = (bf16[4,400]{1,0:T(4,128)(2,1)S(1)}, bf16[4,400]{1,0:T(4,128)(2,1)}, u32[]{:S(2)}) copy-start(bf16[4,400]{1,0:T(4,128)(2,1)} %param.34) | copy-start | bytes 9604
  112.4 53.1 %copy-start.62 = (bf16[400,132]{0,1:T(8,128)(2,1)S(1)}, bf16[400,132]{0,1:T(8,128)(2,1)}, u32[]{:S(2)}) copy-start(bf16[400,132]{0,1:T(8,128)(2,1)} %param.36) | copy-start | bytes 316804
  112.4 53.3 %copy-start.65 = (bf16[100,400]{0,1:T(8,128)(2,1)S(1)}, bf16[100,400]{0,1:T(8,128)(2,1)}, u32[]{:S(2)}) copy-start(bf16[100,400]{0,1:T(8,128)(2,1)} %param.37) | copy-start | bytes 240004
  187.7 22.9 %copy-start.58 = (bf16[800,32]{1,0:T(8,128)(2,1)}, bf16[800,32]{1,0:T(8,128)(2,1)S(1)}, u32[]{:S(2)}) copy-start(bf16[800,32]{1,0:T(8,128)(2,1)S(1)} %slice.258) | copy-start | bytes 153604
  187.9 22.7 %copy-start.60 = (bf16[800,100]{1,0:T(8,128)(2,1)}, bf16[800,100]{1,0:T(8,128)(2,1)S(1)}, u32[]{:S(2)}) copy-start(bf16[800,100]{1,0:T(8,128)(2,1)S(1)} %slice.257) | copy-start | bytes 480004
  188.2 22.4 %copy-start.104 = (bf16[256]{0:T(256)(128)(2,1)}, bf16[256]{0:T(256)(128)(2,1)S(1)}, u32[]{:S(2)}) copy-start(bf16[256]{0:T(256)(128)(2,1)S(1)} %pad.65.clone) | copy-start | bytes 1540
  188.3 22.3 %copy-start.106 = (bf16[256]{0:T(256)(128)(2,1)}, bf16[256]{0:T(256)(128)(2,1)S(1)}, u32[]{:S(2)}) copy-start(bf16[256]{0:T(256)(128)(2,1)S(1)} %pad.63.clone) | copy-start | bytes 1540
  190.7 11.7 %copy-start.85 = (f32[800]{0:T(1024)}, f32[800]{0:T(1024)S(1)}, u32[]{:S(2)}) copy-start(f32[800]{0:T(1024)S(1)} %get-tuple-element.288) | copy-start | bytes 9604
  190.7 11.7 %copy-start.87 = (f32[800]{0:T(1024)}, f32[800]{0:T(1024)S(1)}, u32[]{:S(2)}) copy-start(f32[800]{0:T(1024)S(1)} %get-tuple-element.289) | copy-start | bytes 9604
  190.7 11.7 %copy-start.89 = (f32[800]{0:T(1024)}, f32[800]{0:T(1024)S(1)}, u32[]{:S(2)}) copy-start(f32[800]{0:T(1024)S(1)} %get-tuple-element.290) | copy-start | bytes 9604
  190.7 11.7 %copy-start.91 = (f32[800]{0:T(1024)}, f32[800]{0:T(1024)S(1)}, u32[]{:S(2)}) copy-start(f32[800]{0:T(1024)S(1)} %get-tuple-element.291) | copy-start | bytes 9604
  202.3 8.3 copy-start.38
  210.6 37.5 %copy-start.6 = (bf16[2048,800]{1,0:T(8,128)(2,1)}, bf16[2048,800]{1,0:T(8,128)(2,1)S(1)}, u32[]{:S(2)}) copy-start(bf16[2048,800]{1,0:T(8,128)(2,1)S(1)} %get-tuple-element.295.xa_ref) | copy-start | bytes 9830404
  234.7 13.4 %copy-start.18 = (bf16[2048,256]{1,0:T(8,128)(2,1)}, bf16[2048,256]{1,0:T(8,128)(2,1)S(1)}, u32[]{:S(2)}) copy-start(bf16[2048,256]{1,0:T(8,128)(2,1)S(1)} %total_rows.2.dbl_ref) | copy-start | bytes 3145732
  248.1 23.1 %copy-start.15 = (bf16[640,2048]{1,0:T(8,128)(2,1)S(1)}, bf16[640,2048]{1,0:T(8,128)(2,1)}, u32[]{:S(2)}) copy-start(bf16[640,2048]{1,0:T(8,128)(2,1)} %copy-done.14) | copy-start | bytes 7864324
  271.2 41.4 %copy-start.24 = (f32[32,16,800]{2,1,0:T(8,128)}, f32[32,16,800]{2,1,0:T(8,128)S(1)}, u32[]{:S(2)}) copy-start(f32[32,16,800]{2,1,0:T(8,128)S(1)} %get-tuple-element.114.hsave_ref) | copy-start | bytes 4915204
  423.5 43.0 %copy-start.32 = (f32[1600,512]{1,0:T(8,128)S(1)}, f32[1600,512]{1,0:T(8,128)}, u32[]{:S(2)}) copy-start(f32[1600,512]{1,0:T(8,128)} %copy-done.31) | copy-start | bytes 9830404
  423.5 43.0 %copy-start.39 = (f32[512,1600]{0,1:T(8,128)S(1)}, f32[512,1600]{0,1:T(8,128)}, u32[]{:S(2)}) copy-start(f32[512,1600]{0,1:T(8,128)} %param.25) | copy-start | bytes 9830404
  423.5 43.0 %copy-start.75 = (f32[512]{0:T(512)S(1)}, f32[512]{0:T(512)}, u32[]{:S(2)}) copy-start(f32[512]{0:T(512)} %convert_multiply_fusion) | copy-start | bytes 6148
  554.4 361.6 %reduce-scatter.8.cloned.1.call-start = ((), (), s32[]{:S(2)}) async-start(), calls=%async_computation.5 | async-start | bytes 8294400 | tf_op jit(solution)/shard_map/reduce_scatter | solution.py:1699
  554.5 44.2 %copy-start.33 = (f32[1600,512]{1,0:T(8,128)S(1)}, f32[1600,512]{1,0:T(8,128)}, u32[]{:S(2)}) copy-start(f32[1600,512]{1,0:T(8,128)} %copy-done.31) | copy-start | bytes 9830404
  554.5 45.8 %copy-start.40 = (f32[512,1600]{0,1:T(8,128)S(1)}, f32[512,1600]{0,1:T(8,128)}, u32[]{:S(2)}) copy-start(f32[512,1600]{0,1:T(8,128)} %param.25) | copy-start | bytes 9830404
  648.1 39.9 %copy-start.13 = (bf16[1600,2048]{1,0:T(8,128)(2,1)}, bf16[1600,2048]{1,0:T(8,128)(2,1)S(1)}, u32[]{:S(2)}) copy-start(bf16[1600,2048]{1,0:T(8,128)(2,1)S(1)} %gather_rows.2.refs_2_) | copy-start | bytes 19660804
  690.7 12.0 %copy-start.11 = (f32[2048,8]{1,0:T(8,128)S(1)}, f32[2048,8]{1,0:T(8,128)}, u32[]{:S(2)}) copy-start(f32[2048,8]{1,0:T(8,128)} %copy-done.10) | copy-start | bytes 196612
  690.7 12.0 %copy-start.19 = (bf16[2048,256]{1,0:T(8,128)(2,1)S(1)}, bf16[2048,256]{1,0:T(8,128)(2,1)}, u32[]{:S(2)}) copy-start(bf16[2048,256]{1,0:T(8,128)(2,1)} %copy-done.18) | copy-start | bytes 3145732
  690.7 12.0 %copy-start.25 = (f32[32,16,800]{2,1,0:T(8,128)S(1)}, f32[32,16,800]{2,1,0:T(8,128)}, u32[]{:S(2)}) copy-start(f32[32,16,800]{2,1,0:T(8,128)} %copy-done.24) | copy-start | bytes 4915204
  773.7 8.7 copy-start.28
  773.7 8.7 copy-start.30
  773.7 258.8 %reduce-scatter.12.cloned.1.call-start = ((), (), s32[]{:S(2)}) async-start(), calls=%async_computation.7 | async-start | bytes 6912000
  773.8 8.7 copy-start.1
  773.8 8.7 copy-start.16
  782.4 51.2 %copy-start.23 = (f32[2048,256]{1,0:T(8,128)S(1)}, f32[2048,256]{1,0:T(8,128)}, u32[]{:S(2)}) copy-start(f32[2048,256]{1,0:T(8,128)} %get-tuple-element.132.part_ref) | copy-start | bytes 6291460
  833.6 22.0 %copy-start.5 = (bf16[896,2048]{1,0:T(8,128)(2,1)}, bf16[896,2048]{1,0:T(8,128)(2,1)S(1)}, u32[]{:S(2)}) copy-start(bf16[896,2048]{1,0:T(8,128)(2,1)S(1)} %attn_bwd.1.refs_3_) | copy-start | bytes 11010052
  833.6 20.6 %copy-start.7 = (bf16[2048,800]{1,0:T(8,128)(2,1)S(1)}, bf16[2048,800]{1,0:T(8,128)(2,1)}, u32[]{:S(2)}) copy-start(bf16[2048,800]{1,0:T(8,128)(2,1)} %copy-done.6) | copy-start | bytes 9830404
  919.3 44.1 %copy-start.36 = (f32[512,1600]{0,1:T(8,128)S(1)}, f32[512,1600]{0,1:T(8,128)}, u32[]{:S(2)}) copy-start(f32[512,1600]{0,1:T(8,128)} %param.24) | copy-start | bytes 9830404
  919.3 44.1 %copy-start.64 = (f32[1600]{0:T(1024)S(1)}, f32[1600]{0:T(1024)}, u32[]{:S(2)}) copy-start(f32[1600]{0:T(1024)} %copy-done.63) | copy-start | bytes 19204
  919.3 44.1 %copy-start.70 = (f32[512]{0:T(512)S(1)}, f32[512]{0:T(512)}, u32[]{:S(2)}) copy-start(f32[512]{0:T(512)} %copy-done.69) | copy-start | bytes 6148
  963.4 10.8 %copy-start.99 = (pred[768]{0:T(1024)(128)(4,1)S(1)}, pred[768]{0:T(1024)(128)(4,1)}, u32[]{:S(2)}) copy-start(pred[768]{0:T(1024)(128)(4,1)} %constant.85.clone.1) | copy-start | bytes 2308
  975.1 15.3 %copy-start.80 = (f32[512]{0:T(512)S(1)}, f32[512]{0:T(512)}, u32[]{:S(2)}) copy-start(f32[512]{0:T(512)} %copy-done.79) | copy-start | bytes 6148
  1058.8 5.3 copy-start.48
  1058.9 5.3 copy-start.53
  1058.9 5.3 copy-start.54
  1058.9 5.3 copy-start.55
  1058.9 5.3 copy-start.56
  1058.9 6.1 copy-start.49
  1058.9 6.1 copy-start.50
  1058.9 6.1 copy-start.51
  1058.9 6.1 copy-start.52
  (49 other events, 123.9 us)
Sparse Core Ops, SparseCore 0:
  14.5 173.2 all-gather.2
  190.0 185.3 all-gather.4
  554.6 219.0 reduce-scatter.9
  777.2 133.0 reduce-scatter.7
  916.1 116.3 reduce-scatter.11

commit v2 on v1

--- a/solution.py
+++ b/solution.py
@@ -1773,7 +1773,11 @@
     ff_width = w_gate.shape[1]
     ff_step = -(-ff_width // 128) * 128
     blank = jnp.zeros((own_width, ff_step - ff_width), jnp.bfloat16)
-    ffn_all = gather_dp(jnp.concatenate([w_gate, blank, w_up, blank, w_down.T, blank], axis=1))
+    gate_up_local = jnp.concatenate([w_gate, blank, w_up, blank], axis=1)
+    down_local = jnp.concatenate([w_down.T, blank], axis=1)
+    gate_up_local, down_local = tie((gate_up_local, down_local))
+    gate_up_all = gather_dp(gate_up_local)
+    down_all = gather_dp(down_local)
     vector_rows = inner_rows[:, :8].astype(jnp.float32).T
     xproj_rows = inner_rows[:, 8 : 8 + RANK + 2 * STATE]
     dt_weight = inner_rows[:, 8 + RANK + 2 * STATE :].T
@@ -1808,10 +1812,10 @@
     )
     mixed, pull_join = jax.vjp(join_rows_t, inputs_t, attn_sum, ssm_sum, gain_attn, gain_ssm)
     normed_mid, pull_mid = jax.vjp(normalize_t, mixed, gain_mid)
-    normed_low, ffn_all = tie((low(normed_mid), ffn_all))
+    normed_low, gate_up_all = tie((low(normed_mid), gate_up_all))
     whole_mid, gate_rows, up_rows, hidden = turn_rows(
         normed_low,
-        ffn_all,
+        gate_up_all,
         [],
         [(ff_width, jnp.float32), (ff_width, jnp.float32), (ff_width, jnp.bfloat16)],
         [(0, ff_width), (ff_step, ff_step + ff_width)],
@@ -1821,17 +1825,17 @@
         52,
     )
     ffn_rows = product_reduce(
-        [(ffn_all, None, 2 * ff_step, ff_step)], [(hidden, False)], [(0, 0, ff_width, 0)], 6, "down_reduce", 45
+        [(down_all, None, 0, ff_step)], [(hidden, False)], [(0, 0, ff_width, 0)], 6, "down_reduce", 45
     )
     result = mixed + ffn_rows
     all_rows = inputs.shape[0] * lax.axis_size("dp") * lax.axis_size("tensor")
     grad_out = all_rows / valid_total * valid.astype(jnp.float32)[None, :] * (result - teacher.T)
     grad_ffn, grad_gate, grad_up = turn_rows(
         low(grad_out),
-        ffn_all,
+        down_all,
         [gate_rows, up_rows],
         [(ff_width, jnp.bfloat16), (ff_width, jnp.bfloat16)],
-        [(2 * ff_step, 2 * ff_step + ff_width)],
+        [(0, ff_width)],
         backward_gate,
         16,
         "grad_turn",
@@ -1849,7 +1853,7 @@
     grad_gate, grad_up, ffn_grads = tie((grad_gate, grad_up, ffn_grads))
     ffn_shard = scatter_dp(ffn_grads)
     grad_mid_rows = product_reduce(
-        [(ffn_all, None, 0, 2 * ff_step)],
+        [(gate_up_all, None, 0, 2 * ff_step)],
         [(grad_gate, False), (grad_up, False)],
         [(0, 0, ff_width, 0), (0, ff_step, ff_step + ff_width, 1)],
         7,

time: 1080 us -> 1070 us (level)
    pallas_call x1, Pallas kernels: 21.6 us -> 41.2 us  [inner_spread(): pl.pallas_call(spread_kernel, name='inner_spread', in_specs=[whole], out_...]
    all_gather x2 -> x3, waiting for transfers between devices: 12.7 us -> 0.04 us  [per_device(): gather_dp = lambda part: lax.all_gather(part, 'dp', axis=0, tiled=True)]
  transfers between devices with their start and end apart: 5 -> 6, of which waited for: 3 -> 3; matrix products, arithmetic and copies ran while one was open for 14% -> 14% of each run, Pallas kernels for 57% -> 62%
where the time goes in v2:
time: 1070 us
  Pallas kernels  807 us (75%)
  matrix products  85.3 us (8%)
  other arithmetic  57.3 us (5%)
  local copies, waits for them, and re-layouts  53.7 us (5%)
  waiting for transfers between devices  46.4 us (4%)
  between operations  17.6 us (2%)
    pallas_call x5, Pallas kernels, product_reduce(): pl.pallas_call(functools.partial(product_kernel, plan, leads, right_flips...  216 us
    pallas_call x2, Pallas kernels, turn_rows(): pl.pallas_call(functools.partial(turn_kernel, combine, plan, len(ins), le...  91.1 us
    pallas_call x3, Pallas kernels, weight_grads(): pl.pallas_call(functools.partial(weights_kernel, plan), name=name, grid=(...  87.3 us
    pallas_call x2, Pallas kernels, gather_rows(): pl.pallas_call(gather_kernel, name='gather_rows', in_specs=[pl.BlockSpec(...  79.8 us
    pallas_call x1, Pallas kernels, gather_first(): pl.pallas_call(first_kernel, name='gather_first', in_specs=[anywhere] * 2...  58.4 us
    dot_general x5, matrix products, dot_first(): lax.dot_general(left, right, (((0,), (0,)), ((), ())), preferred_element_...  48.5 us
    pallas_call x1, Pallas kernels, attn_backward(): pl.pallas_call(attn_bwd_kernel, name='attn_bwd', grid_spec=pltpu.Prefetch...  42.1 us
    pallas_call x1, Pallas kernels, inner_spread(): pl.pallas_call(spread_kernel, name='inner_spread', in_specs=[whole], out_...  41.2 us
  transfers between devices with their start and end apart: 6, of which 3 were waited for; matrix products, arithmetic and copies ran while one was open for 14% of the time, Pallas kernels for 62%

profile of v2, /device:TPU:17, one launch (start us, length us, event | category | flops | bytes accessed | tf_op | source)
XLA Modules:
  0.0 1067.9 jit_solution(4236520000312132204)
XLA Ops:
  7.2 2.1 reshape.293
  9.4 1.1 constant_dynamic-slice_fusion.3
  10.7 2.5 concatenate.57
  17.0 11.1 %hello.1 = (f32[8,8,256]{2,1,0:T(8,128)}, f32[8,8,128]{2,1,0:T(8,128)}) custom-call(f32[8,256]{1,0:T(8,128)} %fusion.32.gain_ref, f32[8,128]{1,0:T(8,128)} %broadcast_in_dim.73.count_ref), custom_call_target="tpu_custom_call" | custom-call | bytes 31457280 | tf_op jit(solution)/shard_map/hello/pallas_call | solution.py:530
  29.3 1.1 fusion.44
  30.7 2.4 fusion.10
  34.1 58.4 %gather_first.1 = (bf16[1600,2048]{1,0:T(8,128)(2,1)S(1)}, bf16[8,200,896]{2,1,0:T(8,128)(2,1)S(1)}) custom-call(bf16[1600,512]{1,0:T(8,128)(2,1)S(1)} %multiply_convert_fusion.2.part_ref, bf16[200,896]{1,0:T(8,128)(2,1)S(1)} %concatenate.59.shard_ref), custom_call_target="tpu_custom_call" | custom-call | bytes 283115520 | tf_op jit(solution)/shard_map/gather_first/pallas_call | solution.py:251
  92.5 2.8 copy-done.4
  95.2 1.5 copy-done.21
  97.7 2.0 concatenate.66
  103.2 10.2 convolution_convert_fusion.qt_ref.kt_ref.vt_ref
  113.5 40.9 %attn_fwd.1 = (bf16[640,2048]{1,0:T(8,128)(2,1)S(1)}, f32[2,8,2048]{2,1,0:T(8,128)S(1)}) custom-call(s32[16]{0:T(128)S(1)} %pad_add_fusion.4.first_ref, bf16[896,2048]{1,0:T(8,128)(2,1)S(1)} %convolution_convert_fusion.qt_ref.kt_ref.vt_ref, bf16[896,2048]{1,0:T(8,128)(2,1)S(1)} %convolution_convert_fusion.qt_ref.kt_ref.vt_ref, ...), custom_call_target="tpu_custom_call" | custom-call | bytes 157286400 | tf_op jit(solution)/shard_map/attn_fwd/pallas_call | solution.py:1121
  154.5 1.5 copy-done.14
  157.3 41.2 %inner_spread.1 = bf16[2,400,256]{2,1,0:T(8,128)(2,1)S(1)} custom-call(bf16[400,256]{1,0:T(8,128)(2,1)S(1)} %pad.46.part_ref), custom_call_target="tpu_custom_call" | custom-call | bytes 41943040 | tf_op jit(solution)/shard_map/inner_spread/pallas_call | solution.py:922
  199.4 1.4 slice_reduce_fusion.10
  202.4 10.8 %fusion.16 = f32[2048,800]{1,0:T(8,128)S(1)} fusion(bf16[1600,2048]{1,0:T(8,128)(2,1)} %copy-done.4, bf16[1600,3072]{1,0:T(8,128)(2,1)} %all-gather.4.cloned.1.call-done.refs_0_.refs_1_.refs_2_), kind=kOutput, calls=%fused_computation.57 | convolution fusion | flops 5242880000 | bytes 15974400 | tf_op jit(solution)/shard_map/dot_general | solution.py:46
  213.3 8.2 fusion.4
  221.6 1.3 fusion.20.part_ref
  222.9 15.5 %total_rows.2.dbl_ref = bf16[2048,256]{1,0:T(8,128)(2,1)S(1)} custom-call(f32[2048,256]{1,0:T(8,128)S(1)} %fusion.20.part_ref), custom_call_target="tpu_custom_call" | custom-call | bytes 62914560 | tf_op jit(solution)/shard_map/total_rows/pallas_call | solution.py:462
  238.4 14.1 %fusion.14.z_ref = f32[2048,800]{1,0:T(8,128)} fusion(bf16[1600,2048]{1,0:T(8,128)(2,1)} %copy-done.4, bf16[1600,3072]{1,0:T(8,128)(2,1)} %all-gather.4.cloned.1.call-done.refs_0_.refs_1_.refs_2_), kind=kOutput, calls=%fused_computation.55 | convolution fusion | flops 5242880000 | bytes 15974400 | tf_op jit(solution)/shard_map/dot_general | solution.py:46
  252.5 21.3 %scan_fwd.1 = (bf16[2048,800]{1,0:T(8,128)(2,1)S(1)}, f32[32,16,800]{2,1,0:T(8,128)S(1)}) custom-call(bf16[2048,800]{1,0:T(8,128)(2,1)S(1)} %get-tuple-element.299.xa_ref, f32[2048,800]{1,0:T(8,128)} %fusion.14.z_ref, bf16[2048,256]{1,0:T(8,128)(2,1)S(1)} %total_rows.2.dbl_ref, f32[2048,8]{1,0:T(8,128)S(1)} %copy.134.mask_ref, f32[1,2048]{1,0:T(1,128)S(1)} %bitcast.159, ...), custom_call_target="tpu_custom_call" | custom-call | bytes 97517568 | tf_op jit(solution)/shard_map/scan_fwd/pallas_call | solution.py:1586
  273.8 1.8 copy-done.17
  275.6 41.9 %attn_reduce.1 = f32[1600,512]{1,0:T(8,128)S(1)} custom-call(bf16[1600,3072]{1,0:T(8,128)(2,1)} %all-gather.4.cloned.1.call-done.refs_0_.refs_1_.refs_2_, bf16[640,2048]{1,0:T(8,128)(2,1)S(1)} %copy-done.15), custom_call_target="tpu_custom_call" | custom-call | bytes 161480704 | tf_op jit(solution)/shard_map/attn_reduce/pallas_call | solution.py:839
  317.5 42.4 %ssm_reduce.1 = f32[1600,512]{1,0:T(8,128)S(1)} custom-call(bf16[1600,3072]{1,0:T(8,128)(2,1)} %all-gather.4.cloned.1.call-done.refs_0_.refs_1_.refs_2_, bf16[2048,800]{1,0:T(8,128)(2,1)} %copy-done.17), custom_call_target="tpu_custom_call" | custom-call | bytes 161480704 | tf_op jit(solution)/shard_map/ssm_reduce/pallas_call | solution.py:839
  361.7 1.3 copy-done.35
  363.0 1.3 multiply_reduce_fusion.11
  365.0 1.1 copy-done.31
  366.1 1.5 multiply_convert_fusion.1.refs_0_
  367.7 1.4 copy-done.20
  369.1 45.9 %gate_turn.1 = (bf16[1600,2048]{1,0:T(8,128)(2,1)}, f32[2048,1376]{1,0:T(8,128)}, f32[2048,1376]{1,0:T(8,128)}, bf16[2048,1376]{1,0:T(8,128)(2,1)}) custom-call(bf16[1600,512]{1,0:T(8,128)(2,1)S(1)} %copy-done.20, bf16[1600,2816]{1,0:T(8,128)(2,1)} %all-gather.8.cloned.1.call-done.refs_1_.refs_0_), custom_call_target="tpu_custom_call" | custom-call | bytes 196083712 | tf_op jit(solution)/shard_map/gate_turn/pallas_call | solution.py:371
  415.1 43.2 %down_reduce.1 = f32[1600,512]{1,0:T(8,128)S(1)} custom-call(bf16[1600,1408]{1,0:T(8,128)(2,1)} %all-gather.6.cloned.1.call-done.refs_0_.refs_1_, bf16[2048,1376]{1,0:T(8,128)(2,1)} %get-tuple-element.117.refs_1_.refs_5_), custom_call_target="tpu_custom_call" | custom-call | bytes 169869312 | tf_op jit(solution)/shard_map/down_reduce/pallas_call | solution.py:839
  458.3 1.4 fusion.19.refs_0_
  460.3 45.2 %grad_turn.1 = (bf16[1600,2048]{1,0:T(8,128)(2,1)}, bf16[2048,1376]{1,0:T(8,128)(2,1)}, bf16[2048,1376]{1,0:T(8,128)(2,1)}) custom-call(bf16[1600,512]{1,0:T(8,128)(2,1)S(1)} %fusion.19.refs_0_, bf16[1600,1408]{1,0:T(8,128)(2,1)} %all-gather.6.cloned.1.call-done.refs_0_.refs_1_, f32[2048,1376]{1,0:T(8,128)} %get-tuple-element.120.refs_2_, ...), custom_call_target="tpu_custom_call" | custom-call | bytes 196083712 | tf_op jit(solution)/shard_map/grad_turn/pallas_call | solution.py:371
  505.4 40.7 %ffn_weight_grads.1 = bf16[1600,4224]{1,0:T(8,128)(2,1)} custom-call(bf16[1600,2048]{1,0:T(8,128)(2,1)} %get-tuple-element.124.refs_0_.refs_2_, bf16[2048,1376]{1,0:T(8,128)(2,1)} %get-tuple-element.126.refs_1_, bf16[1600,2048]{1,0:T(8,128)(2,1)} %get-tuple-element.124.refs_0_.refs_2_, bf16[2048,1376]{1,0:T(8,128)(2,1)} %get-tuple-element.127.refs_3_.refs_2_, ...), custom_call_target="tpu_custom_call" | custom-call | bytes 165675008 | tf_op jit(solution)/shard_map/ffn_weight_grads/pallas_call | solution.py:591
  546.3 44.0 %mid_reduce.1 = f32[1600,512]{1,0:T(8,128)S(1)} custom-call(bf16[1600,2816]{1,0:T(8,128)(2,1)} %all-gather.8.cloned.1.call-done.refs_1_.refs_0_, bf16[2048,1376]{1,0:T(8,128)(2,1)} %get-tuple-element.126.refs_1_, bf16[2048,1376]{1,0:T(8,128)(2,1)} %get-tuple-element.127.refs_3_.refs_2_), custom_call_target="tpu_custom_call" | custom-call | bytes 188743680 | tf_op jit(solution)/shard_map/mid_reduce/pallas_call | solution.py:839
  590.3 1.5 multiply_reduce_fusion.10
  593.2 4.7 multiply_reduce_fusion.8
  598.0 1.6 fusion.7
  599.6 39.9 %gather_rows.2.refs_2_ = bf16[1600,2048]{1,0:T(8,128)(2,1)S(1)} custom-call(bf16[1600,512]{1,0:T(8,128)(2,1)S(1)} %get-tuple-element.308.part_ref), custom_call_target="tpu_custom_call" | custom-call | bytes 147456000 | tf_op jit(solution)/shard_map/gather_rows/pallas_call | solution.py:129
  639.6 39.9 %gather_rows.3.refs_0_ = bf16[1600,2048]{1,0:T(8,128)(2,1)S(1)} custom-call(bf16[1600,512]{1,0:T(8,128)(2,1)S(1)} %get-tuple-element.129.part_ref), custom_call_target="tpu_custom_call" | custom-call | bytes 147456000 | tf_op jit(solution)/shard_map/gather_rows/pallas_call | solution.py:129
  679.5 2.7 copy-done.12
  682.2 12.1 %fusion.12.gs_ref = f32[2048,800]{1,0:T(8,128)} fusion(bf16[1600,2048]{1,0:T(8,128)(2,1)S(1)} %gather_rows.2.refs_2_, bf16[1600,3072]{1,0:T(8,128)(2,1)} %all-gather.4.cloned.1.call-done.refs_0_.refs_1_.refs_2_), kind=kOutput, calls=%fused_computation.53 | convolution fusion | flops 5242880000 | bytes 15974400 | tf_op jit(solution)/shard_map/dot_general | solution.py:46
  694.3 39.8 %scan_bwd.1 = (bf16[2048,800]{1,0:T(8,128)(2,1)}, f32[2048,800]{1,0:T(8,128)}, f32[2048,256]{1,0:T(8,128)}, f32[100,800]{1,0:T(8,128)S(1)}, f32[8,800]{1,0:T(8,128)S(1)}) custom-call(bf16[2048,800]{1,0:T(8,128)(2,1)} %copy-done.6, f32[2048,800]{1,0:T(8,128)} %fusion.14.z_ref, bf16[2048,256]{1,0:T(8,128)(2,1)S(1)} %copy-done.19, f32[2048,8]{1,0:T(8,128)S(1)} %copy-done.11, ...), custom_call_target="tpu_custom_call" | custom-call | bytes 255852544 | tf_op jit(solution)/shard_map/scan_bwd/pallas_call | solution.py:1613
  734.1 26.8 %mid_weight_grads.1 = bf16[1600,2240]{1,0:T(8,128)(2,1)} custom-call(bf16[1600,2048]{1,0:T(8,128)(2,1)} %copy-done.12, bf16[640,2048]{1,0:T(8,128)(2,1)} %copy-done.14, bf16[1600,2048]{1,0:T(8,128)(2,1)} %copy-done.13, bf16[2048,800]{1,0:T(8,128)(2,1)} %copy-done.17, bf16[1600,2048]{1,0:T(8,128)(2,1)} %copy-done.4, bf16[2048,800]{1,0:T(8,128)(2,1)} %get-tuple-element.134.refs_5_), custom_call_target="tpu_custom_call" | custom-call | bytes 97517568 | tf_op jit(solution)/shard_map/mid_weight_grads/pallas_call | solution.py:591
  761.0 7.9 reduce-scatter.10.cloned.1.call-done
  769.0 8.6 convolution_convert_fusion.1.dot_ref
  777.6 42.1 %attn_bwd.1.refs_3_ = bf16[896,2048]{1,0:T(8,128)(2,1)S(1)} custom-call(s32[16]{0:T(128)S(1)} %copy-done.30, bf16[896,2048]{1,0:T(8,128)(2,1)S(1)} %copy-done.1, bf16[640,2048]{1,0:T(8,128)(2,1)S(1)} %convolution_convert_fusion.1.dot_ref, bf16[640,2048]{1,0:T(8,128)(2,1)S(1)} %copy-done.16, f32[2,8,2048]{2,1,0:T(8,128)S(1)} %copy-done.28, ...), custom_call_target="tpu_custom_call" | custom-call | bytes 167772160 | tf_op jit(solution)/shard_map/attn_bwd/pallas_call | solution.py:1218
  819.9 21.8 %total_rows.3 = bf16[2048,256]{1,0:T(8,128)(2,1)S(1)} custom-call(f32[2048,256]{1,0:T(8,128)S(1)} %copy-done.23), custom_call_target="tpu_custom_call" | custom-call | bytes 62914560 | tf_op jit(solution)/shard_map/total_rows/pallas_call | solution.py:462
  841.7 1.3 convolution_convert_fusion.2
  843.2 26.8 %multiply_reduce_fusion.2 = (f32[800]{0:T(1024)S(1)}, f32[800]{0:T(1024)S(1)}, f32[800]{0:T(1024)S(1)}, f32[800]{0:T(1024)S(1)}, bf16[800]{0:T(1024)(128)(2,1)S(...) fusion(f32[1,2048,800]{2,1,0:T(8,128)} %bitcast.163, ...), kind=kOutput, calls=%fused_computation.12 | convolution fusion | flops 883093760 | bytes 53741376 | tf_op jit(solution)/shard_map/dot_general | solution.py:40
  871.4 13.2 %fusion.3.refs_1_.refs_4_ = bf16[2048,800]{1,0:T(8,128)(2,1)} fusion(f32[1,2048,800]{2,1,0:T(8,128)} %get-tuple-element.303, f32[1,2048,800]{2,1,0:T(8,128)} %get-tuple-element.304, f32[1,2048,800]{2,1,0:T(8,128)} %get-tuple-element.305, f32[1,2048,800]{2,1,0:T(8,128)} %get-tuple-element.306), kind=kLoop, calls=%fused_computation.23 | loop fusion | flops 6553600 | bytes 29491200 | tf_op jit(solution)/shard_map/convert_element_type | solution.py:1697
  884.7 19.8 %last_weight_grads.1 = bf16[1600,1920]{1,0:T(8,128)(2,1)} custom-call(bf16[1600,2048]{1,0:T(8,128)(2,1)} %copy-done.4, bf16[2048,800]{1,0:T(8,128)(2,1)} %fusion.3.refs_1_.refs_4_, bf16[1600,2048]{1,0:T(8,128)(2,1)} %copy-done.4, bf16[896,2048]{1,0:T(8,128)(2,1)} %copy-done.5, bf16[1600,120]{1,0:T(8,128)(2,1)S(1)} %convert_element_type.201.refs_4_), custom_call_target="tpu_custom_call" | custom-call | bytes 75497472 | tf_op jit(solution)/shard_map/last_weight_grads/pallas_call | solution.py:591
  904.4 1.2 reduce-scatter.8.cloned.1.call-done
  905.9 1.8 slice_convert_fusion
  908.8 44.6 %in_reduce.1 = f32[1600,512]{1,0:T(8,128)S(1)} custom-call(bf16[1600,896]{1,0:T(8,128)(2,1)S(1)} %bitcast.156, bf16[1600,3072]{1,0:T(8,128)(2,1)} %all-gather.4.cloned.1.call-done.refs_0_.refs_1_.refs_2_, bf16[1600,3072]{1,0:T(8,128)(2,1)} %all-gather.4.cloned.1.call-done.refs_0_.refs_1_.refs_2_, bf16[896,2048]{1,0:T(8,128)(2,1)} %copy-done.5, ...), custom_call_target="tpu_custom_call" | custom-call | bytes 196083712 | tf_op jit(solution)/shard_map/in_reduce/pallas_call | solution.py:839
  954.5 12.5 %farewell.1 = f32[8,256]{1,0:T(8,128)S(1)} custom-call(f32[8,8,256]{2,1,0:T(8,128)S(1)} %pad.55.part_ref), custom_call_target="tpu_custom_call" | custom-call | bytes 41943040 | tf_op jit(solution)/shard_map/farewell/pallas_call | solution.py:657
  968.0 10.8 %gather_stack.1 = bf16[4,200,768]{2,1,0:T(8,128)(2,1)S(1)} custom-call(bf16[200,768]{1,0:T(8,128)(2,1)S(1)} %slice_select_fusion.part_ref), custom_call_target="tpu_custom_call" | custom-call | bytes 62914560 | tf_op jit(solution)/shard_map/gather_stack/pallas_call | solution.py:706
  980.9 2.4 concatenate.70
  983.3 2.2 slice_bitcast_fusion
  985.5 5.4 fusion.8
  990.9 36.5 %reduce-scatter.12.cloned.1.call-done.last_ref = bf16[200,1920]{1,0:T(8,128)(2,1)} async-done(((bf16[1600,1920]{1,0:T(8,128)(2,1)}), bf16[200,1920]{1,0:T(8,128)(2,1)}) %reduce-scatter.12.cloned.1.call-update) | async-done | bytes 768016 | tf_op jit(solution)/shard_map/optimization_barrier | solution.py:1966
  1029.6 17.7 %gather_final.1 = (bf16[4,200,896]{2,1,0:T(8,128)(2,1)S(1)}, bf16[4,200,128]{2,1,0:T(8,128)(2,1)S(1)}) custom-call(bf16[200,1920]{1,0:T(8,128)(2,1)S(1)} %copy-done.26), custom_call_target="tpu_custom_call" | custom-call | bytes 62914560 | tf_op jit(solution)/shard_map/gather_final/pallas_call | solution.py:1025
  1053.9 1.8 copy.155
  1057.3 1.8 concatenate.71
  (343 shorter events, 36.3 us)
Async XLA Ops:
  7.2 195.2 %all-gather.4.cloned.1.call-start = ((), (), s32[]{:S(2)}) async-start(), calls=%async_computation.3 | async-start | bytes 11059200 | tf_op jit(solution)/shard_map/all_gather | solution.py:1698
  10.7 18.5 %copy-start.66 = (bf16[200,320]{1,0:T(8,128)(2,1)S(1)}, bf16[200,320]{1,0:T(8,128)(2,1)}, u32[]{:S(2)}) copy-start(bf16[200,320]{1,0:T(8,128)(2,1)} %param.31) | copy-start | bytes 384004
  10.7 18.5 %copy-start.67 = (bf16[200,320]{1,0:T(8,128)(2,1)S(1)}, bf16[200,320]{1,0:T(8,128)(2,1)}, u32[]{:S(2)}) copy-start(bf16[200,320]{1,0:T(8,128)(2,1)} %param.30) | copy-start | bytes 384004
  14.4 353.3 %all-gather.8.cloned.1.call-start = ((), (), s32[]{:S(2)}) async-start(), calls=%async_computation.5 | async-start | bytes 10137600 | tf_op jit(solution)/shard_map/all_gather | solution.py:1698
  33.1 59.3 %copy-start.79 = (f32[512]{0:T(512)}, f32[512]{0:T(512)S(1)}, u32[]{:S(2)}) copy-start(f32[512]{0:T(512)S(1)} %fusion.10) | copy-start | bytes 6148
  33.7 58.8 %copy-start.69 = (f32[512]{0:T(512)}, f32[512]{0:T(512)S(1)}, u32[]{:S(2)}) copy-start(f32[512]{0:T(512)S(1)} %fusion.36) | copy-start | bytes 6148
  33.7 63.1 %copy-start.47 = (bf16[1376,200]{0,1:T(8,128)(2,1)S(1)}, bf16[1376,200]{0,1:T(8,128)(2,1)}, u32[]{:S(2)}) copy-start(bf16[1376,200]{0,1:T(8,128)(2,1)} %param.47) | copy-start | bytes 1651204
  33.7 64.0 %copy-start.45 = (bf16[200,1376]{1,0:T(8,128)(2,1)S(1)}, bf16[200,1376]{1,0:T(8,128)(2,1)}, u32[]{:S(2)}) copy-start(bf16[200,1376]{1,0:T(8,128)(2,1)} %param.45) | copy-start | bytes 1651204
  33.7 64.0 %copy-start.46 = (bf16[200,1376]{1,0:T(8,128)(2,1)S(1)}, bf16[200,1376]{1,0:T(8,128)(2,1)}, u32[]{:S(2)}) copy-start(bf16[200,1376]{1,0:T(8,128)(2,1)} %param.46) | copy-start | bytes 1651204
  34.1 66.4 %copy-start.57 = (s32[2048]{0:T(1024)S(1)}, s32[2048]{0:T(1024)}, u32[]{:S(2)}) copy-start(s32[2048]{0:T(1024)} %param.26) | copy-start | bytes 24580
  96.8 5.3 copy-start.95
  96.8 5.4 copy-start.96
  96.8 5.6 copy-start.97
  96.8 5.7 copy-start.98
  99.7 315.4 %all-gather.6.cloned.1.call-start = ((), (), s32[]{:S(2)}) async-start(), calls=%async_computation.4 | async-start | bytes 5068800 | tf_op jit(solution)/shard_map/all_gather | solution.py:1698
  100.4 668.5 %reduce-scatter.10.cloned.1.call-start = ((), (), s32[]{:S(2)}) async-start(), calls=%async_computation.7 | async-start | bytes 15206400
  103.2 149.3 %copy-start.10 = (f32[2048,8]{1,0:T(8,128)}, f32[2048,8]{1,0:T(8,128)S(1)}, u32[]{:S(2)}) copy-start(f32[2048,8]{1,0:T(8,128)S(1)} %copy.134.mask_ref) | copy-start | bytes 196612
  103.2 10.2 copy-start.29
  113.5 41.0 %copy-start = (bf16[896,2048]{1,0:T(8,128)(2,1)}, bf16[896,2048]{1,0:T(8,128)(2,1)S(1)}, u32[]{:S(2)}) copy-start(bf16[896,2048]{1,0:T(8,128)(2,1)S(1)} %convolution_convert_fusion.qt_ref.kt_ref.vt_ref) | copy-start | bytes 11010052
  113.5 43.1 %copy-start.94 = (bf16[4,400]{1,0:T(4,128)(2,1)S(1)}, bf16[4,400]{1,0:T(4,128)(2,1)}, u32[]{:S(2)}) copy-start(bf16[4,400]{1,0:T(4,128)(2,1)} %param.34) | copy-start | bytes 9604
  113.5 43.3 %copy-start.62 = (bf16[400,132]{0,1:T(8,128)(2,1)S(1)}, bf16[400,132]{0,1:T(8,128)(2,1)}, u32[]{:S(2)}) copy-start(bf16[400,132]{0,1:T(8,128)(2,1)} %param.36) | copy-start | bytes 316804
  113.5 43.4 %copy-start.65 = (bf16[100,400]{0,1:T(8,128)(2,1)S(1)}, bf16[100,400]{0,1:T(8,128)(2,1)}, u32[]{:S(2)}) copy-start(bf16[100,400]{0,1:T(8,128)(2,1)} %param.37) | copy-start | bytes 240004
  198.6 22.9 %copy-start.58 = (bf16[800,32]{1,0:T(8,128)(2,1)}, bf16[800,32]{1,0:T(8,128)(2,1)S(1)}, u32[]{:S(2)}) copy-start(bf16[800,32]{1,0:T(8,128)(2,1)S(1)} %slice.258) | copy-start | bytes 153604
  198.8 22.8 %copy-start.60 = (bf16[800,100]{1,0:T(8,128)(2,1)}, bf16[800,100]{1,0:T(8,128)(2,1)S(1)}, u32[]{:S(2)}) copy-start(bf16[800,100]{1,0:T(8,128)(2,1)S(1)} %slice.257) | copy-start | bytes 480004
  199.2 22.4 %copy-start.104 = (bf16[256]{0:T(256)(128)(2,1)}, bf16[256]{0:T(256)(128)(2,1)S(1)}, u32[]{:S(2)}) copy-start(bf16[256]{0:T(256)(128)(2,1)S(1)} %pad.66.clone) | copy-start | bytes 1540
  199.2 22.3 %copy-start.106 = (bf16[256]{0:T(256)(128)(2,1)}, bf16[256]{0:T(256)(128)(2,1)S(1)}, u32[]{:S(2)}) copy-start(bf16[256]{0:T(256)(128)(2,1)S(1)} %pad.64.clone) | copy-start | bytes 1540
  202.3 10.9 %copy-start.85 = (f32[800]{0:T(1024)}, f32[800]{0:T(1024)S(1)}, u32[]{:S(2)}) copy-start(f32[800]{0:T(1024)S(1)} %get-tuple-element.292) | copy-start | bytes 9604
  202.4 10.9 %copy-start.87 = (f32[800]{0:T(1024)}, f32[800]{0:T(1024)S(1)}, u32[]{:S(2)}) copy-start(f32[800]{0:T(1024)S(1)} %get-tuple-element.293) | copy-start | bytes 9604
  202.4 10.9 %copy-start.89 = (f32[800]{0:T(1024)}, f32[800]{0:T(1024)S(1)}, u32[]{:S(2)}) copy-start(f32[800]{0:T(1024)S(1)} %get-tuple-element.294) | copy-start | bytes 9604
  202.4 10.9 %copy-start.91 = (f32[800]{0:T(1024)}, f32[800]{0:T(1024)S(1)}, u32[]{:S(2)}) copy-start(f32[800]{0:T(1024)S(1)} %get-tuple-element.295) | copy-start | bytes 9604
  213.3 8.3 copy-start.38
  221.5 30.9 %copy-start.6 = (bf16[2048,800]{1,0:T(8,128)(2,1)}, bf16[2048,800]{1,0:T(8,128)(2,1)S(1)}, u32[]{:S(2)}) copy-start(bf16[2048,800]{1,0:T(8,128)(2,1)S(1)} %get-tuple-element.299.xa_ref) | copy-start | bytes 9830404
  238.4 14.1 %copy-start.18 = (bf16[2048,256]{1,0:T(8,128)(2,1)}, bf16[2048,256]{1,0:T(8,128)(2,1)S(1)}, u32[]{:S(2)}) copy-start(bf16[2048,256]{1,0:T(8,128)(2,1)S(1)} %total_rows.2.dbl_ref) | copy-start | bytes 3145732
  252.4 23.1 %copy-start.15 = (bf16[640,2048]{1,0:T(8,128)(2,1)S(1)}, bf16[640,2048]{1,0:T(8,128)(2,1)}, u32[]{:S(2)}) copy-start(bf16[640,2048]{1,0:T(8,128)(2,1)} %copy-done.14) | copy-start | bytes 7864324
  275.6 41.9 %copy-start.24 = (f32[32,16,800]{2,1,0:T(8,128)}, f32[32,16,800]{2,1,0:T(8,128)S(1)}, u32[]{:S(2)}) copy-start(f32[32,16,800]{2,1,0:T(8,128)S(1)} %get-tuple-element.118.hsave_ref) | copy-start | bytes 4915204
  415.0 43.2 %copy-start.32 = (f32[1600,512]{1,0:T(8,128)S(1)}, f32[1600,512]{1,0:T(8,128)}, u32[]{:S(2)}) copy-start(f32[1600,512]{1,0:T(8,128)} %copy-done.31) | copy-start | bytes 9830404
  415.1 43.2 %copy-start.39 = (f32[512,1600]{0,1:T(8,128)S(1)}, f32[512,1600]{0,1:T(8,128)}, u32[]{:S(2)}) copy-start(f32[512,1600]{0,1:T(8,128)} %param.25) | copy-start | bytes 9830404
  415.1 43.2 %copy-start.75 = (f32[512]{0:T(512)S(1)}, f32[512]{0:T(512)}, u32[]{:S(2)}) copy-start(f32[512]{0:T(512)} %convert_multiply_fusion) | copy-start | bytes 6148
  546.2 359.5 %reduce-scatter.8.cloned.1.call-start = ((), (), s32[]{:S(2)}) async-start(), calls=%async_computation.6 | async-start | bytes 8294400 | tf_op jit(solution)/shard_map/reduce_scatter | solution.py:1699
  546.2 44.0 %copy-start.33 = (f32[1600,512]{1,0:T(8,128)S(1)}, f32[1600,512]{1,0:T(8,128)}, u32[]{:S(2)}) copy-start(f32[1600,512]{1,0:T(8,128)} %copy-done.31) | copy-start | bytes 9830404
  546.3 45.6 %copy-start.40 = (f32[512,1600]{0,1:T(8,128)S(1)}, f32[512,1600]{0,1:T(8,128)}, u32[]{:S(2)}) copy-start(f32[512,1600]{0,1:T(8,128)} %param.25) | copy-start | bytes 9830404
  639.6 39.9 %copy-start.13 = (bf16[1600,2048]{1,0:T(8,128)(2,1)}, bf16[1600,2048]{1,0:T(8,128)(2,1)S(1)}, u32[]{:S(2)}) copy-start(bf16[1600,2048]{1,0:T(8,128)(2,1)S(1)} %gather_rows.2.refs_2_) | copy-start | bytes 19660804
  682.2 12.1 %copy-start.11 = (f32[2048,8]{1,0:T(8,128)S(1)}, f32[2048,8]{1,0:T(8,128)}, u32[]{:S(2)}) copy-start(f32[2048,8]{1,0:T(8,128)} %copy-done.10) | copy-start | bytes 196612
  682.2 12.1 %copy-start.19 = (bf16[2048,256]{1,0:T(8,128)(2,1)S(1)}, bf16[2048,256]{1,0:T(8,128)(2,1)}, u32[]{:S(2)}) copy-start(bf16[2048,256]{1,0:T(8,128)(2,1)} %copy-done.18) | copy-start | bytes 3145732
  682.2 12.1 %copy-start.25 = (f32[32,16,800]{2,1,0:T(8,128)S(1)}, f32[32,16,800]{2,1,0:T(8,128)}, u32[]{:S(2)}) copy-start(f32[32,16,800]{2,1,0:T(8,128)} %copy-done.24) | copy-start | bytes 4915204
  768.9 8.7 copy-start.28
  768.9 8.7 copy-start.30
  768.9 258.5 %reduce-scatter.12.cloned.1.call-start = ((), (), s32[]{:S(2)}) async-start(), calls=%async_computation.8 | async-start | bytes 6912000
  769.0 8.7 copy-start.1
  769.0 8.7 copy-start.16
  777.6 42.2 %copy-start.23 = (f32[2048,256]{1,0:T(8,128)S(1)}, f32[2048,256]{1,0:T(8,128)}, u32[]{:S(2)}) copy-start(f32[2048,256]{1,0:T(8,128)} %get-tuple-element.136.part_ref) | copy-start | bytes 6291460
  819.8 23.3 %copy-start.5 = (bf16[896,2048]{1,0:T(8,128)(2,1)}, bf16[896,2048]{1,0:T(8,128)(2,1)S(1)}, u32[]{:S(2)}) copy-start(bf16[896,2048]{1,0:T(8,128)(2,1)S(1)} %attn_bwd.1.refs_3_) | copy-start | bytes 11010052
  819.8 21.8 %copy-start.7 = (bf16[2048,800]{1,0:T(8,128)(2,1)S(1)}, bf16[2048,800]{1,0:T(8,128)(2,1)}, u32[]{:S(2)}) copy-start(bf16[2048,800]{1,0:T(8,128)(2,1)} %copy-done.6) | copy-start | bytes 9830404
  908.8 44.6 %copy-start.36 = (f32[512,1600]{0,1:T(8,128)S(1)}, f32[512,1600]{0,1:T(8,128)}, u32[]{:S(2)}) copy-start(f32[512,1600]{0,1:T(8,128)} %param.24) | copy-start | bytes 9830404
  908.8 44.6 %copy-start.64 = (f32[1600]{0:T(1024)S(1)}, f32[1600]{0:T(1024)}, u32[]{:S(2)}) copy-start(f32[1600]{0:T(1024)} %copy-done.63) | copy-start | bytes 19204
  908.8 44.6 %copy-start.70 = (f32[512]{0:T(512)S(1)}, f32[512]{0:T(512)}, u32[]{:S(2)}) copy-start(f32[512]{0:T(512)} %copy-done.69) | copy-start | bytes 6148
  953.4 13.6 %copy-start.99 = (pred[768]{0:T(1024)(128)(4,1)S(1)}, pred[768]{0:T(1024)(128)(4,1)}, u32[]{:S(2)}) copy-start(pred[768]{0:T(1024)(128)(4,1)} %constant.85.clone.1) | copy-start | bytes 2308
  968.0 15.3 %copy-start.80 = (f32[512]{0:T(512)S(1)}, f32[512]{0:T(512)}, u32[]{:S(2)}) copy-start(f32[512]{0:T(512)} %copy-done.79) | copy-start | bytes 6148
  1053.8 5.3 copy-start.48
  1053.8 5.3 copy-start.53
  1053.8 6.1 copy-start.49
  1053.8 6.1 copy-start.50
  1053.8 6.1 copy-start.51
  1053.9 6.1 copy-start.52
  (50 other events, 132.9 us)
Sparse Core Ops, SparseCore 0:
  14.5 168.4 all-gather.3
  185.7 131.8 all-gather.7
  320.3 75.6 all-gather.5
  546.3 222.5 reduce-scatter.9
  772.4 133.2 reduce-scatter.7
  909.7 117.6 reduce-scatter.11
